TPU v7x, 32 devices: a whole 2x2x4 slice. The times are simulated.
32 devices in a mesh: ctx: 4 (over y, core), dp: 8 (over z, x).
Axes of the slice: x: 2, y: 2, z: 4, core: 2. Of those that a mesh axis runs over, the one named last changes fastest.
Arguments:
- x_tokens: bfloat16 [8, 512, 8192], P('dp', 'ctx'), may hold values from -6 to 6
- queries: bfloat16 [8, 512, 4096], P('dp', 'ctx'), may hold values from -110 to 110
- key_weight: bfloat16 [8192, 512], P('dp'), may hold values from -0.0625 to 0.0625
- value_weight: bfloat16 [8192, 512], P('dp'), may hold values from -0.0625 to 0.0625
- positions: int32 [8, 512], P('dp', 'ctx'), may hold values from 0 to 2097151, as said below
- block_lists: int32 [8, 8, 6], P('dp', 'ctx'), may hold values from 0 to 7, as said below
Outputs:
- attention_out: bfloat16 [8, 512, 4096], P('dp', 'ctx')
Inputs may be any that keep to these rules, and one draw needn't show every extreme that they name: `block_lists`: entry i of row q of a sequence's lists is q - i when blocks q - i and q belong to the same document, else q; documents are runs of whole blocks, each of at most 6 blocks, and every sequence has one of exactly 6 blocks. `positions`: each sequence is four runs of 128 tokens; within a run the ids rise by one from token to token, and each run starts at or above the end of the run before it, so ids rise along the sequence.
All inputs are finite; a program needn't handle non-finite values.
Results may differ from a plain program's by a relative error of at most 0.007.
Values may be sent and summed in bfloat16 or wider, within the bound.
No kernel may reach another device: no remote copies, remote signals or barrier semaphores. Data moves between devices by JAX's collectives and lax.ppermute only.
A program may use at most 64 MiB of HBM per device.

v0:
```python
import math

import jax
import jax.numpy as jnp
from jax import lax
from jax.sharding import PartitionSpec as P

HD = 128
BLOCK = 64


neg_large = -1e30


def rope_periods(half_width):
    return jnp.array(
        [
            int(2.0 * math.pi * 500000.0 ** (column / half_width) + 0.5)
            for column in range(half_width)
        ],
        jnp.int32,
    )


def rotate_pairs(features, token_pos, head_size):
    half_width = head_size // 2
    periods = rope_periods(half_width)
    turn_counts = jnp.remainder(token_pos[:, None], periods[None, :])
    angles = 2.0 * math.pi * turn_counts.astype(jnp.float32) / periods.astype(jnp.float32)
    cosine = jnp.cos(angles)[:, None, :]
    sine_part = jnp.sin(angles)[:, None, :]
    shaped = features.reshape(features.shape[0], -1, head_size)
    first_half = shaped[:, :, :half_width]
    second_half = shaped[:, :, half_width:]
    turned = jnp.concatenate(
        [
            first_half * cosine - second_half * sine_part,
            second_half * cosine + first_half * sine_part,
        ],
        axis=2,
    )
    return turned.reshape(features.shape[0], -1)


def head_update(state, allowed, scale_factor):
    query_head, key_head, value_head, head_top, head_total, head_sum = state
    scores = (
        lax.dot_general(
            query_head, key_head, (((1,), (1,)), ((), ())), preferred_element_type=jnp.float32
        )
        * scale_factor
    )
    masked = jnp.where(allowed, scores, neg_large)
    new_top = jnp.maximum(head_top, jnp.max(masked, axis=1))
    probabilities = jnp.where(allowed, jnp.exp(scores - new_top[:, None]), 0.0)
    shrink = jnp.exp(head_top - new_top)
    new_total = head_total * shrink + jnp.sum(probabilities, axis=1)
    new_sum = head_sum * shrink[:, None] + jnp.dot(
        probabilities.astype(jnp.bfloat16), value_head, preferred_element_type=jnp.float32
    )
    return (new_top, new_total, new_sum)


def on_device(x_tokens, queries, key_weight, value_weight, positions, block_lists):
    tokens_local = x_tokens[0]
    tok_rows = tokens_local.shape[0]
    key_width = key_weight.shape[1]
    paired_weight = jnp.concatenate([key_weight, value_weight], axis=1)
    projected = jnp.dot(
        tokens_local,
        lax.all_gather(paired_weight, "dp", axis=0, tiled=True),
        preferred_element_type=jnp.float32,
    )
    token_pos = positions[0]
    key_rot = rotate_pairs(projected[:, :key_width], token_pos, HD).astype(jnp.bfloat16)
    value_cast = projected[:, key_width:].astype(jnp.bfloat16)
    packed = jnp.concatenate([key_rot, value_cast], axis=1)
    query_rot = rotate_pairs(queries[0].astype(jnp.float32), token_pos, HD).astype(jnp.bfloat16)
    kv_heads = key_width // HD
    group_size = query_rot.shape[1] // key_width
    flat_rows = group_size * tok_rows
    grouped = (
        query_rot.reshape(tok_rows, kv_heads, group_size, HD)
        .transpose(1, 2, 0, 3)
        .reshape(kv_heads, flat_rows, HD)
    )
    query_index = lax.axis_index("ctx") * tok_rows + jnp.arange(tok_rows, dtype=jnp.int32)
    local_lists = block_lists[0]
    scale_factor = HD ** (-0.5)
    initial_state = (
        jnp.full((kv_heads, flat_rows), neg_large, jnp.float32),
        jnp.zeros((kv_heads, flat_rows), jnp.float32),
        jnp.zeros((kv_heads, flat_rows, HD), jnp.float32),
    )
    kv_piece = lax.all_gather(packed, "ctx", axis=0, tiled=True)
    span_rows = kv_piece.shape[0]
    key_index = jnp.arange(span_rows, dtype=jnp.int32)
    member = jnp.any(local_lists[:, :, None] == (key_index // BLOCK)[None, None, :], axis=1)
    allowed_rows = jnp.repeat(member, BLOCK, axis=0) & (key_index[None, :] <= query_index[:, None])
    allowed = jnp.tile(allowed_rows, (group_size, 1))
    key_heads = kv_piece[:, :key_width].reshape(span_rows, kv_heads, HD).transpose(1, 0, 2)
    value_heads = kv_piece[:, key_width:].reshape(span_rows, kv_heads, HD).transpose(1, 0, 2)
    head_top, head_total, head_sum = lax.map(
        lambda inputs: head_update(inputs, allowed, scale_factor),
        (grouped, key_heads, value_heads) + tuple(initial_state),
    )
    mixed = head_sum / head_total[:, :, None]
    mixed = (
        mixed.reshape(kv_heads, group_size, tok_rows, HD)
        .transpose(2, 0, 1, 3)
        .reshape(tok_rows, kv_heads * group_size * HD)
    )
    return mixed.astype(jnp.bfloat16)[None]


def solution(mesh):
    return jax.shard_map(
        on_device,
        mesh=mesh,
        in_specs=(
            P("dp", "ctx", None),
            P("dp", "ctx", None),
            P("dp", None),
            P("dp", None),
            P("dp", "ctx"),
            P("dp", "ctx", None),
        ),
        out_specs=P("dp", "ctx", None),
        check_vma=False,
    )
```

profile of v0, /device:TPU:0, one launch (start us, length us, event | category | flops | bytes accessed | tf_op | source)
XLA Modules:
  0.0 294.3 jit_solution(9965251389659764197)
XLA Ops:
  6.5 0.0 copy-start
  6.5 0.0 all-gather.3.cloned.1.call-start
  6.5 3.3 %pad_maximum_fusion = bf16[1024,1024]{1,0:T(8,128)(2,1)} fusion(bf16[1024,512]{1,0:T(8,128)(2,1)} %param.15, bf16[1024,512]{1,0:T(8,128)(2,1)} %param.14), kind=kLoop, calls=%fused_computation.25 | loop fusion | flops 4194304 | bytes 4194304 | tf_op jit(solution)/shard_map/concatenate | solution.py:68
  9.8 0.0 copy-start.3
  9.8 0.0 copy-start.4
  9.8 0.0 copy-start.5
  9.8 0.0 all-gather.3.cloned.1.call-update
  9.9 0.0 all-gather.5.cloned.1.call-start
  9.9 0.6 copy-done.3
  10.5 0.0 copy-done.4
  10.5 0.0 copy-done.5
  10.5 0.5 fusion.32
  11.1 229.2 %all-gather.3.cloned.1.call-done = bf16[8192,1024]{1,0:T(8,128)(2,1)} async-done(((bf16[1024,1024]{1,0:T(8,128)(2,1)}), bf16[8192,1024]{1,0:T(8,128)(2,1)}) %all-gather.3.cloned.1.call-update) | async-done | bytes 16777232 | tf_op jit(solution)/shard_map/all_gather | solution.py:71
  240.3 0.0 copy-done
  240.3 8.2 %fusion.24 = f32[128,1024]{0,1:T(8,128)S(1)} fusion(bf16[8192,1024]{1,0:T(8,128)(2,1)} %all-gather.3.cloned.1.call-done, bf16[1,128,8192]{2,1,0:T(8,128)(2,1)S(1)} %copy-done), kind=kOutput, calls=%fused_computation.32 | convolution fusion | flops 2147483648 | bytes 19398656 | tf_op jit(solution)/shard_map/dot_general | solution.py:69
  248.5 0.0 copy-start.1
  248.6 0.7 pad_maximum_fusion.2
  249.3 0.0 all-gather.5.cloned.1.call-update
  249.3 0.1 copy.22
  249.4 0.1 copy.23
  249.6 0.2 copy-done.1
  249.8 0.2 convert_bitcast_fusion
  250.0 0.4 copy.30
  250.4 0.8 subtract_convert_fusion
  251.2 0.0 copy-start.2
  251.2 0.6 pad_maximum_fusion.1
  251.8 1.4 copy.24
  253.2 0.0 copy-done.2
  253.2 0.1 compare_reduce_fusion
  253.3 0.1 fusion.27
  253.4 0.2 copy.27
  253.6 11.0 %all-gather.5.cloned.1.call-done = bf16[512,1024]{0,1:T(8,128)(2,1)} async-done(((bf16[128,1024]{0,1:T(8,128)(2,1)}), bf16[512,1024]{0,1:T(8,128)(2,1)}) %all-gather.5.cloned.1.call-update) | async-done | bytes 1048592 | tf_op jit(solution)/shard_map/all_gather | solution.py:95
  264.5 1.3 fusion.37
  265.8 1.0 copy.25
  266.8 0.3 copy.26
  267.1 16.4 %while.13 = (s32[]{:T(128)}, f32[4,1024]{1,0:T(4,128)S(1)}, f32[4,1024,128]{2,1,0:T(8,128)}, bf16[4,1024,128]{2,1,0:T(8,128)(2,1)}, bf16[4,512,128]{2,1,0:T(8,12...) while((s32[]{:T(128)}, f32[4,1024]{1,0:T(4,128)S(1)}, ...), condition=%wide.region_4.6_spmd.clone, body=%wide.region_1.5_spmd.clone.sunk | while | flops 274336768 | bytes 9558113 | solution.py:103
  267.1 0.2 tile.20
  267.4 1.6 select_reduce_fusion.2
  268.9 0.6 fusion.45
  269.5 1.6 fusion.46
  271.2 0.2 tile.20
  271.4 1.6 select_reduce_fusion.2
  273.0 0.6 fusion.45
  273.6 1.6 fusion.46
  275.3 0.2 tile.20
  275.5 1.6 select_reduce_fusion.2
  277.1 0.6 fusion.45
  277.7 1.6 fusion.46
  279.4 0.2 tile.20
  279.7 1.6 select_reduce_fusion.2
  281.2 0.6 fusion.45
  281.8 1.6 fusion.46
  283.5 2.0 divide_convert_fusion
  285.5 0.7 copy.39
  286.2 1.3 convert_element_type.62
  (20 shorter events, 0.3 us)
Async XLA Ops:
  6.5 233.8 %copy-start = (bf16[1,128,8192]{2,1,0:T(8,128)(2,1)S(1)}, bf16[1,128,8192]{2,1,0:T(8,128)(2,1)}, u32[]{:S(2)}) copy-start(bf16[1,128,8192]{2,1,0:T(8,128)(2,1)} %param.12) | copy-start | bytes 6291460
  6.5 233.8 %all-gather.3.cloned.1.call-start = ((), (), s32[]{:S(2)}) async-start(), calls=%async_computation | async-start | bytes 18874368 | tf_op jit(solution)/shard_map/all_gather | solution.py:71
  9.8 0.7 copy-start.3
  9.8 0.7 copy-start.4
  9.8 0.7 copy-start.5
  9.9 254.7 %all-gather.5.cloned.1.call-start = ((), (), s32[]{:S(2)}) async-start(), calls=%async_computation.1 | async-start | bytes 1310720 | tf_op jit(solution)/shard_map/all_gather | solution.py:95
  248.5 1.3 copy-start.1
  251.2 2.0 copy-start.2
Sparse Core Ops, SparseCore 0:
  10.0 230.2 all-gather.2
  249.5 15.0 all-gather.4
where the time goes:
time: 295 us; the launch traced here: 294 us
  waiting for transfers between devices  240 us (81%)
  matrix products  20.7 us (7%)
  between operations  13.6 us (5%)
  other arithmetic  10.8 us (4%)
  local copies, waits for them, and re-layouts  8.65 us (3%)
    all_gather x1, waiting for transfers between devices, on_device(): lax.all_gather(paired_weight, 'dp', axis=0, tiled=True)  229 us
    all_gather x1, waiting for transfers between devices, on_device(): kv_piece = lax.all_gather(packed, 'ctx', axis=0, tiled=True)  11 us
    dot_general x1, matrix products, on_device(): jnp.dot(tokens_local, lax.all_gather(paired_weight, 'dp', axis=0, tiled=T...  8.15 us
    dot_general x4, matrix products, head_update(): jnp.dot(probabilities.astype(jnp.bfloat16), value_head, preferred_element...  6.36 us
    dot_general x4, matrix products, head_update(): lax.dot_general(query_head, key_head, (((1,), (1,)), ((), ())), preferred...  6.24 us
  transfers between devices with their start and end apart: 2, of which 2 were waited for; matrix products, arithmetic and copies ran while one was open for 2% of the time, Pallas kernels for 0%

commit v1 on v0

v1 whole, which is shorter than its diff:
```python
import functools
import math

import jax
import jax.numpy as jnp
from jax import lax
from jax.experimental import pallas as pl
from jax.experimental.pallas import tpu as pltpu
from jax.sharding import PartitionSpec as P

HD = 128
BLOCK = 64
LOG2E = 1.4426950408889634

neg_large = -1e30
ANY = pl.BlockSpec(memory_space=pl.ANY)
VMEM = pl.BlockSpec(memory_space=pltpu.VMEM)
SMEM = pl.BlockSpec(memory_space=pltpu.SMEM)
PARAMS = pltpu.CompilerParams(vmem_limit_bytes=40 * 1024 * 1024)


def cost(flops, bytes_accessed, transcendentals=0):
    return pl.CostEstimate(
        flops=flops, bytes_accessed=bytes_accessed, transcendentals=transcendentals
    )


def rope_periods(half_width):
    return jnp.array(
        [
            int(2.0 * math.pi * 500000.0 ** (column / half_width) + 0.5)
            for column in range(half_width)
        ],
        jnp.int32,
    )


def rope_tables(token_pos):
    half_width = HD // 2
    periods = rope_periods(half_width)
    turn_counts = jnp.remainder(token_pos[:, None], periods[None, :])
    angles = 2.0 * math.pi * turn_counts.astype(jnp.float32) / periods.astype(jnp.float32)
    cosine = jnp.cos(angles)
    sine_part = jnp.sin(angles)
    return (
        jnp.concatenate([cosine, cosine], axis=1),
        jnp.concatenate([-sine_part, sine_part], axis=1),
    )


def turn(head, cosine, sine_part):
    return head * cosine + pltpu.roll(head, HD // 2, 1) * sine_part


def cut_weights_kernel(where, key_ref, value_ref, key_out, value_out, sems):
    rows, columns = key_out.shape
    y, core = where[2], where[3]
    copies = []
    for i, (src, dst) in enumerate(((key_ref, key_out), (value_ref, value_out))):
        copy = pltpu.make_async_copy(
            src.at[
                pl.ds(pl.multiple_of(y * rows, rows), rows),
                pl.ds(pl.multiple_of(core * columns, columns), columns),
            ],
            dst,
            sems.at[i],
        )
        copy.start()
        copies.append(copy)
    for copy in copies:
        copy.wait()


def cut_tokens_kernel(n_line, where, x_ref, mine_ref, other_ref, sems):
    z, x, y = where[0], where[1], where[2]
    width = mine_ref.shape[2]
    copies = []
    for side, dst in ((0, other_ref), (1, mine_ref)):
        for j in range(n_line):
            shard = lax.rem(z - j + n_line, n_line) * 2 + (x if side else 1 - x)
            for h in range(2):
                half = 1 - y if h else y
                start = pl.multiple_of((shard * 2 + half) * width, width)
                copy = pltpu.make_async_copy(
                    x_ref.at[:, pl.ds(start, width)],
                    dst.at[2 * j + h],
                    sems.at[side, 2 * j + h],
                )
                copy.start()
                copies.append(copy)
    for copy in copies:
        copy.wait()


def project_kernel(n_parts, where, *refs):
    x_refs, own_ref = refs[:4], refs[4]
    piece_refs = refs[5 : 5 + n_parts - 2]
    own_out, other_out, x_buf, w_buf, x_sems, w_sems = refs[5 + n_parts - 2 :]
    y, core = where[2], where[3]
    tokens = x_refs[0].shape[1]
    rows, columns = w_buf.shape[1:]
    places = (core, 1 - core, 2 + core, 3 - core)
    copies = []
    for p in range(n_parts):
        if p < 2:
            half = y if p == 0 else 1 - y
            src = own_ref.at[
                pl.ds(pl.multiple_of(half * rows, rows), rows),
                pl.ds(pl.multiple_of(core * columns, columns), columns),
            ]
        else:
            src = piece_refs[p - 2]
        copies.append([pltpu.make_async_copy(src, w_buf.at[p], w_sems.at[p])])
        for a in range(4):
            copies[p].append(
                pltpu.make_async_copy(
                    x_refs[a].at[p],
                    x_buf.at[p, pl.ds(pl.multiple_of(places[a] * tokens, tokens), tokens), :],
                    x_sems.at[p, a],
                )
            )
        for copy in copies[p]:
            copy.start()
    total = None
    for p in range(n_parts):
        for copy in copies[p]:
            copy.wait()
        term = jnp.dot(x_buf[p], w_buf[p], preferred_element_type=jnp.float32)
        total = term if total is None else total + term
    own_out[...] = total[: 2 * tokens]
    other_out[...] = total[2 * tokens :].astype(other_out.dtype)


def project(where, x_parts, own_weight, pieces, other_dtype):
    n_parts, tokens, rows = x_parts[0].shape
    columns = own_weight.shape[1] // 2
    return pl.pallas_call(
        functools.partial(project_kernel, n_parts),
        out_shape=(
            jax.ShapeDtypeStruct((2 * tokens, columns), jnp.float32),
            jax.ShapeDtypeStruct((2 * tokens, columns), other_dtype),
        ),
        in_specs=[SMEM] + [ANY] * (5 + len(pieces)),
        out_specs=(VMEM, VMEM),
        scratch_shapes=[
            pltpu.VMEM((n_parts, 4 * tokens, rows), jnp.bfloat16),
            pltpu.VMEM((n_parts, rows, columns), jnp.bfloat16),
            pltpu.SemaphoreType.DMA((n_parts, 4)),
            pltpu.SemaphoreType.DMA((n_parts,)),
        ],
        compiler_params=PARAMS,
        cost_estimate=cost(
            2 * 4 * tokens * n_parts * rows * columns,
            2 * n_parts * rows * (4 * tokens + columns) + 16 * tokens * columns,
        ),
    )(where, *x_parts, own_weight, *pieces)


def finish_keys_kernel(own_ref, came_ref, cosine_ref, sine_ref, out_ref):
    for h in range(out_ref.shape[1] // HD):
        span = slice(h * HD, (h + 1) * HD)
        key = own_ref[:, span] + came_ref[:, span]
        out_ref[:, span] = turn(key, cosine_ref[...], sine_ref[...]).astype(jnp.bfloat16)


def turn_queries_kernel(q_ref, cosine_ref, sine_ref, out_ref):
    for h in range(out_ref.shape[0]):
        query = q_ref[:, h * HD : (h + 1) * HD].astype(jnp.float32)
        out_ref[h] = turn(query, cosine_ref[...], sine_ref[...]).astype(jnp.bfloat16)


def attend_kernel(n_chips, group, where, q_ref, bias_ref, *refs):
    key_refs, value_refs, out_ref = refs[:2], refs[2:4], refs[4]
    core = where[3]
    heads_here = key_refs[0].shape[2] // HD
    span_rows = key_refs[0].shape[1]
    bias = bias_ref[...]
    scale = HD ** (-0.5) * LOG2E
    for side in range(2):
        first_head = (1 - core if side else core) * heads_here
        for i in range(heads_here):
            span = slice(i * HD, (i + 1) * HD)
            keys = key_refs[side][:, :, span].reshape(n_chips * span_rows, HD)
            values = value_refs[side][:, :, span].reshape(n_chips * span_rows, HD)
            for g in range(group):
                head = (first_head + i) * group + g
                query = q_ref[head]
                scores = lax.dot_general(
                    query, keys, (((1,), (1,)), ((), ())), preferred_element_type=jnp.float32
                )
                scores = scores + bias
                top = jnp.max(scores, axis=1, keepdims=True)
                probabilities = jnp.exp2((scores - top) * scale)
                row_total = jnp.sum(probabilities, axis=1, keepdims=True)
                mixed = jnp.dot(
                    probabilities.astype(jnp.bfloat16),
                    values,
                    preferred_element_type=jnp.float32,
                )
                out_ref[:, pl.ds(pl.multiple_of(head * HD, HD), HD)] = (
                    mixed / row_total
                ).astype(jnp.bfloat16)


def on_device(n_ctx, n_dp, x_tokens, queries, key_weight, value_weight, positions, block_lists):
    n_line, n_chips = n_dp // 2, n_ctx // 2
    tokens_local, query_local = x_tokens[0], queries[0]
    tok_rows, query_width = query_local.shape
    shard_rows, key_width = key_weight.shape
    half_rows, half_columns = shard_rows // 2, key_width // 2
    group = query_width // key_width
    ctx, dp = lax.axis_index("ctx"), lax.axis_index("dp")
    chip, core = ctx // 2, ctx % 2
    y = chip % 2
    where = jnp.stack([dp // 2, dp % 2, y, core]).astype(jnp.int32)

    def over_core(array):
        return lax.ppermute(array, "ctx", [(i, i ^ 1) for i in range(n_ctx)])

    def over_y(array):
        return lax.ppermute(array, "ctx", [(i, i ^ 2) for i in range(n_ctx)])

    def over_x(array):
        return lax.ppermute(array, "dp", [(i, i ^ 1) for i in range(n_dp)])

    def over_z(array, step):
        return lax.ppermute(array, "dp", [(i, (i + 2 * step) % n_dp) for i in range(n_dp)])

    def from_chip(array, step, across_x=False):
        if not across_x:
            return lax.ppermute(
                array, "ctx", [(i, (i + 2 * step) % n_ctx) for i in range(n_ctx)]
            )
        pairs = [
            (i * n_dp + d, ((i + 2 * step) % n_ctx) * n_dp + (d ^ 1))
            for i in range(n_ctx)
            for d in range(n_dp)
        ]
        return lax.ppermute(array, ("ctx", "dp"), pairs)

    key_own, value_own = pl.pallas_call(
        cut_weights_kernel,
        out_shape=(jax.ShapeDtypeStruct((half_rows, half_columns), jnp.bfloat16),) * 2,
        in_specs=[SMEM, ANY, ANY],
        out_specs=(ANY, ANY),
        scratch_shapes=[pltpu.SemaphoreType.DMA((2,))],
        cost_estimate=cost(0, 8 * half_rows * half_columns),
    )(where, key_weight, value_weight)
    mine, other = pl.pallas_call(
        functools.partial(cut_tokens_kernel, n_line),
        out_shape=(jax.ShapeDtypeStruct((2 * n_line, tok_rows, half_rows), jnp.bfloat16),) * 2,
        in_specs=[SMEM, ANY],
        out_specs=(ANY, ANY),
        scratch_shapes=[pltpu.SemaphoreType.DMA((2, 2 * n_line))],
        cost_estimate=cost(0, 4 * tokens_local.size),
    )(where, tokens_local)

    def gather_pieces(own):
        came = [None] * n_line
        up = n_line // 2
        came[0] = own
        for j in range(1, up + 1):
            came[j] = over_z(came[j - 1], 1)
            k = n_line - j
            if k > up:
                came[k] = over_z(came[(k + 1) % n_line], -1)
        pieces = []
        for j in range(1, n_line):
            pieces += [came[j], over_y(came[j])]
        return pieces

    key_pieces = gather_pieces(key_own)
    neighbour = over_x(other)
    value_pieces = gather_pieces(value_own)
    sibling = over_core(mine)
    neighbour_sibling = over_core(neighbour)
    x_parts = (mine, sibling, neighbour, neighbour_sibling)

    token_pos = positions[0]
    pos_pair = jnp.stack([token_pos, over_core(positions)[0]])
    pos_chip = jnp.where(core == 0, pos_pair, pos_pair[::-1]).reshape(-1)
    cosine, sine_part = rope_tables(pos_chip)
    own_rows = core * tok_rows
    query_cosine = lax.dynamic_slice_in_dim(cosine, own_rows, tok_rows, 0)
    query_sine = lax.dynamic_slice_in_dim(sine_part, own_rows, tok_rows, 0)
    n_heads = query_width // HD
    query_rot = pl.pallas_call(
        turn_queries_kernel,
        out_shape=jax.ShapeDtypeStruct((n_heads, tok_rows, HD), jnp.bfloat16),
        in_specs=[VMEM] * 3,
        out_specs=VMEM,
        cost_estimate=cost(3 * query_local.size, 4 * query_local.size),
    )(query_local, query_cosine, query_sine)

    chip_rows = 2 * tok_rows
    source_chip = jnp.remainder(chip - jnp.arange(n_chips, dtype=jnp.int32), n_chips)
    key_index = (
        source_chip[:, None] * chip_rows + jnp.arange(chip_rows, dtype=jnp.int32)[None, :]
    ).reshape(-1)
    query_index = ctx * tok_rows + jnp.arange(tok_rows, dtype=jnp.int32)
    member = jnp.any(
        block_lists[0][:, :, None] == (key_index // BLOCK)[None, None, :], axis=1
    )
    allowed = jnp.repeat(member, BLOCK, axis=0) & (key_index[None, :] <= query_index[:, None])
    bias = jnp.where(allowed, 0.0, neg_large).astype(jnp.float32)

    key_part, key_away = project(where, x_parts, key_weight, key_pieces, jnp.float32)
    key_here = pl.pallas_call(
        finish_keys_kernel,
        out_shape=jax.ShapeDtypeStruct(key_part.shape, jnp.bfloat16),
        in_specs=[VMEM] * 4,
        out_specs=VMEM,
        cost_estimate=cost(4 * key_part.size, 10 * key_part.size),
    )(key_part, over_x(key_away), cosine, sine_part)
    keys = jnp.stack([key_here] + [from_chip(key_here, j) for j in range(1, n_chips)])
    keys_other = over_core(keys)

    value_part, value_away = project(where, x_parts, value_weight, value_pieces, jnp.bfloat16)
    value_sent = value_part.astype(jnp.bfloat16)
    value_list = [value_part + over_x(value_away).astype(jnp.float32)]
    for j in range(1, n_chips):
        value_list.append(
            from_chip(value_sent, j).astype(jnp.float32)
            + from_chip(value_away, j, True).astype(jnp.float32)
        )
    values = jnp.stack(value_list).astype(jnp.bfloat16)
    values_other = over_core(values)

    span_rows = n_chips * chip_rows
    mixed = pl.pallas_call(
        functools.partial(attend_kernel, n_chips, group),
        out_shape=jax.ShapeDtypeStruct((tok_rows, query_width), jnp.bfloat16),
        in_specs=[SMEM] + [VMEM] * 6,
        out_specs=VMEM,
        compiler_params=PARAMS,
        cost_estimate=cost(
            4 * tok_rows * query_width * span_rows,
            4 * (tok_rows * query_width + span_rows * key_width),
            tok_rows * n_heads * span_rows,
        ),
    )(where, query_rot, bias, keys, keys_other, values, values_other)
    return mixed[None]


def solution(mesh):
    return jax.shard_map(
        functools.partial(on_device, mesh.shape["ctx"], mesh.shape["dp"]),
        mesh=mesh,
        in_specs=(
            P("dp", "ctx", None),
            P("dp", "ctx", None),
            P("dp", None),
            P("dp", None),
            P("dp", "ctx"),
            P("dp", "ctx", None),
        ),
        out_specs=P("dp", "ctx", None),
        check_vma=False,
    )
```

time: 295 us -> 210 us (0.71)
  waiting for transfers between devices: 240 us -> 56.8 us
  Pallas kernels: 0 us -> 111 us
  starting transfers between devices: 0.04 us -> 30.6 us
  matrix products: 20.7 us -> 0 us
  between operations: 13.6 us -> 0.21 us
  local copies, waits for them, and re-layouts: 8.65 us -> 3.64 us
  other arithmetic: 10.8 us -> 7.02 us
    all_gather x2 -> x0, waiting for transfers between devices: 240 us -> none  [the longest x1 229 us: on_device(): lax.all_gather(paired_weight, 'dp', axis=0, tiled=True)]
    pallas_call x0 -> x7, Pallas kernels: none -> 111 us  [the longest x1 65.6 us: on_device(): pl.pallas_call(functools.partial(cut_tokens_kernel, n_line), out_shape=(j...]
    ppermute x0 -> x23, waiting for transfers between devices: none -> 56.8 us  [the longest x3 24.2 us: over_x(): return lax.ppermute(array, 'dp', [(i, i ^ 1) for i in range(n_dp)])]
    ppermute x0 -> x23, starting transfers between devices: none -> 30.6 us  [the longest x6 11.6 us: over_z(): lax.ppermute(array, 'dp', [(i, (i + 2 * step) % n_dp) for i in range(n_dp)])]
    dot_general x9 -> x0, matrix products: 20.7 us -> none  [the longest x1 8.15 us: on_device(): jnp.dot(tokens_local, lax.all_gather(paired_weight, 'dp', axis=0, tiled=T...]
    concatenate x4 -> x2, other arithmetic: 4.59 us -> 1.6 us  [the longest x1 0.84 us: rope_tables(): jnp.concatenate([cosine, cosine], axis=1)]
  transfers between devices with their start and end apart: 2 -> 23, of which waited for: 2 -> 10; matrix products, arithmetic and copies ran while one was open for 2% -> 3% of each run, Pallas kernels for 0% -> 17%
where the time goes in v1:
time: 210 us; the launch traced here: 209 us
  Pallas kernels  111 us (53%)
  waiting for transfers between devices  56.8 us (27%)
  starting transfers between devices  30.6 us (15%)
  other arithmetic  7.02 us (3%)
  local copies, waits for them, and re-layouts  3.64 us (2%)
    pallas_call x1, Pallas kernels, on_device(): pl.pallas_call(functools.partial(cut_tokens_kernel, n_line), out_shape=(j...  65.6 us
    ppermute x3, waiting for transfers between devices, over_x(): return lax.ppermute(array, 'dp', [(i, i ^ 1) for i in range(n_dp)])  24.2 us
    ppermute x6, waiting for transfers between devices, over_z(): lax.ppermute(array, 'dp', [(i, (i + 2 * step) % n_dp) for i in range(n_dp)])  24.1 us
    pallas_call x1, Pallas kernels, on_device(): pl.pallas_call(cut_weights_kernel, out_shape=(jax.ShapeDtypeStruct((half_...  17.7 us
    pallas_call x2, Pallas kernels, project(): pl.pallas_call(functools.partial(project_kernel, n_parts), out_shape=(jax...  12.9 us
    ppermute x6, starting transfers between devices, over_z(): lax.ppermute(array, 'dp', [(i, (i + 2 * step) % n_dp) for i in range(n_dp)])  11.6 us
    pallas_call x1, Pallas kernels, on_device(): pl.pallas_call(functools.partial(attend_kernel, n_chips, group), out_shap...  10 us
    ppermute x6, starting transfers between devices, over_y(): return lax.ppermute(array, 'ctx', [(i, i ^ 2) for i in range(n_ctx)])  8.33 us
  transfers between devices with their start and end apart: 23, of which 10 were waited for; matrix products, arithmetic and copies ran while one was open for 3% of the time, Pallas kernels for 17%

profile of v1, /device:TPU:0, one launch (start us, length us, event | category | flops | bytes accessed | tf_op | source)
XLA Modules:
  0.0 208.9 jit_solution(1118665009674735302)
XLA Ops:
  0.0 0.7 pad_add_fusion.1.where
  0.7 65.6 %shard_map.74 = (bf16[8,128,512]{2,1,0:T(8,128)(2,1)}, bf16[8,128,512]{2,1,0:T(8,128)(2,1)}) custom-call(s32[4]{0:T(128)} %pad_add_fusion.1.where, bf16[128,8192]{1,0:T(8,128)(2,1)} %bitcast.23), custom_call_target="tpu_custom_call" | custom-call | bytes 4194304 | tf_op jit(solution)/shard_map/pallas_call | solution.py:249
  66.3 0.0 copy-start.2
  66.3 3.0 %collective-permute-start.2 = (bf16[8,128,512]{2,1,0:T(8,128)(2,1)}, bf16[8,128,512]{2,1,0:T(8,128)(2,1)S(1)}, u32[]{:S(2)}, u32[]{:S(2)}) collective-permute-start(bf16[8,128,512]{2,1,0:T(8,128)(2,1)} %get-tuple-element.14), channel_id=1, source_target_pairs={{0,1},{1,0},{2,3},{3,2},{4,5},{5,4},{6,7},{7,6},{8,9},{9,8},{10,11... | collective-permute-start | bytes 3145736 | tf_op jit(solution)/shard_map/ppermute | solution.py:224
  69.3 0.0 collective-permute-start.1
  69.3 23.4 %collective-permute-done.2.refs_2_ = bf16[8,128,512]{2,1,0:T(8,128)(2,1)S(1)} collective-permute-done((bf16[8,128,512]{2,1,0:T(8,128)(2,1)}, bf16[8,128,512]{2,1,0:T(8,128)(2,1)S(1)}, u32[]{:S(2)}, u32[]{:S(2)}) %collective-permute-start.2) | collective-permute-done | bytes 1048608 | tf_op jit(solution)/shard_map/ppermute | solution.py:224
  92.6 0.0 collective-permute-start.3
  92.6 0.5 collective-permute-start
  93.2 17.7 %shard_map.75 = (bf16[512,256]{1,0:T(8,128)(2,1)}, bf16[512,256]{1,0:T(8,128)(2,1)}) custom-call(s32[4]{0:T(128)} %pad_add_fusion.1.where, bf16[1024,512]{1,0:T(8,128)(2,1)} %refs_4_.2, bf16[1024,512]{1,0:T(8,128)(2,1)} %refs_4_.3), custom_call_target="tpu_custom_call" | custom-call | bytes 1048576 | tf_op jit(solution)/shard_map/pallas_call | solution.py:241
  110.8 1.9 collective-permute-start.13
  112.7 2.1 %collective-permute-start.17 = (bf16[512,256]{1,0:T(8,128)(2,1)}, bf16[512,256]{1,0:T(8,128)(2,1)S(1)}, u32[]{:S(2)}, u32[]{:S(2)}) collective-permute-start(bf16[512,256]{1,0:T(8,128)(2,1)} %get-tuple-element.18), channel_id=1, source_target_pairs={{0,6},{1,7},{2,0},{3,1},{4,2},{5,3},{6,4},{7,5},{8,14},{9,15},{10,... | collective-permute-start | bytes 786440 | tf_op jit(solution)/shard_map/ppermute | solution.py:227
  114.8 0.0 collective-permute-done
  114.8 0.0 collective-permute-start.4
  114.8 7.4 %collective-permute-done.13.refs_5_ = bf16[512,256]{1,0:T(8,128)(2,1)} collective-permute-done((bf16[512,256]{1,0:T(8,128)(2,1)}, bf16[512,256]{1,0:T(8,128)(2,1)}, u32[]{:S(2)}, u32[]{:S(2)}) %collective-permute-start.13) | collective-permute-done | bytes 262176 | tf_op jit(solution)/shard_map/ppermute | solution.py:227
  122.2 7.6 %collective-permute-start.8 = (bf16[512,256]{1,0:T(8,128)(2,1)}, bf16[512,256]{1,0:T(8,128)(2,1)}, u32[]{:S(2)}, u32[]{:S(2)}) collective-permute-start(bf16[512,256]{1,0:T(8,128)(2,1)} %get-tuple-element.15), channel_id=1, source_target_pairs={{0,6},{1,7},{2,0},{3,1},{4,2},{5,3},{6,4},{7,5},{8,14},{9,15},{10,... | collective-permute-start | bytes 786440 | tf_op jit(solution)/shard_map/ppermute | solution.py:227
  129.8 0.0 collective-permute-start.15
  129.9 3.5 %collective-permute-done.4.refs_5_ = bf16[512,256]{1,0:T(8,128)(2,1)S(1)} collective-permute-done((bf16[512,256]{1,0:T(8,128)(2,1)}, bf16[512,256]{1,0:T(8,128)(2,1)S(1)}, u32[]{:S(2)}, u32[]{:S(2)}) %collective-permute-start.4) | collective-permute-done | bytes 262176 | tf_op jit(solution)/shard_map/ppermute | solution.py:227
  133.4 1.8 collective-permute-start.14
  135.2 0.1 add_bitcast_fusion
  135.2 2.6 %collective-permute-done.8.refs_9_ = bf16[512,256]{1,0:T(8,128)(2,1)} collective-permute-done((bf16[512,256]{1,0:T(8,128)(2,1)}, bf16[512,256]{1,0:T(8,128)(2,1)}, u32[]{:S(2)}, u32[]{:S(2)}) %collective-permute-start.8) | collective-permute-done | bytes 262176 | tf_op jit(solution)/shard_map/ppermute | solution.py:227
  137.8 1.7 collective-permute-start.18
  139.6 4.5 %collective-permute-done.15.refs_7_ = bf16[512,256]{1,0:T(8,128)(2,1)} collective-permute-done((bf16[512,256]{1,0:T(8,128)(2,1)}, bf16[512,256]{1,0:T(8,128)(2,1)}, u32[]{:S(2)}, u32[]{:S(2)}) %collective-permute-start.15) | collective-permute-done | bytes 262176 | tf_op jit(solution)/shard_map/ppermute | solution.py:227
  144.1 0.0 collective-permute-start.6
  144.1 0.0 collective-permute-done.14.refs_6_
  144.1 1.5 collective-permute-start.16
  145.7 0.7 collective-permute-done.18.refs_10_
  146.4 1.3 collective-permute-start.5
  147.6 6.0 %collective-permute-done.6.refs_7_ = bf16[512,256]{1,0:T(8,128)(2,1)} collective-permute-done((bf16[512,256]{1,0:T(8,128)(2,1)S(1)}, bf16[512,256]{1,0:T(8,128)(2,1)}, u32[]{:S(2)}, u32[]{:S(2)}) %collective-permute-start.6) | collective-permute-done | bytes 262176 | tf_op jit(solution)/shard_map/ppermute | solution.py:227
  153.7 1.3 collective-permute-start.9
  154.9 0.7 collective-permute-start.7
  155.7 0.0 collective-permute-done.1.refs_1_
  155.7 0.9 copy-done.5
  156.7 6.4 %shard_map.78 = (f32[256,256]{1,0:T(8,128)S(1)}, bf16[256,256]{1,0:T(8,128)(2,1)S(1)}) custom-call(s32[4]{0:T(128)S(1)} %copy-done.7, bf16[8,128,512]{2,1,0:T(8,128)(2,1)S(1)} %copy-done.2, bf16[8,128,512]{2,1,0:T(8,128)(2,1)} %collective-permute-done.1.refs_1_, bf16[8,128,512]{2,1,0:T(8,128)(2,1)S(1)} %collective-permute-done.2.refs_2_, ...), custom_call_target="tpu_custom_call" | custom-call | flops 1073741824 | bytes 6815744 | tf_op jit(solution)/shard_map/pallas_call | solution.py:137
  163.1 1.3 collective-permute-start.19
  164.4 0.7 select_bitcast_fusion
  165.1 1.6 collective-permute-start.21
  166.7 5.0 %collective-permute-done.7.refs_8_ = bf16[512,256]{1,0:T(8,128)(2,1)S(1)} collective-permute-done((bf16[512,256]{1,0:T(8,128)(2,1)}, bf16[512,256]{1,0:T(8,128)(2,1)S(1)}, u32[]{:S(2)}, u32[]{:S(2)}) %collective-permute-start.7) | collective-permute-done | bytes 262176 | tf_op jit(solution)/shard_map/ppermute | solution.py:221
  171.6 6.5 %shard_map.76 = (f32[256,256]{1,0:T(8,128)S(1)}, f32[256,256]{1,0:T(8,128)S(1)}) custom-call(s32[4]{0:T(128)S(1)} %copy-done.7, bf16[8,128,512]{2,1,0:T(8,128)(2,1)S(1)} %copy-done.2, bf16[8,128,512]{2,1,0:T(8,128)(2,1)} %collective-permute-done.1.refs_1_, bf16[8,128,512]{2,1,0:T(8,128)(2,1)S(1)} %collective-permute-done.2.refs_2_, ...), custom_call_target="tpu_custom_call" | custom-call | flops 1073741824 | bytes 6815744 | tf_op jit(solution)/shard_map/pallas_call | solution.py:137
  178.1 0.0 copy-start.6
  178.1 0.7 copy-done.6
  178.8 1.2 collective-permute-start.10
  180.1 0.0 collective-permute-done.19
  180.1 1.6 collective-permute-start.20
  181.7 1.8 fusion.6
  183.6 0.8 pad_maximum_fusion.2
  184.4 0.8 collective-permute-done.10.came_ref
  185.2 0.7 copy-done.8
  185.9 1.9 shard_map.77
  187.8 1.3 collective-permute-start.11
  189.1 0.0 collective-permute-done.21
  189.1 0.0 collective-permute-done.20
  189.1 0.9 fusion.2
  190.1 0.1 collective-permute-start.22
  190.2 2.8 %collective-permute-done.11 = bf16[256,256]{1,0:T(8,128)(2,1)S(1)} collective-permute-done((bf16[256,256]{1,0:T(8,128)(2,1)}, bf16[256,256]{1,0:T(8,128)(2,1)S(1)}, u32[]{:S(2)}, u32[]{:S(2)}) %collective-permute-start.11) | collective-permute-done | bytes 131104 | tf_op jit(solution)/shard_map/ppermute | solution.py:231
  193.0 0.9 pad_maximum_fusion.refs_0_
  193.9 0.1 collective-permute-start.12
  194.0 0.1 compare_reduce_fusion
  194.1 0.1 fusion.bias_ref
  194.2 0.8 fusion.9
  195.0 2.7 %shard_map.73.q_ref = bf16[32,128,128]{2,1,0:T(8,128)(2,1)} custom-call(bf16[128,4096]{1,0:T(8,128)(2,1)} %bitcast.24, f32[128,128]{1,0:T(8,128)} %get-tuple-element.27.cosine_ref, f32[128,128]{1,0:T(8,128)} %get-tuple-element.26.sine_ref), custom_call_target="tpu_custom_call" | custom-call | flops 1572864 | bytes 2097152 | tf_op jit(solution)/shard_map/pallas_call | solution.py:287
  197.7 0.0 collective-permute-done.22.refs_3_
  197.7 0.0 collective-permute-done.12.refs_1_
  197.7 1.2 copy-done.3
  198.9 10.0 %shard_map.79 = bf16[128,4096]{1,0:T(8,128)(2,1)} custom-call(s32[4]{0:T(128)S(1)} %copy-done.7, bf16[32,128,128]{2,1,0:T(8,128)(2,1)S(1)} %copy-done.3, f32[128,512]{1,0:T(8,128)S(1)} %fusion.bias_ref, bf16[2,256,256]{2,1,0:T(8,128)(2,1)S(1)} %pad_maximum_fusion.refs_0_, bf16[2,256,256]{2,1,0:T(8,128)(2,1)S(1)} %collective-permute-done.12.refs_1_, ...), custom_call_target="tpu_custom_call" | custom-call | flops 1073741824 | bytes 3145728 | tf_op jit(solution)/shard_map/pallas_call | solution.py:330
  (37 shorter events, 0.2 us)
Async XLA Ops:
  0.0 92.6 %copy-start.9 = (s32[1,128]{1,0:T(1,128)S(1)}, s32[1,128]{1,0:T(1,128)}, u32[]{:S(2)}) copy-start(s32[1,128]{1,0:T(1,128)} %param.11) | copy-start | bytes 1540
  0.7 155.0 %copy-start = (bf16[1024,512]{1,0:T(8,128)(2,1)S(1)}, bf16[1024,512]{1,0:T(8,128)(2,1)}, u32[]{:S(2)}) copy-start(bf16[1024,512]{1,0:T(8,128)(2,1)} %refs_4_.3) | copy-start | bytes 3145732
  0.7 155.0 %copy-start.7 = (s32[4]{0:T(128)S(1)}, s32[4]{0:T(128)}, u32[]{:S(2)}) copy-start(s32[4]{0:T(128)} %pad_add_fusion.1.where) | copy-start | bytes 52
  66.3 89.5 %copy-start.2 = (bf16[8,128,512]{2,1,0:T(8,128)(2,1)S(1)}, bf16[8,128,512]{2,1,0:T(8,128)(2,1)}, u32[]{:S(2)}) copy-start(bf16[8,128,512]{2,1,0:T(8,128)(2,1)} %get-tuple-element.13.refs_0_) | copy-start | bytes 3145732
  66.3 26.4 %collective-permute-start.2 = (bf16[8,128,512]{2,1,0:T(8,128)(2,1)}, bf16[8,128,512]{2,1,0:T(8,128)(2,1)S(1)}, u32[]{:S(2)}, u32[]{:S(2)}) collective-permute-start(bf16[8,128,512]{2,1,0:T(8,128)(2,1)} %get-tuple-element.14), channel_id=1, source_target_pairs={{0,1},{1,0},{2,3},{3,2},{4,5},{5,4},{6,7},{7,6},{8,9},{9,8},{10,11... | collective-permute-start | bytes 3145736 | tf_op jit(solution)/shard_map/ppermute | solution.py:224
  69.3 86.4 %collective-permute-start.1 = (bf16[8,128,512]{2,1,0:T(8,128)(2,1)}, bf16[8,128,512]{2,1,0:T(8,128)(2,1)}, u32[]{:S(2)}, u32[]{:S(2)}) collective-permute-start(bf16[8,128,512]{2,1,0:T(8,128)(2,1)} %get-tuple-element.13.refs_0_), channel_id=1, source_target_pairs={{0,8},{8,0},{16,24},{24,16},{1,9},{9,1},{17,25},{25,17},{2,10},{10... | collective-permute-start | bytes 3145736 | tf_op jit(solution)/shard_map/ppermute | solution.py:218
  92.6 63.1 %collective-permute-start.3 = (bf16[8,128,512]{2,1,0:T(8,128)(2,1)S(1)}, bf16[8,128,512]{2,1,0:T(8,128)(2,1)}, u32[]{:S(2)}, u32[]{:S(2)}) collective-permute-start(bf16[8,128,512]{2,1,0:T(8,128)(2,1)S(1)} %collective-permute-done.2.refs_2_), channel_id=1, source_target_pairs={{0,8},{8,0},{16,24},{24,16},{1,9},{9,1},{17,25},{25,17},{2,10},{10... | collective-permute-start | bytes 3145736 | tf_op jit(solution)/shard_map/ppermute | solution.py:218
  92.6 22.2 %collective-permute-start = (s32[1,128]{1,0:T(1,128)S(1)}, s32[1,128]{1,0:T(1,128)S(1)}, u32[]{:S(2)}, u32[]{:S(2)}) collective-permute-start(s32[1,128]{1,0:T(1,128)S(1)} %copy-done.9), channel_id=1, source_target_pairs={{0,8},{8,0},{16,24},{24,16},{1,9},{9,1},{17,25},{25,17},{2,10},{10... | collective-permute-start | bytes 1544 | tf_op jit(solution)/shard_map/ppermute | solution.py:218
  110.8 11.4 %collective-permute-start.13 = (bf16[512,256]{1,0:T(8,128)(2,1)}, bf16[512,256]{1,0:T(8,128)(2,1)}, u32[]{:S(2)}, u32[]{:S(2)}) collective-permute-start(bf16[512,256]{1,0:T(8,128)(2,1)} %get-tuple-element.18), channel_id=1, source_target_pairs={{0,2},{1,3},{2,4},{3,5},{4,6},{5,7},{6,0},{7,1},{8,10},{9,11},{10,... | collective-permute-start | bytes 786440 | tf_op jit(solution)/shard_map/ppermute | solution.py:227
  112.7 17.1 %collective-permute-start.17 = (bf16[512,256]{1,0:T(8,128)(2,1)}, bf16[512,256]{1,0:T(8,128)(2,1)S(1)}, u32[]{:S(2)}, u32[]{:S(2)}) collective-permute-start(bf16[512,256]{1,0:T(8,128)(2,1)} %get-tuple-element.18), channel_id=1, source_target_pairs={{0,6},{1,7},{2,0},{3,1},{4,2},{5,3},{6,4},{7,5},{8,14},{9,15},{10,... | collective-permute-start | bytes 786440 | tf_op jit(solution)/shard_map/ppermute | solution.py:227
  114.8 40.9 %copy-start.10 = (s32[1,128]{1,0:T(1,128)}, s32[1,128]{1,0:T(1,128)S(1)}, u32[]{:S(2)}) copy-start(s32[1,128]{1,0:T(1,128)S(1)} %collective-permute-done) | copy-start | bytes 1540
  114.8 18.6 %collective-permute-start.4 = (bf16[512,256]{1,0:T(8,128)(2,1)}, bf16[512,256]{1,0:T(8,128)(2,1)S(1)}, u32[]{:S(2)}, u32[]{:S(2)}) collective-permute-start(bf16[512,256]{1,0:T(8,128)(2,1)} %get-tuple-element.15), channel_id=1, source_target_pairs={{0,2},{1,3},{2,4},{3,5},{4,6},{5,7},{6,0},{7,1},{8,10},{9,11},{10,... | collective-permute-start | bytes 786440 | tf_op jit(solution)/shard_map/ppermute | solution.py:227
  122.2 15.6 %collective-permute-start.8 = (bf16[512,256]{1,0:T(8,128)(2,1)}, bf16[512,256]{1,0:T(8,128)(2,1)}, u32[]{:S(2)}, u32[]{:S(2)}) collective-permute-start(bf16[512,256]{1,0:T(8,128)(2,1)} %get-tuple-element.15), channel_id=1, source_target_pairs={{0,6},{1,7},{2,0},{3,1},{4,2},{5,3},{6,4},{7,5},{8,14},{9,15},{10,... | collective-permute-start | bytes 786440 | tf_op jit(solution)/shard_map/ppermute | solution.py:227
  129.8 3.5 %copy-start.4 = (bf16[512,256]{1,0:T(8,128)(2,1)}, bf16[512,256]{1,0:T(8,128)(2,1)S(1)}, u32[]{:S(2)}) copy-start(bf16[512,256]{1,0:T(8,128)(2,1)S(1)} %collective-permute-done.17.refs_9_) | copy-start | bytes 786436
  129.8 14.2 %collective-permute-start.15 = (bf16[512,256]{1,0:T(8,128)(2,1)}, bf16[512,256]{1,0:T(8,128)(2,1)}, u32[]{:S(2)}, u32[]{:S(2)}) collective-permute-start(bf16[512,256]{1,0:T(8,128)(2,1)} %collective-permute-done.13.refs_5_), channel_id=1, source_target_pairs={{0,2},{1,3},{2,4},{3,5},{4,6},{5,7},{6,0},{7,1},{8,10},{9,11},{10,... | collective-permute-start | bytes 786440 | tf_op jit(solution)/shard_map/ppermute | solution.py:227
  133.4 10.7 %collective-permute-start.14 = (bf16[512,256]{1,0:T(8,128)(2,1)}, bf16[512,256]{1,0:T(8,128)(2,1)}, u32[]{:S(2)}, u32[]{:S(2)}) collective-permute-start(bf16[512,256]{1,0:T(8,128)(2,1)} %collective-permute-done.13.refs_5_), channel_id=1, source_target_pairs={{0,16},{8,24},{16,0},{24,8},{1,17},{9,25},{17,1},{25,9},{2,18},{10... | collective-permute-start | bytes 786440 | tf_op jit(solution)/shard_map/ppermute | solution.py:221
  137.8 8.5 %collective-permute-start.18 = (bf16[512,256]{1,0:T(8,128)(2,1)}, bf16[512,256]{1,0:T(8,128)(2,1)}, u32[]{:S(2)}, u32[]{:S(2)}) collective-permute-start(bf16[512,256]{1,0:T(8,128)(2,1)} %copy-done.4), channel_id=1, source_target_pairs={{0,16},{8,24},{16,0},{24,8},{1,17},{9,25},{17,1},{25,9},{2,18},{10... | collective-permute-start | bytes 786440 | tf_op jit(solution)/shard_map/ppermute | solution.py:221
  144.1 9.6 %collective-permute-start.6 = (bf16[512,256]{1,0:T(8,128)(2,1)S(1)}, bf16[512,256]{1,0:T(8,128)(2,1)}, u32[]{:S(2)}, u32[]{:S(2)}) collective-permute-start(bf16[512,256]{1,0:T(8,128)(2,1)S(1)} %collective-permute-done.4.refs_5_), channel_id=1, source_target_pairs={{0,2},{1,3},{2,4},{3,5},{4,6},{5,7},{6,0},{7,1},{8,10},{9,11},{10,... | collective-permute-start | bytes 786440 | tf_op jit(solution)/shard_map/ppermute | solution.py:227
  144.1 10.9 %collective-permute-start.16 = (bf16[512,256]{1,0:T(8,128)(2,1)}, bf16[512,256]{1,0:T(8,128)(2,1)}, u32[]{:S(2)}, u32[]{:S(2)}) collective-permute-start(bf16[512,256]{1,0:T(8,128)(2,1)} %collective-permute-done.15.refs_7_), channel_id=1, source_target_pairs={{0,16},{8,24},{16,0},{24,8},{1,17},{9,25},{17,1},{25,9},{2,18},{10... | collective-permute-start | bytes 786440 | tf_op jit(solution)/shard_map/ppermute | solution.py:221
  145.7 26.0 %copy-start.1 = (bf16[1024,512]{1,0:T(8,128)(2,1)S(1)}, bf16[1024,512]{1,0:T(8,128)(2,1)}, u32[]{:S(2)}) copy-start(bf16[1024,512]{1,0:T(8,128)(2,1)} %refs_4_.2) | copy-start | bytes 3145732
  146.4 20.3 %collective-permute-start.5 = (bf16[512,256]{1,0:T(8,128)(2,1)S(1)}, bf16[512,256]{1,0:T(8,128)(2,1)S(1)}, u32[]{:S(2)}, u32[]{:S(2)}) collective-permute-start(bf16[512,256]{1,0:T(8,128)(2,1)S(1)} %collective-permute-done.4.refs_5_), channel_id=1, source_target_pairs={{0,16},{8,24},{16,0},{24,8},{1,17},{9,25},{17,1},{25,9},{2,18},{10... | collective-permute-start | bytes 786440 | tf_op jit(solution)/shard_map/ppermute | solution.py:221
  153.7 13.0 %collective-permute-start.9 = (bf16[512,256]{1,0:T(8,128)(2,1)}, bf16[512,256]{1,0:T(8,128)(2,1)S(1)}, u32[]{:S(2)}, u32[]{:S(2)}) collective-permute-start(bf16[512,256]{1,0:T(8,128)(2,1)} %collective-permute-done.8.refs_9_), channel_id=1, source_target_pairs={{0,16},{8,24},{16,0},{24,8},{1,17},{9,25},{17,1},{25,9},{2,18},{10... | collective-permute-start | bytes 786440 | tf_op jit(solution)/shard_map/ppermute | solution.py:221
  154.9 16.7 %collective-permute-start.7 = (bf16[512,256]{1,0:T(8,128)(2,1)}, bf16[512,256]{1,0:T(8,128)(2,1)S(1)}, u32[]{:S(2)}, u32[]{:S(2)}) collective-permute-start(bf16[512,256]{1,0:T(8,128)(2,1)} %collective-permute-done.6.refs_7_), channel_id=1, source_target_pairs={{0,16},{8,24},{16,0},{24,8},{1,17},{9,25},{17,1},{25,9},{2,18},{10... | collective-permute-start | bytes 786440 | tf_op jit(solution)/shard_map/ppermute | solution.py:221
  155.7 1.0 copy-start.5
  156.7 7.8 %copy-start.11 = (s32[1,128]{1,0:T(1,128)S(1)}, s32[1,128]{1,0:T(1,128)}, u32[]{:S(2)}) copy-start(s32[1,128]{1,0:T(1,128)} %copy-done.10) | copy-start | bytes 1540
  163.1 17.0 %collective-permute-start.19 = (bf16[256,256]{1,0:T(8,128)(2,1)S(1)}, bf16[256,256]{1,0:T(8,128)(2,1)S(1)}, u32[]{:S(2)}, u32[]{:S(2)}) collective-permute-start(bf16[256,256]{1,0:T(8,128)(2,1)S(1)} %get-tuple-element.20), channel_id=1, source_target_pairs={{0,1},{1,0},{2,3},{3,2},{4,5},{5,4},{6,7},{7,6},{8,9},{9,8},{10,11... | collective-permute-start | bytes 393224 | tf_op jit(solution)/shard_map/ppermute | solution.py:224
  165.1 16.6 %copy-start.13 = (f32[64]{0:T(128)S(1)}, f32[64]{0:T(128)}, u32[]{:S(2)}) copy-start(f32[64]{0:T(128)} %constant.100) | copy-start | bytes 772
  165.1 16.6 %copy-start.14 = (s32[64]{0:T(128)S(1)}, s32[64]{0:T(128)}, u32[]{:S(2)}) copy-start(s32[64]{0:T(128)} %constant.96) | copy-start | bytes 772
  165.1 24.0 %collective-permute-start.21 = (bf16[256,256]{1,0:T(8,128)(2,1)S(1)}, bf16[256,256]{1,0:T(8,128)(2,1)}, u32[]{:S(2)}, u32[]{:S(2)}) collective-permute-start(bf16[256,256]{1,0:T(8,128)(2,1)S(1)} %get-tuple-element.20), channel_id=1, source_target_pairs={{0,17},{1,16},{2,19},{3,18},{4,21},{5,20},{6,23},{7,22},{8,25},{9,... | collective-permute-start | bytes 393224 | tf_op jit(solution)/shard_map/ppermute | solution.py:239
  178.1 0.7 copy-start.6
  178.8 15.2 %copy-start.12 = (s32[1,2,6]{2,1,0:T(2,128)S(1)}, s32[1,2,6]{2,1,0:T(2,128)}, u32[]{:S(2)}) copy-start(s32[1,2,6]{2,1,0:T(2,128)} %param.12) | copy-start | bytes 148
  178.8 6.4 %collective-permute-start.10 = (f32[256,256]{1,0:T(8,128)S(1)}, f32[256,256]{1,0:T(8,128)S(1)}, u32[]{:S(2)}, u32[]{:S(2)}) collective-permute-start(f32[256,256]{1,0:T(8,128)S(1)} %get-tuple-element.17), channel_id=1, source_target_pairs={{0,1},{1,0},{2,3},{3,2},{4,5},{5,4},{6,7},{7,6},{8,9},{9,8},{10,11... | collective-permute-start | bytes 786440 | tf_op jit(solution)/shard_map/ppermute | solution.py:224
  180.1 9.0 %collective-permute-start.20 = (bf16[256,256]{1,0:T(8,128)(2,1)S(1)}, bf16[256,256]{1,0:T(8,128)(2,1)S(1)}, u32[]{:S(2)}, u32[]{:S(2)}) collective-permute-start(bf16[256,256]{1,0:T(8,128)(2,1)S(1)} %get-tuple-element.22), channel_id=1, source_target_pairs={{0,16},{8,24},{16,0},{24,8},{1,17},{9,25},{17,1},{25,9},{2,18},{10... | collective-permute-start | bytes 393224 | tf_op jit(solution)/shard_map/ppermute | solution.py:231
  185.2 0.7 copy-start.8
  187.8 5.2 %collective-permute-start.11 = (bf16[256,256]{1,0:T(8,128)(2,1)}, bf16[256,256]{1,0:T(8,128)(2,1)S(1)}, u32[]{:S(2)}, u32[]{:S(2)}) collective-permute-start(bf16[256,256]{1,0:T(8,128)(2,1)} %shard_map.77), channel_id=1, source_target_pairs={{0,16},{8,24},{16,0},{24,8},{1,17},{9,25},{17,1},{25,9},{2,18},{10... | collective-permute-start | bytes 393224 | tf_op jit(solution)/shard_map/ppermute | solution.py:231
  190.1 7.6 %collective-permute-start.22 = (bf16[2,256,256]{2,1,0:T(8,128)(2,1)S(1)}, bf16[2,256,256]{2,1,0:T(8,128)(2,1)S(1)}, u32[]{:S(2)}, u32[]{:S(2)}) collective-permute-start(bf16[2,256,256]{2,1,0:T(8,128)(2,1)S(1)} %pad_maximum_fusion.1.refs_2_), channel_id=1, source_target_pairs={{0,8},{8,0},{16,24},{24,16},{1,9},{9,1},{17,25},{25,17},{2,10},{10... | collective-permute-start | bytes 786440 | tf_op jit(solution)/shard_map/ppermute | solution.py:218
  193.9 3.8 %collective-permute-start.12 = (bf16[2,256,256]{2,1,0:T(8,128)(2,1)S(1)}, bf16[2,256,256]{2,1,0:T(8,128)(2,1)S(1)}, u32[]{:S(2)}, u32[]{:S(2)}) collective-permute-start(bf16[2,256,256]{2,1,0:T(8,128)(2,1)S(1)} %pad_maximum_fusion.refs_0_), channel_id=1, source_target_pairs={{0,8},{8,0},{16,24},{24,16},{1,9},{9,1},{17,25},{25,17},{2,10},{10... | collective-permute-start | bytes 786440 | tf_op jit(solution)/shard_map/ppermute | solution.py:218
  197.7 1.2 copy-start.3

commit v2 on v1

v2 whole, which is shorter than its diff:
```python
import functools
import math

import jax
import jax.numpy as jnp
from jax import lax
from jax.experimental import pallas as pl
from jax.experimental.pallas import tpu as pltpu
from jax.sharding import PartitionSpec as P

HD = 128
BLOCK = 64
LOG2E = 1.4426950408889634

neg_large = -1e30
ANY = pl.BlockSpec(memory_space=pl.ANY)
VMEM = pl.BlockSpec(memory_space=pltpu.VMEM)
SMEM = pl.BlockSpec(memory_space=pltpu.SMEM)


def params(held):
    return pltpu.CompilerParams(vmem_limit_bytes=held + 6 * 1024 * 1024)


def cost(flops, bytes_accessed, transcendentals=0):
    return pl.CostEstimate(
        flops=flops, bytes_accessed=bytes_accessed, transcendentals=transcendentals
    )


def rope_periods(half_width):
    return jnp.array(
        [
            int(2.0 * math.pi * 500000.0 ** (column / half_width) + 0.5)
            for column in range(half_width)
        ],
        jnp.int32,
    )


def rope_tables(token_pos):
    half_width = HD // 2
    periods = rope_periods(half_width)
    turn_counts = jnp.remainder(token_pos[:, None], periods[None, :])
    angles = 2.0 * math.pi * turn_counts.astype(jnp.float32) / periods.astype(jnp.float32)
    cosine = jnp.cos(angles)
    sine_part = jnp.sin(angles)
    return (
        jnp.concatenate([cosine, cosine], axis=1),
        jnp.concatenate([-sine_part, sine_part], axis=1),
    )


def turn(head, cosine, sine_part):
    return head * cosine + pltpu.roll(head, HD // 2, 1) * sine_part


def cut_weight_kernel(where, weight_ref, *refs):
    out_ref, sem = refs[-2:]
    rows, columns = out_ref.shape
    y, core = where[2], where[3]
    copy = pltpu.make_async_copy(
        weight_ref.at[
            pl.ds(pl.multiple_of(y * rows, rows), rows),
            pl.ds(pl.multiple_of(core * columns, columns), columns),
        ],
        out_ref,
        sem,
    )
    copy.start()
    copy.wait()


def cut_weight(where, weight, *after):
    rows, columns = weight.shape[0] // 2, weight.shape[1] // 2
    return pl.pallas_call(
        cut_weight_kernel,
        out_shape=jax.ShapeDtypeStruct((rows, columns), jnp.bfloat16),
        in_specs=[SMEM, ANY] + [ANY] * len(after),
        out_specs=VMEM,
        scratch_shapes=[pltpu.SemaphoreType.DMA(())],
        compiler_params=params(2 * rows * columns),
        cost_estimate=cost(0, 4 * rows * columns),
    )(where, weight, *after)


def cut_tokens_kernel(n_line, where, x_ref, *refs):
    out_refs, sems = refs[-5:-1], refs[-1]
    z, x, y = where[0], where[1], where[2]
    width = out_refs[0].shape[2]
    copies = []
    for i in (1, 2, 3, 0):
        for j in range(n_line):
            shard = lax.rem(z - j + n_line, n_line) * 2 + (1 - x if i & 1 else x)
            half = 1 - y if i & 2 else y
            start = pl.multiple_of((shard * 2 + half) * width, width)
            copy = pltpu.make_async_copy(
                x_ref.at[:, pl.ds(start, width)], out_refs[i].at[j], sems.at[i, j]
            )
            copy.start()
            copies.append(copy)
    for copy in copies:
        copy.wait()


def cut_tokens(where, tokens, n_line, *after):
    rows, columns = tokens.shape
    width = columns // (4 * n_line)
    return pl.pallas_call(
        functools.partial(cut_tokens_kernel, n_line),
        out_shape=(jax.ShapeDtypeStruct((n_line, rows, width), jnp.bfloat16),) * 4,
        in_specs=[SMEM, ANY] + [ANY] * len(after),
        out_specs=(VMEM,) * 4,
        scratch_shapes=[pltpu.SemaphoreType.DMA((4, n_line))],
        compiler_params=params(2 * tokens.size),
        cost_estimate=cost(0, 4 * tokens.size),
    )(where, tokens, *after)


def project_kernel(n_sets, n_parts, with_start, n_after, where, *refs):
    refs = list(refs)
    x_refs, refs = refs[: 2 * n_sets], refs[2 * n_sets :]
    w_refs, refs = refs[:n_parts], refs[n_parts:]
    start_refs, refs = (refs[:n_sets], refs[n_sets:]) if with_start else (None, refs)
    outs = refs[n_after:]
    core = where[3]
    tokens = x_refs[0].shape[1]
    for s in range(n_sets):
        for side in range(2):
            x_ref = x_refs[2 * s + side]
            place = pl.ds(pl.multiple_of((1 - core if side else core) * tokens, tokens), tokens)
            total = start_refs[s][place, :] if with_start else None
            for j in range(n_parts):
                term = jnp.dot(x_ref[j], w_refs[j][...], preferred_element_type=jnp.float32)
                total = term if total is None else total + term
            for out in outs[s::n_sets]:
                out[place, :] = total.astype(out.dtype)


def project(where, sets, first, pieces, starts, out_types, *after):
    n_line, tokens, rows = sets[0][0].shape
    columns = pieces[0].shape[1]
    n_parts, n_sets = len(pieces), len(sets)
    blocks = first // n_parts
    x_spec = pl.BlockSpec((n_parts, tokens, rows), lambda: (blocks, 0, 0))
    x_args = [array for pair in sets for array in pair]
    starts = list(starts or [])
    shapes = tuple(
        jax.ShapeDtypeStruct((2 * tokens, columns), t) for t in out_types for _ in sets
    )
    held = n_sets * 4 * tokens * (n_parts * rows + 4 * columns) + 2 * n_parts * rows * columns
    return pl.pallas_call(
        functools.partial(project_kernel, n_sets, n_parts, bool(starts), len(after)),
        out_shape=shapes,
        in_specs=[SMEM]
        + [x_spec] * len(x_args)
        + [VMEM] * (n_parts + len(starts))
        + [ANY] * len(after),
        out_specs=(VMEM,) * len(shapes),
        compiler_params=params(held),
        cost_estimate=cost(4 * n_sets * tokens * n_parts * rows * columns, held),
    )(where, *x_args, *pieces, *starts, *after)


def add_up(refs, span=slice(None)):
    total = refs[0][:, span].astype(jnp.float32)
    for ref in refs[1:]:
        total = total + ref[:, span].astype(jnp.float32)
    return total


def finish_keys_kernel(own_ref, x_ref, y_ref, xy_ref, cosine_ref, sine_ref, out_ref):
    for h in range(out_ref.shape[1] // HD):
        span = slice(h * HD, (h + 1) * HD)
        key = add_up((own_ref, x_ref, y_ref, xy_ref), span)
        out_ref[:, span] = turn(key, cosine_ref[...], sine_ref[...]).astype(jnp.bfloat16)


def finish_values_kernel(own_ref, x_ref, y_ref, xy_ref, out_ref):
    out_ref[...] = add_up((own_ref, x_ref, y_ref, xy_ref)).astype(jnp.bfloat16)


def turn_queries_kernel(q_ref, cosine_ref, sine_ref, after_ref, out_ref):
    for h in range(out_ref.shape[0]):
        query = q_ref[:, h * HD : (h + 1) * HD].astype(jnp.float32)
        out_ref[h] = turn(query, cosine_ref[...], sine_ref[...]).astype(jnp.bfloat16)


def weigh_kernel(n_chips, group, where, q_ref, bias_ref, *refs):
    key_refs, weight_ref, total_ref = refs[: 2 * n_chips], refs[-2], refs[-1]
    core = where[3]
    heads_here = key_refs[0].shape[1] // HD
    bias = bias_ref[...]
    scale = HD ** (-0.5) * LOG2E
    lane = lax.broadcasted_iota(jnp.int32, total_ref.shape, 1)
    totals = jnp.zeros(total_ref.shape, jnp.float32)
    for side in range(2):
        first_head = (1 - core if side else core) * heads_here
        for i in range(heads_here):
            span = slice(i * HD, (i + 1) * HD)
            keys = jnp.concatenate(
                [ref[:, span] for ref in key_refs[side * n_chips : (side + 1) * n_chips]], axis=0
            )
            for g in range(group):
                slot = (side * heads_here + i) * group + g
                query = q_ref[(first_head + i) * group + g]
                scores = lax.dot_general(
                    query, keys, (((1,), (1,)), ((), ())), preferred_element_type=jnp.float32
                )
                scores = scores + bias
                top = jnp.max(scores, axis=1, keepdims=True)
                probabilities = jnp.exp2((scores - top) * scale)
                row_total = jnp.sum(probabilities, axis=1, keepdims=True)
                totals = jnp.where(lane == slot, row_total, totals)
                weight_ref[slot] = probabilities.astype(jnp.bfloat16)
    total_ref[...] = totals


def mix_kernel(n_chips, group, where, weight_ref, total_ref, *refs):
    value_refs, out_ref = refs[: 2 * n_chips], refs[-1]
    core = where[3]
    heads_here = value_refs[0].shape[1] // HD
    tokens, span_rows = weight_ref.shape[1:]
    inverse = 1.0 / total_ref[...]
    for side in range(2):
        first_head = (1 - core if side else core) * heads_here
        for i in range(heads_here):
            span = slice(i * HD, (i + 1) * HD)
            values = jnp.concatenate(
                [ref[:, span] for ref in value_refs[side * n_chips : (side + 1) * n_chips]],
                axis=0,
            )
            slot = (side * heads_here + i) * group
            mixed = jnp.dot(
                weight_ref[slot : slot + group].reshape(group * tokens, span_rows),
                values,
                preferred_element_type=jnp.float32,
            )
            for g in range(group):
                head = (first_head + i) * group + g
                out_ref[:, pl.ds(pl.multiple_of(head * HD, HD), HD)] = (
                    mixed[g * tokens : (g + 1) * tokens] * inverse[:, slot + g : slot + g + 1]
                ).astype(jnp.bfloat16)


def on_device(n_ctx, n_dp, x_tokens, queries, key_weight, value_weight, positions, block_lists):
    n_line, n_chips = n_dp // 2, n_ctx // 2
    tokens_local, query_local = x_tokens[0], queries[0]
    tok_rows, query_width = query_local.shape
    shard_rows, key_width = key_weight.shape
    half_rows, half_columns = shard_rows // 2, key_width // 2
    group = query_width // key_width
    ctx, dp = lax.axis_index("ctx"), lax.axis_index("dp")
    chip, core = ctx // 2, ctx % 2
    y = chip % 2
    where = jnp.stack([dp // 2, dp % 2, y, core]).astype(jnp.int32)

    def over_core(array):
        return lax.ppermute(array, "ctx", [(i, i ^ 1) for i in range(n_ctx)])

    def over_y(array):
        return lax.ppermute(array, "ctx", [(i, i ^ 2) for i in range(n_ctx)])

    def over_x(array):
        return lax.ppermute(array, "dp", [(i, i ^ 1) for i in range(n_dp)])

    def over_z(array, step):
        return lax.ppermute(array, "dp", [(i, (i + 2 * step) % n_dp) for i in range(n_dp)])

    def over_xy(array):
        pairs = [
            (i * n_dp + d, (i ^ 2) * n_dp + (d ^ 1)) for i in range(n_ctx) for d in range(n_dp)
        ]
        return lax.ppermute(array, ("ctx", "dp"), pairs)

    def from_chip(array, step):
        return lax.ppermute(array, "ctx", [(i, (i + 2 * step) % n_ctx) for i in range(n_ctx)])

    up = n_line // 2

    def gather_pieces(own):
        came = [None] * n_line
        came[0] = own
        for j in range(1, up + 1):
            came[j] = over_z(came[j - 1], 1)
            k = n_line - j
            if k > up:
                came[k] = over_z(came[(k + 1) % n_line], -1)
        return came

    key_own = cut_weight(where, key_weight)
    key_pieces = gather_pieces(key_own)
    cuts = cut_tokens(where, tokens_local, n_line, key_own)
    held = [cuts[0], over_x(cuts[1]), over_y(cuts[2]), over_xy(cuts[3])]
    value_own = cut_weight(where, value_weight, key_pieces[1], cuts[0])
    value_pieces = gather_pieces(value_own)
    sets = [(array, over_core(array)) for array in held]

    token_pos = positions[0]
    pos_pair = jnp.stack([token_pos, over_core(positions)[0]])
    pos_chip = jnp.where(core == 0, pos_pair, pos_pair[::-1]).reshape(-1)
    cosine, sine_part = rope_tables(pos_chip)
    own_rows = core * tok_rows
    query_cosine = lax.dynamic_slice_in_dim(cosine, own_rows, tok_rows, 0)
    query_sine = lax.dynamic_slice_in_dim(sine_part, own_rows, tok_rows, 0)
    n_heads = query_width // HD
    query_rot = pl.pallas_call(
        turn_queries_kernel,
        out_shape=jax.ShapeDtypeStruct((n_heads, tok_rows, HD), jnp.bfloat16),
        in_specs=[VMEM] * 3 + [ANY],
        out_specs=VMEM,
        compiler_params=params(4 * query_local.size),
        cost_estimate=cost(3 * query_local.size, 4 * query_local.size),
    )(query_local, query_cosine, query_sine, cuts[0])

    chip_rows = 2 * tok_rows
    source_chip = jnp.remainder(chip - jnp.arange(n_chips, dtype=jnp.int32), n_chips)
    key_index = (
        source_chip[:, None] * chip_rows + jnp.arange(chip_rows, dtype=jnp.int32)[None, :]
    ).reshape(-1)
    query_index = ctx * tok_rows + jnp.arange(tok_rows, dtype=jnp.int32)
    member = jnp.any(
        block_lists[0][:, :, None] == (key_index // BLOCK)[None, None, :], axis=1
    )
    allowed = jnp.repeat(member, BLOCK, axis=0) & (key_index[None, :] <= query_index[:, None])
    bias = jnp.where(allowed, 0.0, neg_large).astype(jnp.float32)

    f32, bf16 = jnp.float32, jnp.bfloat16
    key_parts = project(
        where, sets, 0, key_pieces, None, (f32,), query_rot, bias, cosine, sine_part
    )
    key_here = pl.pallas_call(
        finish_keys_kernel,
        out_shape=jax.ShapeDtypeStruct(key_parts[0].shape, bf16),
        in_specs=[VMEM] * 6,
        out_specs=VMEM,
        compiler_params=params(26 * key_parts[0].size),
        cost_estimate=cost(6 * key_parts[0].size, 26 * key_parts[0].size),
    )(
        key_parts[0], over_x(key_parts[1]), over_y(key_parts[2]), over_xy(key_parts[3]),
        cosine, sine_part,
    )
    keys = [key_here] + [from_chip(key_here, j) for j in range(1, n_chips)]
    keys += [over_core(array) for array in keys]

    value_parts = project(where, sets, 0, value_pieces, None, (bf16,), key_parts[0])
    value_here = pl.pallas_call(
        finish_values_kernel,
        out_shape=jax.ShapeDtypeStruct(value_parts[0].shape, bf16),
        in_specs=[VMEM] * 4,
        out_specs=VMEM,
        compiler_params=params(10 * value_parts[0].size),
        cost_estimate=cost(3 * value_parts[0].size, 10 * value_parts[0].size),
    )(value_parts[0], over_x(value_parts[1]), over_y(value_parts[2]), over_xy(value_parts[3]))
    values = [value_here] + [from_chip(value_here, j) for j in range(1, n_chips)]
    values += [over_core(array) for array in values]

    span_rows = n_chips * chip_rows
    weights, totals = pl.pallas_call(
        functools.partial(weigh_kernel, n_chips, group),
        out_shape=(
            jax.ShapeDtypeStruct((n_heads, tok_rows, span_rows), bf16),
            jax.ShapeDtypeStruct((tok_rows, HD), f32),
        ),
        in_specs=[SMEM] + [VMEM] * (2 + len(keys)),
        out_specs=(VMEM, VMEM),
        compiler_params=params(
            tok_rows * (4 * query_width + 2 * n_heads * span_rows + 8 * span_rows)
        ),
        cost_estimate=cost(
            2 * tok_rows * query_width * span_rows,
            2 * tok_rows * (query_width + n_heads * span_rows),
            tok_rows * n_heads * span_rows,
        ),
    )(where, query_rot, bias, *keys)
    mixed = pl.pallas_call(
        functools.partial(mix_kernel, n_chips, group),
        out_shape=jax.ShapeDtypeStruct((tok_rows, query_width), bf16),
        in_specs=[SMEM] + [VMEM] * (2 + len(values)),
        out_specs=VMEM,
        compiler_params=params(
            tok_rows * (4 * query_width + 2 * n_heads * span_rows) + 4 * span_rows * key_width
        ),
        cost_estimate=cost(
            2 * tok_rows * query_width * span_rows,
            2 * tok_rows * (query_width + n_heads * span_rows),
        ),
    )(where, weights, totals, *values)
    return mixed[None]


def solution(mesh):
    return jax.shard_map(
        functools.partial(on_device, mesh.shape["ctx"], mesh.shape["dp"]),
        mesh=mesh,
        in_specs=(
            P("dp", "ctx", None),
            P("dp", "ctx", None),
            P("dp", None),
            P("dp", None),
            P("dp", "ctx"),
            P("dp", "ctx", None),
        ),
        out_specs=P("dp", "ctx", None),
        check_vma=False,
    )
```

time: 210 us -> 91 us (0.43)
  Pallas kernels: 111 us -> 14.1 us
  waiting for transfers between devices: 56.8 us -> 42.2 us
  starting transfers between devices: 30.6 us -> 24.4 us
  other arithmetic: 7.02 us -> 4.46 us
    pallas_call x5 -> x8, Pallas kernels: 106 us -> 13.5 us  [the longest x2 4.03 us: project(): pl.pallas_call(functools.partial(project_kernel, n_sets, n_parts, bool(st...]
    ppermute x3, waiting for transfers between devices: 24.2 us -> 8.1 us  [over_x(): return lax.ppermute(array, 'dp', [(i, i ^ 1) for i in range(n_dp)])]
    ppermute x6 -> x3, waiting for transfers between devices: 5.67 us -> 16 us  [over_y(): return lax.ppermute(array, 'ctx', [(i, i ^ 2) for i in range(n_ctx)])]
    ppermute x6, waiting for transfers between devices: 24.1 us -> 14.5 us  [over_z(): lax.ppermute(array, 'dp', [(i, (i + 2 * step) % n_dp) for i in range(n_dp)])]
    ppermute x6 -> x3, starting transfers between devices: 8.33 us -> 2.6 us  [over_y(): return lax.ppermute(array, 'ctx', [(i, i ^ 2) for i in range(n_ctx)])]
    pallas_call x1, Pallas kernels: 2.7 us -> 0.49 us  [on_device(): pl.pallas_call(turn_queries_kernel, out_shape=jax.ShapeDtypeStruct((n_hea...]
    unnamed x31 -> x13, local copies, waits for them, and re-layouts: 3.61 us -> 5.27 us
  transfers between devices with their start and end apart: 23 -> 26, of which waited for: 10 -> 11; matrix products, arithmetic and copies ran while one was open for 3% -> 5% of each run, Pallas kernels for 17% -> 12%
where the time goes in v2:
time: 91 us; the launch traced here: 90.7 us
  waiting for transfers between devices  42.2 us (46%)
  starting transfers between devices  24.4 us (27%)
  Pallas kernels  14.1 us (15%)
  local copies, waits for them, and re-layouts  5.3 us (6%)
  other arithmetic  4.46 us (5%)
    ppermute x3, waiting for transfers between devices, over_y(): return lax.ppermute(array, 'ctx', [(i, i ^ 2) for i in range(n_ctx)])  16 us
    ppermute x6, waiting for transfers between devices, over_z(): lax.ppermute(array, 'dp', [(i, (i + 2 * step) % n_dp) for i in range(n_dp)])  14.5 us
    ppermute x6, starting transfers between devices, over_z(): lax.ppermute(array, 'dp', [(i, (i + 2 * step) % n_dp) for i in range(n_dp)])  9.66 us
    ppermute x3, waiting for transfers between devices, over_x(): return lax.ppermute(array, 'dp', [(i, i ^ 1) for i in range(n_dp)])  8.1 us
    unnamed x13, local copies, waits for them, and re-layouts  5.27 us
    ppermute x3, starting transfers between devices, over_x(): return lax.ppermute(array, 'dp', [(i, i ^ 1) for i in range(n_dp)])  4.72 us
    pallas_call x2, Pallas kernels, project(): pl.pallas_call(functools.partial(project_kernel, n_sets, n_parts, bool(st...  4.03 us
    ppermute x2, waiting for transfers between devices, from_chip(): lax.ppermute(array, 'ctx', [(i, (i + 2 * step) % n_ctx) for i in range(n_...  3.48 us
  transfers between devices with their start and end apart: 26, of which 11 were waited for; matrix products, arithmetic and copies ran while one was open for 5% of the time, Pallas kernels for 12%

profile of v2, /device:TPU:0, one launch (start us, length us, event | category | flops | bytes accessed | tf_op | source)
XLA Modules:
  0.0 90.7 jit_solution(15488752391465792644)
XLA Ops:
  0.0 0.5 collective-permute-start
  0.5 0.1 pad_add_fusion.1.where
  0.5 1.2 %copy-done.2 = bf16[1024,512]{1,0:T(8,128)(2,1)S(1)} copy-done((bf16[1024,512]{1,0:T(8,128)(2,1)S(1)}, bf16[1024,512]{1,0:T(8,128)(2,1)}, u32[]{:S(2)}) %copy-start.2) | copy-done | bytes 1048600
  1.8 0.6 shard_map.73.refs_0_.refs_8_
  2.3 2.7 %collective-permute-start.8 = (bf16[512,256]{1,0:T(8,128)(2,1)S(1)}, bf16[512,256]{1,0:T(8,128)(2,1)S(1)}, u32[]{:S(2)}, u32[]{:S(2)}) collective-permute-start(bf16[512,256]{1,0:T(8,128)(2,1)S(1)} %shard_map.73.refs_0_.refs_8_), channel_id=1, source_target_pairs={{0,2},{1,3},{2,4},{3,5},{4,6},{5,7},{6,0},{7,1},{8,10},{9,11},{10,... | collective-permute-start | bytes 786440 | tf_op jit(solution)/shard_map/ppermute | solution.py:268
  5.0 1.6 %copy-done = bf16[1,128,8192]{2,1,0:T(8,128)(2,1)S(1)} copy-done((bf16[1,128,8192]{2,1,0:T(8,128)(2,1)S(1)}, bf16[1,128,8192]{2,1,0:T(8,128)(2,1)}, u32[]{:S(2)}) %copy-start) | copy-done | bytes 2097176
  6.6 2.2 %shard_map.74 = (bf16[4,128,512]{2,1,0:T(8,128)(2,1)S(1)}, bf16[4,128,512]{2,1,0:T(8,128)(2,1)}, bf16[4,128,512]{2,1,0:T(8,128)(2,1)}, bf16[4,128,512]{2,1,0:T(8,128)(2,1)}) custom-call(s32[4]{0:T(128)S(1)} %pad_add_fusion.1.where, bf16[128,8192]{1,0:T(8,128)(2,1)S(1)} %bitcast.17, bf16[512,256]{1,0:T(8,128)(2,1)S(1)} %shard_map.73.refs_0_.refs_8_), custom_call_target="tpu_custom_call" | custom-call | bytes 4194304 | tf_op jit(solution)/shard_map/pallas_call | solution.py:109
  8.9 1.6 %collective-permute-start.2 = (bf16[4,128,512]{2,1,0:T(8,128)(2,1)}, bf16[4,128,512]{2,1,0:T(8,128)(2,1)S(1)}, u32[]{:S(2)}, u32[]{:S(2)}) collective-permute-start(bf16[4,128,512]{2,1,0:T(8,128)(2,1)} %get-tuple-element.20), channel_id=1, source_target_pairs={{0,1},{1,0},{2,3},{3,2},{4,5},{5,4},{6,7},{7,6},{8,9},{9,8},{10,11... | collective-permute-start | bytes 1572872 | tf_op jit(solution)/shard_map/ppermute | solution.py:265
  10.4 1.5 %collective-permute-start.4 = (bf16[4,128,512]{2,1,0:T(8,128)(2,1)}, bf16[4,128,512]{2,1,0:T(8,128)(2,1)S(1)}, u32[]{:S(2)}, u32[]{:S(2)}) collective-permute-start(bf16[4,128,512]{2,1,0:T(8,128)(2,1)} %get-tuple-element.21), channel_id=1, source_target_pairs={{0,16},{8,24},{16,0},{24,8},{1,17},{9,25},{17,1},{25,9},{2,18},{10... | collective-permute-start | bytes 1572872 | tf_op jit(solution)/shard_map/ppermute | solution.py:262
  11.9 0.5 collective-permute-start.6
  12.4 0.1 add_bitcast_fusion
  12.5 0.0 collective-permute-done
  12.5 0.1 collective-permute-start.1
  12.6 0.8 compare_reduce_fusion
  13.4 0.1 fusion.refs_13_.bias_ref
  13.5 0.5 collective-permute-done.8.refs_9_.refs_0_
  14.0 1.7 %collective-permute-start.10 = (bf16[512,256]{1,0:T(8,128)(2,1)S(1)}, bf16[512,256]{1,0:T(8,128)(2,1)}, u32[]{:S(2)}, u32[]{:S(2)}) collective-permute-start(bf16[512,256]{1,0:T(8,128)(2,1)S(1)} %shard_map.73.refs_0_.refs_8_), channel_id=1, source_target_pairs={{0,6},{1,7},{2,0},{3,1},{4,2},{5,3},{6,4},{7,5},{8,14},{9,15},{10,... | collective-permute-start | bytes 786440 | tf_op jit(solution)/shard_map/ppermute | solution.py:268
  15.7 0.7 pad_add_fusion
  16.4 7.5 %collective-permute-done.2.refs_2_ = bf16[4,128,512]{2,1,0:T(8,128)(2,1)S(1)} collective-permute-done((bf16[4,128,512]{2,1,0:T(8,128)(2,1)}, bf16[4,128,512]{2,1,0:T(8,128)(2,1)S(1)}, u32[]{:S(2)}, u32[]{:S(2)}) %collective-permute-start.2) | collective-permute-done | bytes 524320 | tf_op jit(solution)/shard_map/ppermute | solution.py:265
  23.9 0.0 collective-permute-start.3
  23.9 11.7 %collective-permute-done.4.refs_4_ = bf16[4,128,512]{2,1,0:T(8,128)(2,1)S(1)} collective-permute-done((bf16[4,128,512]{2,1,0:T(8,128)(2,1)}, bf16[4,128,512]{2,1,0:T(8,128)(2,1)S(1)}, u32[]{:S(2)}, u32[]{:S(2)}) %collective-permute-start.4) | collective-permute-done | bytes 524320 | tf_op jit(solution)/shard_map/ppermute | solution.py:262
  35.6 0.0 collective-permute-done.6.refs_6_
  35.6 0.5 collective-permute-start.7
  36.1 0.7 select_bitcast_fusion
  36.8 1.2 %copy-done.1 = bf16[1024,512]{1,0:T(8,128)(2,1)S(1)} copy-done((bf16[1024,512]{1,0:T(8,128)(2,1)S(1)}, bf16[1024,512]{1,0:T(8,128)(2,1)}, u32[]{:S(2)}) %copy-start.1) | copy-done | bytes 1048600
  38.0 0.6 shard_map.79.refs_8_
  38.6 1.6 %collective-permute-start.17 = (bf16[512,256]{1,0:T(8,128)(2,1)S(1)}, bf16[512,256]{1,0:T(8,128)(2,1)S(1)}, u32[]{:S(2)}, u32[]{:S(2)}) collective-permute-start(bf16[512,256]{1,0:T(8,128)(2,1)S(1)} %shard_map.79.refs_8_), channel_id=1, source_target_pairs={{0,2},{1,3},{2,4},{3,5},{4,6},{5,7},{6,0},{7,1},{8,10},{9,11},{10,... | collective-permute-start | bytes 786440 | tf_op jit(solution)/shard_map/ppermute | solution.py:268
  40.2 1.6 %collective-permute-start.9 = (bf16[512,256]{1,0:T(8,128)(2,1)S(1)}, bf16[512,256]{1,0:T(8,128)(2,1)S(1)}, u32[]{:S(2)}, u32[]{:S(2)}) collective-permute-start(bf16[512,256]{1,0:T(8,128)(2,1)S(1)} %collective-permute-done.8.refs_9_.refs_0_), channel_id=1, source_target_pairs={{0,2},{1,3},{2,4},{3,5},{4,6},{5,7},{6,0},{7,1},{8,10},{9,11},{10,... | collective-permute-start | bytes 786440 | tf_op jit(solution)/shard_map/ppermute | solution.py:268
  41.8 1.8 %fusion.4 = (f32[256,64]{1,0:T(8,128)S(1)}, f32[256,64]{1,0:T(8,128)S(1)}, f32[256,64]{1,0:T(8,128)S(1)}) fusion(f32[64]{0:T(128)S(1)} %copy-done.4, s32[64]{0:T(128)S(1)} %copy-done.5, s32[256]{0:T(256)S(1)} %select_bitcast_fusion), kind=kLoop, calls=%fused_computation.9 | loop fusion | flops 163840 | bytes 198144 | tf_op jit(solution)/shard_map/sin | solution.py:47
  43.6 0.1 fusion.7
  43.7 0.0 copy-start.3
  43.8 1.2 %copy-done.3 = bf16[1,128,4096]{2,1,0:T(8,128)(2,1)S(1)} copy-done((bf16[1,128,4096]{2,1,0:T(8,128)(2,1)S(1)}, bf16[1,128,4096]{2,1,0:T(8,128)(2,1)}, u32[]{:S(2)}) %copy-start.3) | copy-done | bytes 1048600
  45.0 0.5 shard_map.75.refs_12_.q_ref
  45.5 0.1 pad_maximum_fusion
  45.6 8.7 %collective-permute-done.9.refs_10_ = bf16[512,256]{1,0:T(8,128)(2,1)S(1)} collective-permute-done((bf16[512,256]{1,0:T(8,128)(2,1)S(1)}, bf16[512,256]{1,0:T(8,128)(2,1)S(1)}, u32[]{:S(2)}, u32[]{:S(2)}) %collective-permute-start.9) | collective-permute-done | bytes 262176 | tf_op jit(solution)/shard_map/ppermute | solution.py:268
  54.3 0.5 collective-permute-start.19
  54.8 1.5 %collective-permute-start.18 = (bf16[512,256]{1,0:T(8,128)(2,1)S(1)}, bf16[512,256]{1,0:T(8,128)(2,1)S(1)}, u32[]{:S(2)}, u32[]{:S(2)}) collective-permute-start(bf16[512,256]{1,0:T(8,128)(2,1)S(1)} %collective-permute-done.17.refs_9_), channel_id=1, source_target_pairs={{0,2},{1,3},{2,4},{3,5},{4,6},{5,7},{6,0},{7,1},{8,10},{9,11},{10,... | collective-permute-start | bytes 786440 | tf_op jit(solution)/shard_map/ppermute | solution.py:268
  56.3 0.0 collective-permute-done.5.refs_5_
  56.3 0.0 collective-permute-done.7.refs_7_
  56.3 2.2 %shard_map.76 = (f32[256,256]{1,0:T(8,128)S(1)}, f32[256,256]{1,0:T(8,128)S(1)}, f32[256,256]{1,0:T(8,128)S(1)}, f32[256,256]{1,0:T(8,128)S(1)}) custom-call(s32[4]{0:T(128)S(1)} %pad_add_fusion.1.where, bf16[4,128,512]{2,1,0:T(8,128)(2,1)S(1)} %get-tuple-element.19.after_ref.refs_0_.refs_1_, bf16[4,128,512]{2,1,0:T(8,128)(2,1)S(1)} %collective-permute-done.1.refs_1_, ...), custom_call_target="tpu_custom_call" | custom-call | flops 1073741824 | bytes 7340032 | tf_op jit(solution)/shard_map/pallas_call | solution.py:152
  58.5 1.3 %collective-permute-start.11 = (f32[256,256]{1,0:T(8,128)S(1)}, f32[256,256]{1,0:T(8,128)S(1)}, u32[]{:S(2)}, u32[]{:S(2)}) collective-permute-start(f32[256,256]{1,0:T(8,128)S(1)} %get-tuple-element.24), channel_id=1, source_target_pairs={{0,1},{1,0},{2,3},{3,2},{4,5},{5,4},{6,7},{7,6},{8,9},{9,8},{10,11... | collective-permute-start | bytes 786440 | tf_op jit(solution)/shard_map/ppermute | solution.py:265
  59.8 0.8 collective-permute-start.12
  60.7 1.4 %collective-permute-start.13 = (f32[256,256]{1,0:T(8,128)S(1)}, f32[256,256]{1,0:T(8,128)S(1)}, u32[]{:S(2)}, u32[]{:S(2)}) collective-permute-start(f32[256,256]{1,0:T(8,128)S(1)} %get-tuple-element.26), channel_id=1, source_target_pairs={{0,17},{1,16},{2,19},{3,18},{4,21},{5,20},{6,23},{7,22},{8,25},{9,... | collective-permute-start | bytes 786440 | tf_op jit(solution)/shard_map/ppermute | solution.py:274
  62.1 1.2 %collective-permute-done.19.refs_11_ = bf16[512,256]{1,0:T(8,128)(2,1)S(1)} collective-permute-done((bf16[512,256]{1,0:T(8,128)(2,1)S(1)}, bf16[512,256]{1,0:T(8,128)(2,1)S(1)}, u32[]{:S(2)}, u32[]{:S(2)}) %collective-permute-start.19) | collective-permute-done | bytes 262176 | tf_op jit(solution)/shard_map/ppermute | solution.py:268
  63.3 4.2 %collective-permute-done.18.refs_10_ = bf16[512,256]{1,0:T(8,128)(2,1)S(1)} collective-permute-done((bf16[512,256]{1,0:T(8,128)(2,1)S(1)}, bf16[512,256]{1,0:T(8,128)(2,1)S(1)}, u32[]{:S(2)}, u32[]{:S(2)}) %collective-permute-start.18) | collective-permute-done | bytes 262176 | tf_op jit(solution)/shard_map/ppermute | solution.py:268
  67.5 1.8 %shard_map.80 = (bf16[256,256]{1,0:T(8,128)(2,1)S(1)}, bf16[256,256]{1,0:T(8,128)(2,1)S(1)}, bf16[256,256]{1,0:T(8,128)(2,1)S(1)}, bf16[256,256]{1,0:T(8,128)(2,1)S(1)}) custom-call(s32[4]{0:T(128)S(1)} %pad_add_fusion.1.where, bf16[4,128,512]{2,1,0:T(8,128)(2,1)S(1)} %get-tuple-element.19.after_ref.refs_0_.refs_1_, ...), custom_call_target="tpu_custom_call" | custom-call | flops 1073741824 | bytes 7340032 | tf_op jit(solution)/shard_map/pallas_call | solution.py:152
  69.3 1.9 %collective-permute-start.20 = (bf16[256,256]{1,0:T(8,128)(2,1)S(1)}, bf16[256,256]{1,0:T(8,128)(2,1)S(1)}, u32[]{:S(2)}, u32[]{:S(2)}) collective-permute-start(bf16[256,256]{1,0:T(8,128)(2,1)S(1)} %get-tuple-element.30), channel_id=1, source_target_pairs={{0,1},{1,0},{2,3},{3,2},{4,5},{5,4},{6,7},{7,6},{8,9},{9,8},{10,11... | collective-permute-start | bytes 393224 | tf_op jit(solution)/shard_map/ppermute | solution.py:265
  71.1 0.3 collective-permute-start.21
  71.4 0.0 collective-permute-done.11.x_ref
  71.4 1.4 %collective-permute-start.22 = (bf16[256,256]{1,0:T(8,128)(2,1)S(1)}, bf16[256,256]{1,0:T(8,128)(2,1)S(1)}, u32[]{:S(2)}, u32[]{:S(2)}) collective-permute-start(bf16[256,256]{1,0:T(8,128)(2,1)S(1)} %get-tuple-element.32), channel_id=1, source_target_pairs={{0,17},{1,16},{2,19},{3,18},{4,21},{5,20},{6,23},{7,22},{8,25},{9,... | collective-permute-start | bytes 393224 | tf_op jit(solution)/shard_map/ppermute | solution.py:274
  72.8 0.0 collective-permute-done.12.y_ref
  72.8 0.1 collective-permute-done.13.xy_ref
  72.9 0.2 shard_map.77.refs_0_
  73.0 1.5 %collective-permute-start.14 = (bf16[256,256]{1,0:T(8,128)(2,1)S(1)}, bf16[256,256]{1,0:T(8,128)(2,1)S(1)}, u32[]{:S(2)}, u32[]{:S(2)}) collective-permute-start(bf16[256,256]{1,0:T(8,128)(2,1)S(1)} %shard_map.77.refs_0_), channel_id=1, source_target_pairs={{0,16},{8,24},{16,0},{24,8},{1,17},{9,25},{17,1},{25,9},{2,18},{10... | collective-permute-start | bytes 393224 | tf_op jit(solution)/shard_map/ppermute | solution.py:277
  74.6 0.6 collective-permute-done.20.x_ref
  75.2 4.3 %collective-permute-done.21.y_ref = bf16[256,256]{1,0:T(8,128)(2,1)S(1)} collective-permute-done((bf16[256,256]{1,0:T(8,128)(2,1)S(1)}, bf16[256,256]{1,0:T(8,128)(2,1)S(1)}, u32[]{:S(2)}, u32[]{:S(2)}) %collective-permute-start.21) | collective-permute-done | bytes 131104 | tf_op jit(solution)/shard_map/ppermute | solution.py:262
  79.5 0.1 shard_map.81.refs_0_
  79.6 1.0 %collective-permute-start.23 = (bf16[256,256]{1,0:T(8,128)(2,1)S(1)}, bf16[256,256]{1,0:T(8,128)(2,1)S(1)}, u32[]{:S(2)}, u32[]{:S(2)}) collective-permute-start(bf16[256,256]{1,0:T(8,128)(2,1)S(1)} %shard_map.81.refs_0_), channel_id=1, source_target_pairs={{0,16},{8,24},{16,0},{24,8},{1,17},{9,25},{17,1},{25,9},{2,18},{10... | collective-permute-start | bytes 393224 | tf_op jit(solution)/shard_map/ppermute | solution.py:277
  80.6 0.0 collective-permute-start.15
  80.6 1.7 %collective-permute-done.14.refs_1_ = bf16[256,256]{1,0:T(8,128)(2,1)S(1)} collective-permute-done((bf16[256,256]{1,0:T(8,128)(2,1)S(1)}, bf16[256,256]{1,0:T(8,128)(2,1)S(1)}, u32[]{:S(2)}, u32[]{:S(2)}) %collective-permute-start.14) | collective-permute-done | bytes 131104 | tf_op jit(solution)/shard_map/ppermute | solution.py:277
  82.3 0.5 collective-permute-start.24
  82.8 1.8 %collective-permute-done.23.refs_1_ = bf16[256,256]{1,0:T(8,128)(2,1)S(1)} collective-permute-done((bf16[256,256]{1,0:T(8,128)(2,1)S(1)}, bf16[256,256]{1,0:T(8,128)(2,1)S(1)}, u32[]{:S(2)}, u32[]{:S(2)}) %collective-permute-start.23) | collective-permute-done | bytes 131104 | tf_op jit(solution)/shard_map/ppermute | solution.py:277
  84.6 3.1 %shard_map.78 = (bf16[32,128,512]{2,1,0:T(8,128)(2,1)S(1)}, f32[128,128]{1,0:T(8,128)S(1)}) custom-call(s32[4]{0:T(128)S(1)} %pad_add_fusion.1.where, bf16[32,128,128]{2,1,0:T(8,128)(2,1)S(1)} %shard_map.75.refs_12_.q_ref, f32[128,512]{1,0:T(8,128)S(1)} %fusion.refs_13_.bias_ref, bf16[256,256]{1,0:T(8,128)(2,1)S(1)} %shard_map.77.refs_0_, ...), custom_call_target="tpu_custom_call" | custom-call | flops 536870912 | bytes 5242880 | tf_op jit(solution)/shard_map/pallas_call | solution.py:359
  87.8 2.9 %shard_map.82 = bf16[128,4096]{1,0:T(8,128)(2,1)} custom-call(s32[4]{0:T(128)S(1)} %pad_add_fusion.1.where, bf16[32,128,512]{2,1,0:T(8,128)(2,1)S(1)} %get-tuple-element.27.weight_ref, f32[128,128]{1,0:T(8,128)S(1)} %get-tuple-element.28.total_ref, bf16[256,256]{1,0:T(8,128)(2,1)S(1)} %shard_map.81.refs_0_, ...), custom_call_target="tpu_custom_call" | custom-call | flops 536870912 | bytes 5242880 | tf_op jit(solution)/shard_map/pallas_call | solution.py:376
  (24 shorter events, 0.1 us)
Async XLA Ops:
  0.0 41.8 %copy-start.4 = (f32[64]{0:T(128)S(1)}, f32[64]{0:T(128)}, u32[]{:S(2)}) copy-start(f32[64]{0:T(128)} %constant.100) | copy-start | bytes 772
  0.0 41.8 %copy-start.5 = (s32[64]{0:T(128)S(1)}, s32[64]{0:T(128)}, u32[]{:S(2)}) copy-start(s32[64]{0:T(128)} %constant.96) | copy-start | bytes 772
  0.0 12.5 %collective-permute-start = (s32[1,128]{1,0:T(1,128)}, s32[1,128]{1,0:T(1,128)S(1)}, u32[]{:S(2)}, u32[]{:S(2)}) collective-permute-start(s32[1,128]{1,0:T(1,128)} %param.11), channel_id=1, source_target_pairs={{0,8},{8,0},{16,24},{24,16},{1,9},{9,1},{17,25},{25,17},{2,10},{10... | collective-permute-start | bytes 1544 | tf_op jit(solution)/shard_map/ppermute | solution.py:259
  0.5 1.2 %copy-start.2 = (bf16[1024,512]{1,0:T(8,128)(2,1)S(1)}, bf16[1024,512]{1,0:T(8,128)(2,1)}, u32[]{:S(2)}) copy-start(bf16[1024,512]{1,0:T(8,128)(2,1)} %weight_ref.2) | copy-start | bytes 3145732
  2.3 11.6 %collective-permute-start.8 = (bf16[512,256]{1,0:T(8,128)(2,1)S(1)}, bf16[512,256]{1,0:T(8,128)(2,1)S(1)}, u32[]{:S(2)}, u32[]{:S(2)}) collective-permute-start(bf16[512,256]{1,0:T(8,128)(2,1)S(1)} %shard_map.73.refs_0_.refs_8_), channel_id=1, source_target_pairs={{0,2},{1,3},{2,4},{3,5},{4,6},{5,7},{6,0},{7,1},{8,10},{9,11},{10,... | collective-permute-start | bytes 786440 | tf_op jit(solution)/shard_map/ppermute | solution.py:268
  5.0 1.6 %copy-start = (bf16[1,128,8192]{2,1,0:T(8,128)(2,1)S(1)}, bf16[1,128,8192]{2,1,0:T(8,128)(2,1)}, u32[]{:S(2)}) copy-start(bf16[1,128,8192]{2,1,0:T(8,128)(2,1)} %param.7) | copy-start | bytes 6291460
  8.9 15.0 %collective-permute-start.2 = (bf16[4,128,512]{2,1,0:T(8,128)(2,1)}, bf16[4,128,512]{2,1,0:T(8,128)(2,1)S(1)}, u32[]{:S(2)}, u32[]{:S(2)}) collective-permute-start(bf16[4,128,512]{2,1,0:T(8,128)(2,1)} %get-tuple-element.20), channel_id=1, source_target_pairs={{0,1},{1,0},{2,3},{3,2},{4,5},{5,4},{6,7},{7,6},{8,9},{9,8},{10,11... | collective-permute-start | bytes 1572872 | tf_op jit(solution)/shard_map/ppermute | solution.py:265
  10.4 25.2 %collective-permute-start.4 = (bf16[4,128,512]{2,1,0:T(8,128)(2,1)}, bf16[4,128,512]{2,1,0:T(8,128)(2,1)S(1)}, u32[]{:S(2)}, u32[]{:S(2)}) collective-permute-start(bf16[4,128,512]{2,1,0:T(8,128)(2,1)} %get-tuple-element.21), channel_id=1, source_target_pairs={{0,16},{8,24},{16,0},{24,8},{1,17},{9,25},{17,1},{25,9},{2,18},{10... | collective-permute-start | bytes 1572872 | tf_op jit(solution)/shard_map/ppermute | solution.py:262
  11.9 23.6 %collective-permute-start.6 = (bf16[4,128,512]{2,1,0:T(8,128)(2,1)}, bf16[4,128,512]{2,1,0:T(8,128)(2,1)S(1)}, u32[]{:S(2)}, u32[]{:S(2)}) collective-permute-start(bf16[4,128,512]{2,1,0:T(8,128)(2,1)} %get-tuple-element.22), channel_id=1, source_target_pairs={{0,17},{1,16},{2,19},{3,18},{4,21},{5,20},{6,23},{7,22},{8,25},{9,... | collective-permute-start | bytes 1572872 | tf_op jit(solution)/shard_map/ppermute | solution.py:274
  12.5 27.7 %collective-permute-start.1 = (bf16[4,128,512]{2,1,0:T(8,128)(2,1)S(1)}, bf16[4,128,512]{2,1,0:T(8,128)(2,1)S(1)}, u32[]{:S(2)}, u32[]{:S(2)}) collective-permute-start(bf16[4,128,512]{2,1,0:T(8,128)(2,1)S(1)} %get-tuple-element.19.after_ref.refs_0_.refs_1_), channel_id=1, source_target_pairs={{0,8},{8,0},{16,24},{24,16},{1,9},{9,1},{17,25},{25,17},{2,10},{10... | collective-permute-start | bytes 1572872 | tf_op jit(solution)/shard_map/ppermute | solution.py:259
  14.0 24.6 %collective-permute-start.10 = (bf16[512,256]{1,0:T(8,128)(2,1)S(1)}, bf16[512,256]{1,0:T(8,128)(2,1)}, u32[]{:S(2)}, u32[]{:S(2)}) collective-permute-start(bf16[512,256]{1,0:T(8,128)(2,1)S(1)} %shard_map.73.refs_0_.refs_8_), channel_id=1, source_target_pairs={{0,6},{1,7},{2,0},{3,1},{4,2},{5,3},{6,4},{7,5},{8,14},{9,15},{10,... | collective-permute-start | bytes 786440 | tf_op jit(solution)/shard_map/ppermute | solution.py:268
  23.9 32.4 %collective-permute-start.3 = (bf16[4,128,512]{2,1,0:T(8,128)(2,1)S(1)}, bf16[4,128,512]{2,1,0:T(8,128)(2,1)S(1)}, u32[]{:S(2)}, u32[]{:S(2)}) collective-permute-start(bf16[4,128,512]{2,1,0:T(8,128)(2,1)S(1)} %collective-permute-done.2.refs_2_), channel_id=1, source_target_pairs={{0,8},{8,0},{16,24},{24,16},{1,9},{9,1},{17,25},{25,17},{2,10},{10... | collective-permute-start | bytes 1572872 | tf_op jit(solution)/shard_map/ppermute | solution.py:259
  35.6 20.7 %collective-permute-start.5 = (bf16[4,128,512]{2,1,0:T(8,128)(2,1)S(1)}, bf16[4,128,512]{2,1,0:T(8,128)(2,1)S(1)}, u32[]{:S(2)}, u32[]{:S(2)}) collective-permute-start(bf16[4,128,512]{2,1,0:T(8,128)(2,1)S(1)} %collective-permute-done.4.refs_4_), channel_id=1, source_target_pairs={{0,8},{8,0},{16,24},{24,16},{1,9},{9,1},{17,25},{25,17},{2,10},{10... | collective-permute-start | bytes 1572872 | tf_op jit(solution)/shard_map/ppermute | solution.py:259
  35.6 20.7 %collective-permute-start.7 = (bf16[4,128,512]{2,1,0:T(8,128)(2,1)S(1)}, bf16[4,128,512]{2,1,0:T(8,128)(2,1)S(1)}, u32[]{:S(2)}, u32[]{:S(2)}) collective-permute-start(bf16[4,128,512]{2,1,0:T(8,128)(2,1)S(1)} %collective-permute-done.6.refs_6_), channel_id=1, source_target_pairs={{0,8},{8,0},{16,24},{24,16},{1,9},{9,1},{17,25},{25,17},{2,10},{10... | collective-permute-start | bytes 1572872 | tf_op jit(solution)/shard_map/ppermute | solution.py:259
  36.8 1.2 %copy-start.1 = (bf16[1024,512]{1,0:T(8,128)(2,1)S(1)}, bf16[1024,512]{1,0:T(8,128)(2,1)}, u32[]{:S(2)}) copy-start(bf16[1024,512]{1,0:T(8,128)(2,1)} %weight_ref.3) | copy-start | bytes 3145732
  38.6 16.2 %collective-permute-start.17 = (bf16[512,256]{1,0:T(8,128)(2,1)S(1)}, bf16[512,256]{1,0:T(8,128)(2,1)S(1)}, u32[]{:S(2)}, u32[]{:S(2)}) collective-permute-start(bf16[512,256]{1,0:T(8,128)(2,1)S(1)} %shard_map.79.refs_8_), channel_id=1, source_target_pairs={{0,2},{1,3},{2,4},{3,5},{4,6},{5,7},{6,0},{7,1},{8,10},{9,11},{10,... | collective-permute-start | bytes 786440 | tf_op jit(solution)/shard_map/ppermute | solution.py:268
  40.2 14.1 %collective-permute-start.9 = (bf16[512,256]{1,0:T(8,128)(2,1)S(1)}, bf16[512,256]{1,0:T(8,128)(2,1)S(1)}, u32[]{:S(2)}, u32[]{:S(2)}) collective-permute-start(bf16[512,256]{1,0:T(8,128)(2,1)S(1)} %collective-permute-done.8.refs_9_.refs_0_), channel_id=1, source_target_pairs={{0,2},{1,3},{2,4},{3,5},{4,6},{5,7},{6,0},{7,1},{8,10},{9,11},{10,... | collective-permute-start | bytes 786440 | tf_op jit(solution)/shard_map/ppermute | solution.py:268
  43.7 1.2 %copy-start.3 = (bf16[1,128,4096]{2,1,0:T(8,128)(2,1)S(1)}, bf16[1,128,4096]{2,1,0:T(8,128)(2,1)}, u32[]{:S(2)}) copy-start(bf16[1,128,4096]{2,1,0:T(8,128)(2,1)} %param.8) | copy-start | bytes 3145732
  54.3 9.0 %collective-permute-start.19 = (bf16[512,256]{1,0:T(8,128)(2,1)S(1)}, bf16[512,256]{1,0:T(8,128)(2,1)S(1)}, u32[]{:S(2)}, u32[]{:S(2)}) collective-permute-start(bf16[512,256]{1,0:T(8,128)(2,1)S(1)} %shard_map.79.refs_8_), channel_id=1, source_target_pairs={{0,6},{1,7},{2,0},{3,1},{4,2},{5,3},{6,4},{7,5},{8,14},{9,15},{10,... | collective-permute-start | bytes 786440 | tf_op jit(solution)/shard_map/ppermute | solution.py:268
  54.8 12.7 %collective-permute-start.18 = (bf16[512,256]{1,0:T(8,128)(2,1)S(1)}, bf16[512,256]{1,0:T(8,128)(2,1)S(1)}, u32[]{:S(2)}, u32[]{:S(2)}) collective-permute-start(bf16[512,256]{1,0:T(8,128)(2,1)S(1)} %collective-permute-done.17.refs_9_), channel_id=1, source_target_pairs={{0,2},{1,3},{2,4},{3,5},{4,6},{5,7},{6,0},{7,1},{8,10},{9,11},{10,... | collective-permute-start | bytes 786440 | tf_op jit(solution)/shard_map/ppermute | solution.py:268
  58.5 12.8 %collective-permute-start.11 = (f32[256,256]{1,0:T(8,128)S(1)}, f32[256,256]{1,0:T(8,128)S(1)}, u32[]{:S(2)}, u32[]{:S(2)}) collective-permute-start(f32[256,256]{1,0:T(8,128)S(1)} %get-tuple-element.24), channel_id=1, source_target_pairs={{0,1},{1,0},{2,3},{3,2},{4,5},{5,4},{6,7},{7,6},{8,9},{9,8},{10,11... | collective-permute-start | bytes 786440 | tf_op jit(solution)/shard_map/ppermute | solution.py:265
  59.8 13.0 %collective-permute-start.12 = (f32[256,256]{1,0:T(8,128)S(1)}, f32[256,256]{1,0:T(8,128)S(1)}, u32[]{:S(2)}, u32[]{:S(2)}) collective-permute-start(f32[256,256]{1,0:T(8,128)S(1)} %get-tuple-element.25), channel_id=1, source_target_pairs={{0,16},{8,24},{16,0},{24,8},{1,17},{9,25},{17,1},{25,9},{2,18},{10... | collective-permute-start | bytes 786440 | tf_op jit(solution)/shard_map/ppermute | solution.py:262
  60.7 12.2 %collective-permute-start.13 = (f32[256,256]{1,0:T(8,128)S(1)}, f32[256,256]{1,0:T(8,128)S(1)}, u32[]{:S(2)}, u32[]{:S(2)}) collective-permute-start(f32[256,256]{1,0:T(8,128)S(1)} %get-tuple-element.26), channel_id=1, source_target_pairs={{0,17},{1,16},{2,19},{3,18},{4,21},{5,20},{6,23},{7,22},{8,25},{9,... | collective-permute-start | bytes 786440 | tf_op jit(solution)/shard_map/ppermute | solution.py:274
  69.3 5.9 %collective-permute-start.20 = (bf16[256,256]{1,0:T(8,128)(2,1)S(1)}, bf16[256,256]{1,0:T(8,128)(2,1)S(1)}, u32[]{:S(2)}, u32[]{:S(2)}) collective-permute-start(bf16[256,256]{1,0:T(8,128)(2,1)S(1)} %get-tuple-element.30), channel_id=1, source_target_pairs={{0,1},{1,0},{2,3},{3,2},{4,5},{5,4},{6,7},{7,6},{8,9},{9,8},{10,11... | collective-permute-start | bytes 393224 | tf_op jit(solution)/shard_map/ppermute | solution.py:265
  71.1 8.4 %collective-permute-start.21 = (bf16[256,256]{1,0:T(8,128)(2,1)S(1)}, bf16[256,256]{1,0:T(8,128)(2,1)S(1)}, u32[]{:S(2)}, u32[]{:S(2)}) collective-permute-start(bf16[256,256]{1,0:T(8,128)(2,1)S(1)} %get-tuple-element.31), channel_id=1, source_target_pairs={{0,16},{8,24},{16,0},{24,8},{1,17},{9,25},{17,1},{25,9},{2,18},{10... | collective-permute-start | bytes 393224 | tf_op jit(solution)/shard_map/ppermute | solution.py:262
  71.4 8.1 %collective-permute-start.22 = (bf16[256,256]{1,0:T(8,128)(2,1)S(1)}, bf16[256,256]{1,0:T(8,128)(2,1)S(1)}, u32[]{:S(2)}, u32[]{:S(2)}) collective-permute-start(bf16[256,256]{1,0:T(8,128)(2,1)S(1)} %get-tuple-element.32), channel_id=1, source_target_pairs={{0,17},{1,16},{2,19},{3,18},{4,21},{5,20},{6,23},{7,22},{8,25},{9,... | collective-permute-start | bytes 393224 | tf_op jit(solution)/shard_map/ppermute | solution.py:274
  73.0 9.3 %collective-permute-start.14 = (bf16[256,256]{1,0:T(8,128)(2,1)S(1)}, bf16[256,256]{1,0:T(8,128)(2,1)S(1)}, u32[]{:S(2)}, u32[]{:S(2)}) collective-permute-start(bf16[256,256]{1,0:T(8,128)(2,1)S(1)} %shard_map.77.refs_0_), channel_id=1, source_target_pairs={{0,16},{8,24},{16,0},{24,8},{1,17},{9,25},{17,1},{25,9},{2,18},{10... | collective-permute-start | bytes 393224 | tf_op jit(solution)/shard_map/ppermute | solution.py:277
  79.6 5.0 %collective-permute-start.23 = (bf16[256,256]{1,0:T(8,128)(2,1)S(1)}, bf16[256,256]{1,0:T(8,128)(2,1)S(1)}, u32[]{:S(2)}, u32[]{:S(2)}) collective-permute-start(bf16[256,256]{1,0:T(8,128)(2,1)S(1)} %shard_map.81.refs_0_), channel_id=1, source_target_pairs={{0,16},{8,24},{16,0},{24,8},{1,17},{9,25},{17,1},{25,9},{2,18},{10... | collective-permute-start | bytes 393224 | tf_op jit(solution)/shard_map/ppermute | solution.py:277
  80.6 4.0 %collective-permute-start.15 = (bf16[256,256]{1,0:T(8,128)(2,1)S(1)}, bf16[256,256]{1,0:T(8,128)(2,1)S(1)}, u32[]{:S(2)}, u32[]{:S(2)}) collective-permute-start(bf16[256,256]{1,0:T(8,128)(2,1)S(1)} %shard_map.77.refs_0_), channel_id=1, source_target_pairs={{0,8},{8,0},{16,24},{24,16},{1,9},{9,1},{17,25},{25,17},{2,10},{10... | collective-permute-start | bytes 393224 | tf_op jit(solution)/shard_map/ppermute | solution.py:259
  82.3 2.3 %collective-permute-start.16 = (bf16[256,256]{1,0:T(8,128)(2,1)S(1)}, bf16[256,256]{1,0:T(8,128)(2,1)S(1)}, u32[]{:S(2)}, u32[]{:S(2)}) collective-permute-start(bf16[256,256]{1,0:T(8,128)(2,1)S(1)} %collective-permute-done.14.refs_1_), channel_id=1, source_target_pairs={{0,8},{8,0},{16,24},{24,16},{1,9},{9,1},{17,25},{25,17},{2,10},{10... | collective-permute-start | bytes 393224 | tf_op jit(solution)/shard_map/ppermute | solution.py:259
  82.3 5.4 %collective-permute-start.24 = (bf16[256,256]{1,0:T(8,128)(2,1)S(1)}, bf16[256,256]{1,0:T(8,128)(2,1)S(1)}, u32[]{:S(2)}, u32[]{:S(2)}) collective-permute-start(bf16[256,256]{1,0:T(8,128)(2,1)S(1)} %shard_map.81.refs_0_), channel_id=1, source_target_pairs={{0,8},{8,0},{16,24},{24,16},{1,9},{9,1},{17,25},{25,17},{2,10},{10... | collective-permute-start | bytes 393224 | tf_op jit(solution)/shard_map/ppermute | solution.py:259
  84.6 3.2 %collective-permute-start.25 = (bf16[256,256]{1,0:T(8,128)(2,1)S(1)}, bf16[256,256]{1,0:T(8,128)(2,1)S(1)}, u32[]{:S(2)}, u32[]{:S(2)}) collective-permute-start(bf16[256,256]{1,0:T(8,128)(2,1)S(1)} %collective-permute-done.23.refs_1_), channel_id=1, source_target_pairs={{0,8},{8,0},{16,24},{24,16},{1,9},{9,1},{17,25},{25,17},{2,10},{10... | collective-permute-start | bytes 393224 | tf_op jit(solution)/shard_map/ppermute | solution.py:259

commit v3 on v2

v3 whole, which is shorter than its diff:
```python
import functools
import math

import jax
import jax.numpy as jnp
from jax import lax
from jax.experimental import pallas as pl
from jax.experimental.pallas import tpu as pltpu
from jax.sharding import PartitionSpec as P

HD = 128
BLOCK = 64
LOG2E = 1.4426950408889634

neg_large = -1e30
HEADROOM = 2 * 1024 * 1024
ANY = pl.BlockSpec(memory_space=pl.ANY)
VMEM = pl.BlockSpec(memory_space=pltpu.VMEM)
SMEM = pl.BlockSpec(memory_space=pltpu.SMEM)


def params(held):
    return pltpu.CompilerParams(vmem_limit_bytes=held + HEADROOM)


def cost(flops, bytes_accessed, transcendentals=0):
    return pl.CostEstimate(
        flops=flops, bytes_accessed=bytes_accessed, transcendentals=transcendentals
    )


def rope_periods(half_width):
    return jnp.array(
        [
            int(2.0 * math.pi * 500000.0 ** (column / half_width) + 0.5)
            for column in range(half_width)
        ],
        jnp.int32,
    )


def rope_tables(token_pos):
    half_width = HD // 2
    periods = rope_periods(half_width)
    turn_counts = jnp.remainder(token_pos[:, None], periods[None, :])
    angles = 2.0 * math.pi * turn_counts.astype(jnp.float32) / periods.astype(jnp.float32)
    cosine = jnp.cos(angles)
    sine_part = jnp.sin(angles)
    return (
        jnp.concatenate([cosine, cosine], axis=1),
        jnp.concatenate([-sine_part, sine_part], axis=1),
    )


def turn(head, cosine, sine_part):
    return head * cosine + pltpu.roll(head, HD // 2, 1) * sine_part


def part_of(weight_ref, where, shape):
    rows, columns = shape
    y, core = where[2], where[3]
    return weight_ref[
        pl.ds(pl.multiple_of(y * rows, rows), rows),
        pl.ds(pl.multiple_of(core * columns, columns), columns),
    ]


def cut_weight_kernel(where, weight_ref, *refs):
    refs[-1][...] = part_of(weight_ref, where, refs[-1].shape)


def cut_weight(where, weight, *after):
    part = (weight.shape[0] // 2, weight.shape[1] // 2)
    return pl.pallas_call(
        cut_weight_kernel,
        out_shape=jax.ShapeDtypeStruct(part, jnp.bfloat16),
        in_specs=[SMEM, VMEM] + [ANY] * len(after),
        out_specs=VMEM,
        compiler_params=params(4 * weight.size),
        cost_estimate=cost(0, 3 * weight.size),
    )(where, weight, *after)


def cut_tokens_kernel(n_line, where, x_ref, *refs):
    out_refs = refs[-4:]
    z, x, y = where[0], where[1], where[2]
    width = out_refs[0].shape[2]
    for i in (1, 2, 3, 0):
        for j in range(n_line):
            shard = lax.rem(z - j + n_line, n_line) * 2 + (1 - x if i & 1 else x)
            half = 1 - y if i & 2 else y
            start = pl.multiple_of((shard * 2 + half) * width, width)
            out_refs[i][j] = x_ref[:, pl.ds(start, width)]


def cut_tokens(where, tokens, n_line, *after):
    rows, columns = tokens.shape
    shape = (n_line, rows, columns // (4 * n_line))
    return pl.pallas_call(
        functools.partial(cut_tokens_kernel, n_line),
        out_shape=(jax.ShapeDtypeStruct(shape, jnp.bfloat16),) * 4,
        in_specs=[SMEM, VMEM] + [ANY] * len(after),
        out_specs=(VMEM,) * 4,
        compiler_params=params(4 * tokens.size),
        cost_estimate=cost(0, 4 * tokens.size),
    )(where, tokens, *after)


def project_kernel(n_sets, lines, with_start, n_after, where, *refs):
    n_parts = len(lines)
    refs = list(refs)
    x_refs, refs = refs[: 2 * n_sets], refs[2 * n_sets :]
    w_refs, refs = refs[:n_parts], refs[n_parts:]
    start_refs, refs = (refs[:n_sets], refs[n_sets:]) if with_start else (None, refs)
    outs = refs[n_after:]
    core = where[3]
    tokens = x_refs[0].shape[1]
    for s in range(n_sets):
        for side in range(2):
            x_ref = x_refs[2 * s + side]
            place = pl.ds(pl.multiple_of((1 - core if side else core) * tokens, tokens), tokens)
            total = start_refs[s][place, :] if with_start else None
            for j, w_ref in zip(lines, w_refs):
                term = jnp.dot(x_ref[j], w_ref[...], preferred_element_type=jnp.float32)
                total = term if total is None else total + term
            for out in outs[s::n_sets]:
                out[place, :] = total.astype(out.dtype)


def project(where, sets, lines, pieces, starts, out_types, *after):
    n_line, tokens, rows = sets[0][0].shape
    columns = pieces[0].shape[1]
    n_parts, n_sets = len(lines), len(sets)
    pieces = [pieces[j] for j in lines]
    x_args = [array for pair in sets for array in pair]
    starts = list(starts or [])
    shapes = tuple(
        jax.ShapeDtypeStruct((2 * tokens, columns), t) for t in out_types for _ in sets
    )
    held = n_sets * 4 * tokens * (n_line * rows + 4 * columns) + 2 * n_parts * rows * columns
    return pl.pallas_call(
        functools.partial(project_kernel, n_sets, lines, bool(starts), len(after)),
        out_shape=shapes,
        in_specs=[SMEM]
        + [VMEM] * len(x_args)
        + [VMEM] * (n_parts + len(starts))
        + [ANY] * len(after),
        out_specs=(VMEM,) * len(shapes),
        compiler_params=params(held),
        cost_estimate=cost(4 * n_sets * tokens * n_parts * rows * columns, held),
    )(where, *x_args, *pieces, *starts, *after)


def add_up(refs, span=slice(None)):
    total = refs[0][:, span].astype(jnp.float32)
    for ref in refs[1:]:
        total = total + ref[:, span].astype(jnp.float32)
    return total


def finish_keys_kernel(own_ref, x_ref, y_ref, xy_ref, cosine_ref, sine_ref, out_ref):
    for h in range(out_ref.shape[1] // HD):
        span = slice(h * HD, (h + 1) * HD)
        key = add_up((own_ref, x_ref, y_ref, xy_ref), span)
        out_ref[:, span] = turn(key, cosine_ref[...], sine_ref[...]).astype(jnp.bfloat16)


def finish_values_kernel(own_ref, x_ref, y_ref, xy_ref, out_ref):
    out_ref[...] = add_up((own_ref, x_ref, y_ref, xy_ref)).astype(jnp.bfloat16)


def turn_queries_kernel(q_ref, cosine_ref, sine_ref, after_ref, out_ref):
    for h in range(out_ref.shape[0]):
        query = q_ref[:, h * HD : (h + 1) * HD].astype(jnp.float32)
        out_ref[h] = turn(query, cosine_ref[...], sine_ref[...]).astype(jnp.bfloat16)


def mask_kernel(chip_rows, n_chips, where, lists_ref, out_ref):
    span_rows, tokens = out_ref.shape
    chip, core = where[4], where[3]
    for j in range(n_chips):
        first_key = lax.rem(chip - j + n_chips, n_chips) * chip_rows
        shape = (chip_rows, tokens)
        key = first_key + lax.broadcasted_iota(jnp.int32, shape, 0)
        column = lax.broadcasted_iota(jnp.int32, shape, 1)
        query = chip * chip_rows + core * tokens + column
        key_block, query_row = key // BLOCK, column // BLOCK
        listed = key < 0
        for row in range(lists_ref.shape[0]):
            for entry in range(lists_ref.shape[1]):
                listed = listed | ((key_block == lists_ref[row, entry]) & (query_row == row))
        out_ref[j * chip_rows : (j + 1) * chip_rows, :] = jnp.where(
            listed & (key <= query), 0.0, neg_large
        ).astype(jnp.bfloat16)


def weigh_kernel(n_chips, group, where, q_ref, bias_ref, *refs):
    key_refs, (weight_ref, total_ref, scores) = refs[: 2 * n_chips], refs[2 * n_chips :]
    core = where[3]
    heads_here = key_refs[0].shape[1] // HD
    tokens = q_ref.shape[1]
    span_rows, lanes = scores.shape
    together = lanes // tokens
    scale = HD ** (-0.5) * LOG2E
    square = (tokens, tokens)
    row, column = (lax.broadcasted_iota(jnp.int32, square, axis) for axis in range(2))
    pick = (row == column).astype(jnp.float32).astype(jnp.bfloat16)
    for side in range(2):
        first_head = (1 - core if side else core) * heads_here
        for i in range(heads_here):
            span = slice(i * HD, (i + 1) * HD)
            keys = jnp.concatenate(
                [ref[:, span] for ref in key_refs[side * n_chips : (side + 1) * n_chips]], axis=0
            )
            keys = jnp.concatenate([keys, bias_ref[...]], axis=1)
            pair = side * heads_here + i
            for g in range(0, group, together):
                query = jnp.concatenate(
                    [
                        jnp.concatenate([q_ref[(first_head + i) * group + g + t], pick], axis=1)
                        for t in range(together)
                    ],
                    axis=0,
                )
                scores[...] = lax.dot_general(
                    keys, query, (((1,), (1,)), ((), ())), preferred_element_type=jnp.float32
                )
                top = scores[:8]
                for r in range(8, span_rows, 8):
                    top = jnp.maximum(top, scores[r : r + 8])
                top = jnp.max(top, axis=0, keepdims=True)
                total = jnp.zeros((16, lanes), jnp.float32)
                columns = slice(g * tokens, g * tokens + lanes)
                for r in range(0, span_rows, 16):
                    probabilities = jnp.exp2((scores[r : r + 16] - top) * scale)
                    total = total + probabilities
                    weight_ref[pair, r : r + 16, columns] = probabilities.astype(jnp.bfloat16)
                total_ref[pair, :, columns] = jnp.sum(total, axis=0, keepdims=True)


def mix_kernel(n_chips, group, where, weight_ref, total_ref, *refs):
    value_refs, out_ref, buf, sems = refs[: 2 * n_chips], refs[-3], refs[-2], refs[-1]
    core = where[3]
    heads_here = value_refs[0].shape[1] // HD
    tokens = out_ref.shape[0]
    width = group * HD
    copies = []
    for side in range(2):
        first_head = (1 - core if side else core) * heads_here
        for i in range(heads_here):
            span = slice(i * HD, (i + 1) * HD)
            values = jnp.concatenate(
                [ref[:, span] for ref in value_refs[side * n_chips : (side + 1) * n_chips]],
                axis=0,
            )
            pair = side * heads_here + i
            mixed = jnp.dot(
                values.T, weight_ref[pair], preferred_element_type=jnp.float32
            ) * (1.0 / total_ref[pair])
            for g in range(group):
                buf[pair, :, g * HD : (g + 1) * HD] = mixed[
                    :, g * tokens : (g + 1) * tokens
                ].T.astype(jnp.bfloat16)
            start = pl.multiple_of((first_head + i) * width, width)
            copies.append(
                pltpu.make_async_copy(
                    buf.at[pair], out_ref.at[:, pl.ds(start, width)], sems.at[pair]
                )
            )
            copies[-1].start()
    for copy in copies:
        copy.wait()


def on_device(n_ctx, n_dp, x_tokens, queries, key_weight, value_weight, positions, block_lists):
    n_line, n_chips = n_dp // 2, n_ctx // 2
    tokens_local, query_local = x_tokens[0], queries[0]
    tok_rows, query_width = query_local.shape
    shard_rows, key_width = key_weight.shape
    half_rows, half_columns = shard_rows // 2, key_width // 2
    group = query_width // key_width
    ctx, dp = lax.axis_index("ctx"), lax.axis_index("dp")
    chip, core = ctx // 2, ctx % 2
    y = chip % 2
    where = jnp.stack([dp // 2, dp % 2, y, core, chip]).astype(jnp.int32)

    def over_core(array):
        return lax.ppermute(array, "ctx", [(i, i ^ 1) for i in range(n_ctx)])

    def over_y(array):
        return lax.ppermute(array, "ctx", [(i, i ^ 2) for i in range(n_ctx)])

    def over_x(array):
        return lax.ppermute(array, "dp", [(i, i ^ 1) for i in range(n_dp)])

    def over_z(array, step):
        return lax.ppermute(array, "dp", [(i, (i + 2 * step) % n_dp) for i in range(n_dp)])

    def over_xy(array):
        pairs = [
            (i * n_dp + d, (i ^ 2) * n_dp + (d ^ 1)) for i in range(n_ctx) for d in range(n_dp)
        ]
        return lax.ppermute(array, ("ctx", "dp"), pairs)

    def from_chip(array, step):
        return lax.ppermute(array, "ctx", [(i, (i + 2 * step) % n_ctx) for i in range(n_ctx)])

    up = n_line // 2

    def gather_pieces(own, late, after):
        came = [None] * n_line
        came[0] = own
        for j in range(1, up + 1):
            k = n_line - j
            if k > up:
                came[k] = over_z(came[(k + 1) % n_line], -1)
            before = came[j - 1]
            if j == up and (late or after):
                before = lax.optimization_barrier(
                    (before, *([came[up + 1]] if late else []), *after)
                )[0]
            came[j] = over_z(before, 1)
        return came

    cuts = cut_tokens(where, tokens_local, n_line)
    key_own = cut_weight(where, key_weight, cuts[0])
    token_pos = positions[0]
    pos_pair = jnp.stack([token_pos, over_core(positions)[0]])
    pos_chip = jnp.where(core == 0, pos_pair, pos_pair[::-1]).reshape(-1)
    cosine, sine_part = rope_tables(pos_chip)
    own_rows = core * tok_rows
    query_cosine = lax.dynamic_slice_in_dim(cosine, own_rows, tok_rows, 0)
    query_sine = lax.dynamic_slice_in_dim(sine_part, own_rows, tok_rows, 0)
    n_heads = query_width // HD
    query_rot = pl.pallas_call(
        turn_queries_kernel,
        out_shape=jax.ShapeDtypeStruct((n_heads, tok_rows, HD), jnp.bfloat16),
        in_specs=[VMEM] * 3 + [ANY],
        out_specs=VMEM,
        compiler_params=params(4 * query_local.size),
        cost_estimate=cost(3 * query_local.size, 4 * query_local.size),
    )(query_local, query_cosine, query_sine, key_own)

    chip_rows = 2 * tok_rows
    bias = pl.pallas_call(
        functools.partial(mask_kernel, chip_rows, n_chips),
        out_shape=jax.ShapeDtypeStruct((n_chips * chip_rows, tok_rows), jnp.bfloat16),
        in_specs=[SMEM, SMEM],
        out_specs=VMEM,
        compiler_params=params(16 * chip_rows * tok_rows),
        cost_estimate=cost(20 * n_chips * chip_rows * tok_rows, 0),
    )(where, block_lists[0])

    key_pieces = gather_pieces(key_own, True, [bias, cosine, sine_part])
    held = [cuts[0], over_x(cuts[1]), over_y(cuts[2]), over_xy(cuts[3])]
    value_own = cut_weight(where, value_weight, cuts[0])
    value_pieces = gather_pieces(value_own, False, [])

    held[1:] = lax.optimization_barrier(
        (*held[1:], key_pieces[up], value_pieces[1], query_rot)
    )[:3]
    sets = [(array, over_core(array)) for array in held]

    f32, bf16 = jnp.float32, jnp.bfloat16
    every = list(range(n_line))
    key_parts = project(
        where, sets, every, key_pieces, None, (f32,), key_own
    )
    key_here = pl.pallas_call(
        finish_keys_kernel,
        out_shape=jax.ShapeDtypeStruct(key_parts[0].shape, bf16),
        in_specs=[VMEM] * 6,
        out_specs=VMEM,
        compiler_params=params(26 * key_parts[0].size),
        cost_estimate=cost(6 * key_parts[0].size, 26 * key_parts[0].size),
    )(
        key_parts[0], over_x(key_parts[1]), over_y(key_parts[2]), over_xy(key_parts[3]),
        cosine, sine_part,
    )
    keys = [key_here] + [from_chip(key_here, j) for j in range(1, n_chips)]
    keys += [over_core(array) for array in keys]

    early = [j for j in every if j != up]
    early_values = project(where, sets, early, value_pieces, None, (f32,), key_parts[0])
    value_parts = project(where, sets, [up], value_pieces, early_values, (bf16,))
    value_here = pl.pallas_call(
        finish_values_kernel,
        out_shape=jax.ShapeDtypeStruct(value_parts[0].shape, bf16),
        in_specs=[VMEM] * 4,
        out_specs=VMEM,
        compiler_params=params(10 * value_parts[0].size),
        cost_estimate=cost(3 * value_parts[0].size, 10 * value_parts[0].size),
    )(value_parts[0], over_x(value_parts[1]), over_y(value_parts[2]), over_xy(value_parts[3]))
    values = [value_here] + [from_chip(value_here, j) for j in range(1, n_chips)]
    values += [over_core(array) for array in values]

    span_rows = n_chips * chip_rows
    pairs, lanes = 2 * (keys[0].shape[1] // HD), group * tok_rows
    held = 2 * tok_rows * (query_width + n_heads * span_rows)
    weights, totals = pl.pallas_call(
        functools.partial(weigh_kernel, n_chips, group),
        out_shape=(
            jax.ShapeDtypeStruct((pairs, span_rows, lanes), bf16),
            jax.ShapeDtypeStruct((pairs, 1, lanes), f32),
        ),
        in_specs=[SMEM] + [VMEM] * (2 + len(keys)),
        out_specs=(VMEM, VMEM),
        scratch_shapes=[pltpu.VMEM((span_rows, 2 * tok_rows), f32)],
        compiler_params=params(held + 10 * bias.size + 4 * span_rows * key_width),
        cost_estimate=cost(
            2 * tok_rows * query_width * span_rows, held, tok_rows * n_heads * span_rows
        ),
    )(where, query_rot, bias, *keys)
    mixed = pl.pallas_call(
        functools.partial(mix_kernel, n_chips, group),
        out_shape=jax.ShapeDtypeStruct((tok_rows, query_width), bf16),
        in_specs=[SMEM] + [VMEM] * (2 + len(values)),
        out_specs=ANY,
        scratch_shapes=[
            pltpu.VMEM((pairs, tok_rows, group * HD), bf16),
            pltpu.SemaphoreType.DMA((pairs,)),
        ],
        compiler_params=params(held + 4 * span_rows * key_width),
        cost_estimate=cost(2 * tok_rows * query_width * span_rows, held),
    )(where, weights, totals, *values)
    return mixed[None]


def solution(mesh):
    return jax.shard_map(
        functools.partial(on_device, mesh.shape["ctx"], mesh.shape["dp"]),
        mesh=mesh,
        in_specs=(
            P("dp", "ctx", None),
            P("dp", "ctx", None),
            P("dp", None),
            P("dp", None),
            P("dp", "ctx"),
            P("dp", "ctx", None),
        ),
        out_specs=P("dp", "ctx", None),
        check_vma=False,
    )
```

time: 91 us -> 75.4 us (0.83)
  waiting for transfers between devices: 42.2 us -> 28.2 us
  starting transfers between devices: 24.4 us -> 22.2 us
  Pallas kernels: 14.1 us -> 15.2 us
    ppermute x3, waiting for transfers between devices: 16 us -> 5.44 us  [over_y(): return lax.ppermute(array, 'ctx', [(i, i ^ 2) for i in range(n_ctx)])]
    ppermute x3, waiting for transfers between devices: 8.1 us -> 1.13 us  [over_x(): return lax.ppermute(array, 'dp', [(i, i ^ 1) for i in range(n_dp)])]
    pallas_call x4 -> x6, Pallas kernels: 5.18 us -> 7.59 us  [the longest x3 4.83 us: project(): pl.pallas_call(functools.partial(project_kernel, n_sets, lines, bool(star...]
    ppermute x3, waiting for transfers between devices: 0.07 us -> 1.88 us  [over_xy(): return lax.ppermute(array, ('ctx', 'dp'), pairs)]
    ppermute x2, starting transfers between devices: 2.56 us -> 1.38 us  [from_chip(): lax.ppermute(array, 'ctx', [(i, (i + 2 * step) % n_ctx) for i in range(n_...]
    concatenate x1, other arithmetic: 0.11 us -> 1.04 us  [rope_tables(): jnp.concatenate([-sine_part, sine_part], axis=1)]
    unnamed x13 -> x26, local copies, waits for them, and re-layouts: 5.27 us -> 5.44 us
  transfers between devices with their start and end apart: 26 -> 26, of which waited for: 11 -> 13; matrix products, arithmetic and copies ran while one was open for 5% -> 5% of each run, Pallas kernels for 12% -> 14%
where the time goes in v3:
time: 75.4 us; the launch traced here: 75 us
  waiting for transfers between devices  28.2 us (37%)
  starting transfers between devices  22.2 us (29%)
  Pallas kernels  15.2 us (20%)
  local copies, waits for them, and re-layouts  5.55 us (7%)
  other arithmetic  3.68 us (5%)
    ppermute x6, waiting for transfers between devices, over_z(): lax.ppermute(array, 'dp', [(i, (i + 2 * step) % n_dp) for i in range(n_dp)])  15.1 us
    ppermute x6, starting transfers between devices, over_z(): lax.ppermute(array, 'dp', [(i, (i + 2 * step) % n_dp) for i in range(n_dp)])  9.17 us
    unnamed x26, local copies, waits for them, and re-layouts  5.44 us
    ppermute x3, waiting for transfers between devices, over_y(): return lax.ppermute(array, 'ctx', [(i, i ^ 2) for i in range(n_ctx)])  5.44 us
    pallas_call x3, Pallas kernels, project(): pl.pallas_call(functools.partial(project_kernel, n_sets, lines, bool(star...  4.83 us
    ppermute x3, starting transfers between devices, over_x(): return lax.ppermute(array, 'dp', [(i, i ^ 1) for i in range(n_dp)])  4.24 us
    ppermute x2, waiting for transfers between devices, from_chip(): lax.ppermute(array, 'ctx', [(i, (i + 2 * step) % n_ctx) for i in range(n_...  3.76 us
    ppermute x3, starting transfers between devices, over_xy(): return lax.ppermute(array, ('ctx', 'dp'), pairs)  3.26 us
  transfers between devices with their start and end apart: 26, of which 13 were waited for; matrix products, arithmetic and copies ran while one was open for 5% of the time, Pallas kernels for 14%

profile of v3, /device:TPU:0, one launch (start us, length us, event | category | flops | bytes accessed | tf_op | source)
XLA Modules:
  0.0 75.0 jit_solution(10868829043697027588)
XLA Ops:
  0.0 0.1 stack.26.where
  0.1 1.6 %copy-done = bf16[1,128,8192]{2,1,0:T(8,128)(2,1)S(1)} copy-done((bf16[1,128,8192]{2,1,0:T(8,128)(2,1)S(1)}, bf16[1,128,8192]{2,1,0:T(8,128)(2,1)}, u32[]{:S(2)}) %copy-start) | copy-done | bytes 2097176
  1.7 1.7 %shard_map.73 = (bf16[4,128,512]{2,1,0:T(8,128)(2,1)S(1)}, bf16[4,128,512]{2,1,0:T(8,128)(2,1)}, bf16[4,128,512]{2,1,0:T(8,128)(2,1)}, bf16[4,128,512]{2,1,0:T(8,128)(2,1)S(1)}) custom-call(s32[5]{0:T(128)S(1)} %stack.26.where, bf16[128,8192]{1,0:T(8,128)(2,1)S(1)} %bitcast.11), custom_call_target="tpu_custom_call" | custom-call | bytes 4194304 | tf_op jit(solution)/shard_map/pallas_call | solution.py:99
  3.4 1.4 %copy-done.1 = bf16[1024,512]{1,0:T(8,128)(2,1)S(1)} copy-done((bf16[1024,512]{1,0:T(8,128)(2,1)S(1)}, bf16[1024,512]{1,0:T(8,128)(2,1)}, u32[]{:S(2)}) %copy-start.1) | copy-done | bytes 1048600
  4.8 0.6 shard_map.74.after_ref.refs_8_.refs_12_
  5.4 3.1 %collective-permute-start.5 = (bf16[512,256]{1,0:T(8,128)(2,1)S(1)}, bf16[512,256]{1,0:T(8,128)(2,1)}, u32[]{:S(2)}, u32[]{:S(2)}) collective-permute-start(bf16[512,256]{1,0:T(8,128)(2,1)S(1)} %shard_map.74.after_ref.refs_8_.refs_12_), channel_id=1, source_target_pairs={{0,2},{1,3},{2,4},{3,5},{4,6},{5,7},{6,0},{7,1},{8,10},{9,11},{10,... | collective-permute-start | bytes 786440 | tf_op jit(solution)/shard_map/ppermute | solution.py:297
  8.5 2.1 %collective-permute-start.6 = (bf16[512,256]{1,0:T(8,128)(2,1)S(1)}, bf16[512,256]{1,0:T(8,128)(2,1)}, u32[]{:S(2)}, u32[]{:S(2)}) collective-permute-start(bf16[512,256]{1,0:T(8,128)(2,1)S(1)} %shard_map.74.after_ref.refs_8_.refs_12_), channel_id=1, source_target_pairs={{0,6},{1,7},{2,0},{3,1},{4,2},{5,3},{6,4},{7,5},{8,14},{9,15},{10,... | collective-permute-start | bytes 786440 | tf_op jit(solution)/shard_map/ppermute | solution.py:297
  10.6 0.0 collective-permute-start
  10.6 1.6 %collective-permute-start.2 = (bf16[4,128,512]{2,1,0:T(8,128)(2,1)}, bf16[4,128,512]{2,1,0:T(8,128)(2,1)S(1)}, u32[]{:S(2)}, u32[]{:S(2)}) collective-permute-start(bf16[4,128,512]{2,1,0:T(8,128)(2,1)} %get-tuple-element.28), channel_id=1, source_target_pairs={{0,1},{1,0},{2,3},{3,2},{4,5},{5,4},{6,7},{7,6},{8,9},{9,8},{10,11... | collective-permute-start | bytes 1572872 | tf_op jit(solution)/shard_map/ppermute | solution.py:294
  12.2 1.5 %collective-permute-start.3 = (bf16[4,128,512]{2,1,0:T(8,128)(2,1)}, bf16[4,128,512]{2,1,0:T(8,128)(2,1)S(1)}, u32[]{:S(2)}, u32[]{:S(2)}) collective-permute-start(bf16[4,128,512]{2,1,0:T(8,128)(2,1)} %get-tuple-element.29), channel_id=1, source_target_pairs={{0,16},{8,24},{16,0},{24,8},{1,17},{9,25},{17,1},{25,9},{2,18},{10... | collective-permute-start | bytes 1572872 | tf_op jit(solution)/shard_map/ppermute | solution.py:291
  13.8 0.6 shard_map.77.refs_8_
  14.3 0.7 copy-done.4
  15.0 1.6 %shard_map.76.bias_ref = bf16[512,128]{1,0:T(8,128)(2,1)S(1)} custom-call(s32[5]{0:T(128)S(1)} %stack.26.where, s32[2,6]{1,0:T(2,128)S(1)} %bitcast.13), custom_call_target="tpu_custom_call" | custom-call | flops 1310720 | tf_op jit(solution)/shard_map/pallas_call | solution.py:345
  16.7 0.4 collective-permute-start.4
  17.1 2.5 %fusion.3 = (f32[256,64]{1,0:T(8,128)S(1)}, f32[256,64]{1,0:T(8,128)S(1)}, f32[256,64]{1,0:T(8,128)S(1)}) fusion(f32[64]{0:T(128)} %constant.72, s32[64]{0:T(128)S(1)} %copy-done.12, s32[256]{0:T(256)S(1)} %select_bitcast_fusion), kind=kLoop, calls=%fused_computation.7 | loop fusion | flops 163840 | bytes 198144 | tf_op jit(solution)/shard_map/sin | solution.py:48
  19.7 0.1 pad_maximum_fusion
  19.8 0.5 copy-done.10
  20.3 0.0 collective-permute-start.8
  20.3 1.7 %collective-permute-done.6.refs_11_ = bf16[512,256]{1,0:T(8,128)(2,1)} collective-permute-done((bf16[512,256]{1,0:T(8,128)(2,1)S(1)}, bf16[512,256]{1,0:T(8,128)(2,1)}, u32[]{:S(2)}, u32[]{:S(2)}) %collective-permute-start.6) | collective-permute-done | bytes 262176 | tf_op jit(solution)/shard_map/ppermute | solution.py:297
  22.0 1.9 %collective-permute-start.7 = (bf16[512,256]{1,0:T(8,128)(2,1)}, bf16[512,256]{1,0:T(8,128)(2,1)S(1)}, u32[]{:S(2)}, u32[]{:S(2)}) collective-permute-start(bf16[512,256]{1,0:T(8,128)(2,1)} %collective-permute-done.5.refs_9_), channel_id=1, source_target_pairs={{0,2},{1,3},{2,4},{3,5},{4,6},{5,7},{6,0},{7,1},{8,10},{9,11},{10,... | collective-permute-start | bytes 786440 | tf_op jit(solution)/shard_map/ppermute | solution.py:297
  23.9 1.0 %fusion.6 = (f32[128,128]{1,0:T(8,128)S(1)}, f32[128,128]{1,0:T(8,128)S(1)}) fusion(s32[]{:T(128)S(6)} %select_n.53, f32[256,64]{1,0:T(8,128)} %copy-done.9, f32[256,64]{1,0:T(8,128)} %copy-done.8, f32[256,64]{1,0:T(8,128)} %copy-done.10), kind=kLoop, calls=%fused_computation.16 | loop fusion | flops 32768 | bytes 327684 | tf_op jit(solution)/shard_map/concatenate | solution.py:51
  24.9 0.0 copy-start.3
  25.0 1.2 %copy-done.3 = bf16[1,128,4096]{2,1,0:T(8,128)(2,1)S(1)} copy-done((bf16[1,128,4096]{2,1,0:T(8,128)(2,1)S(1)}, bf16[1,128,4096]{2,1,0:T(8,128)(2,1)}, u32[]{:S(2)}) %copy-start.3) | copy-done | bytes 1048600
  26.2 0.5 shard_map.75.q_ref
  26.7 5.1 %collective-permute-done.8.refs_9_ = bf16[512,256]{1,0:T(8,128)(2,1)S(1)} collective-permute-done((bf16[512,256]{1,0:T(8,128)(2,1)}, bf16[512,256]{1,0:T(8,128)(2,1)S(1)}, u32[]{:S(2)}, u32[]{:S(2)}) %collective-permute-start.8) | collective-permute-done | bytes 262176 | tf_op jit(solution)/shard_map/ppermute | solution.py:297
  31.7 4.1 %collective-permute-done.7.refs_10_ = bf16[512,256]{1,0:T(8,128)(2,1)S(1)} collective-permute-done((bf16[512,256]{1,0:T(8,128)(2,1)}, bf16[512,256]{1,0:T(8,128)(2,1)S(1)}, u32[]{:S(2)}, u32[]{:S(2)}) %collective-permute-start.7) | collective-permute-done | bytes 262176 | tf_op jit(solution)/shard_map/ppermute | solution.py:297
  35.8 0.0 collective-permute-done.2.refs_2_
  35.8 1.9 %collective-permute-done.3.refs_4_ = bf16[4,128,512]{2,1,0:T(8,128)(2,1)S(1)} collective-permute-done((bf16[4,128,512]{2,1,0:T(8,128)(2,1)}, bf16[4,128,512]{2,1,0:T(8,128)(2,1)S(1)}, u32[]{:S(2)}, u32[]{:S(2)}) %collective-permute-start.3) | collective-permute-done | bytes 524320 | tf_op jit(solution)/shard_map/ppermute | solution.py:291
  37.7 0.0 collective-permute-done.4.refs_6_
  37.7 0.0 collective-permute-start.10
  37.7 0.5 collective-permute-start.11
  38.3 0.0 collective-permute-start.9
  38.3 1.8 %collective-permute-start.19 = (bf16[512,256]{1,0:T(8,128)(2,1)S(1)}, bf16[512,256]{1,0:T(8,128)(2,1)S(1)}, u32[]{:S(2)}, u32[]{:S(2)}) collective-permute-start(bf16[512,256]{1,0:T(8,128)(2,1)S(1)} %copy-done.5), channel_id=1, source_target_pairs={{0,6},{1,7},{2,0},{3,1},{4,2},{5,3},{6,4},{7,5},{8,14},{9,15},{10,... | collective-permute-start | bytes 786440 | tf_op jit(solution)/shard_map/ppermute | solution.py:297
  40.1 0.2 collective-permute-start.18
  40.3 0.1 collective-permute-done.11.refs_7_
  40.4 0.7 collective-permute-done.9.refs_3_
  41.2 2.3 %shard_map.78 = (f32[256,256]{1,0:T(8,128)S(1)}, f32[256,256]{1,0:T(8,128)S(1)}, f32[256,256]{1,0:T(8,128)S(1)}, f32[256,256]{1,0:T(8,128)S(1)}) custom-call(s32[5]{0:T(128)S(1)} %stack.26.where, bf16[4,128,512]{2,1,0:T(8,128)(2,1)S(1)} %get-tuple-element.27.refs_0_, bf16[4,128,512]{2,1,0:T(8,128)(2,1)S(1)} %collective-permute-done.1.refs_1_, ...), custom_call_target="tpu_custom_call" | custom-call | flops 1073741824 | bytes 7340032 | tf_op jit(solution)/shard_map/pallas_call | solution.py:141
  43.5 1.3 %collective-permute-start.12 = (f32[256,256]{1,0:T(8,128)S(1)}, f32[256,256]{1,0:T(8,128)S(1)}, u32[]{:S(2)}, u32[]{:S(2)}) collective-permute-start(f32[256,256]{1,0:T(8,128)S(1)} %get-tuple-element.36), channel_id=1, source_target_pairs={{0,1},{1,0},{2,3},{3,2},{4,5},{5,4},{6,7},{7,6},{8,9},{9,8},{10,11... | collective-permute-start | bytes 786440 | tf_op jit(solution)/shard_map/ppermute | solution.py:294
  44.8 0.8 %collective-permute-start.13 = (f32[256,256]{1,0:T(8,128)S(1)}, f32[256,256]{1,0:T(8,128)S(1)}, u32[]{:S(2)}, u32[]{:S(2)}) collective-permute-start(f32[256,256]{1,0:T(8,128)S(1)} %get-tuple-element.37), channel_id=1, source_target_pairs={{0,16},{8,24},{16,0},{24,8},{1,17},{9,25},{17,1},{25,9},{2,18},{10... | collective-permute-start | bytes 786440 | tf_op jit(solution)/shard_map/ppermute | solution.py:291
  45.6 1.4 %collective-permute-start.14 = (f32[256,256]{1,0:T(8,128)S(1)}, f32[256,256]{1,0:T(8,128)S(1)}, u32[]{:S(2)}, u32[]{:S(2)}) collective-permute-start(f32[256,256]{1,0:T(8,128)S(1)} %get-tuple-element.38), channel_id=1, source_target_pairs={{0,17},{1,16},{2,19},{3,18},{4,21},{5,20},{6,23},{7,22},{8,25},{9,... | collective-permute-start | bytes 786440 | tf_op jit(solution)/shard_map/ppermute | solution.py:303
  47.0 0.1 collective-permute-done.19.refs_10_
  47.1 1.5 %shard_map.81 = (f32[256,256]{1,0:T(8,128)S(1)}, f32[256,256]{1,0:T(8,128)S(1)}, f32[256,256]{1,0:T(8,128)S(1)}, f32[256,256]{1,0:T(8,128)S(1)}) custom-call(s32[5]{0:T(128)S(1)} %stack.26.where, bf16[4,128,512]{2,1,0:T(8,128)(2,1)S(1)} %get-tuple-element.27.refs_0_, bf16[4,128,512]{2,1,0:T(8,128)(2,1)S(1)} %collective-permute-done.1.refs_1_, ...), custom_call_target="tpu_custom_call" | custom-call | flops 805306368 | bytes 7077888 | tf_op jit(solution)/shard_map/pallas_call | solution.py:141
  48.7 4.1 %collective-permute-done.18.refs_8_ = bf16[512,256]{1,0:T(8,128)(2,1)S(1)} collective-permute-done((bf16[512,256]{1,0:T(8,128)(2,1)S(1)}, bf16[512,256]{1,0:T(8,128)(2,1)S(1)}, u32[]{:S(2)}, u32[]{:S(2)}) %collective-permute-start.18) | collective-permute-done | bytes 262176 | tf_op jit(solution)/shard_map/ppermute | solution.py:297
  52.8 1.0 %shard_map.82 = (bf16[256,256]{1,0:T(8,128)(2,1)S(1)}, bf16[256,256]{1,0:T(8,128)(2,1)S(1)}, bf16[256,256]{1,0:T(8,128)(2,1)S(1)}, bf16[256,256]{1,0:T(8,128)(2,1)S(1)}) custom-call(s32[5]{0:T(128)S(1)} %stack.26.where, bf16[4,128,512]{2,1,0:T(8,128)(2,1)S(1)} %get-tuple-element.27.refs_0_, bf16[4,128,512]{2,1,0:T(8,128)(2,1)S(1)} %collective-permute-done.1.refs_1_, ...), custom_call_target="tpu_custom_call" | custom-call | flops 268435456 | bytes 6553600 | tf_op jit(solution)/shard_map/pallas_call | solution.py:141
  53.8 1.3 %collective-permute-start.20 = (bf16[256,256]{1,0:T(8,128)(2,1)S(1)}, bf16[256,256]{1,0:T(8,128)(2,1)S(1)}, u32[]{:S(2)}, u32[]{:S(2)}) collective-permute-start(bf16[256,256]{1,0:T(8,128)(2,1)S(1)} %get-tuple-element.46), channel_id=1, source_target_pairs={{0,1},{1,0},{2,3},{3,2},{4,5},{5,4},{6,7},{7,6},{8,9},{9,8},{10,11... | collective-permute-start | bytes 393224 | tf_op jit(solution)/shard_map/ppermute | solution.py:294
  55.1 0.8 %collective-permute-start.21 = (bf16[256,256]{1,0:T(8,128)(2,1)S(1)}, bf16[256,256]{1,0:T(8,128)(2,1)S(1)}, u32[]{:S(2)}, u32[]{:S(2)}) collective-permute-start(bf16[256,256]{1,0:T(8,128)(2,1)S(1)} %get-tuple-element.47), channel_id=1, source_target_pairs={{0,16},{8,24},{16,0},{24,8},{1,17},{9,25},{17,1},{25,9},{2,18},{10... | collective-permute-start | bytes 393224 | tf_op jit(solution)/shard_map/ppermute | solution.py:291
  55.9 0.0 collective-permute-done.12.x_ref
  55.9 1.4 %collective-permute-start.22 = (bf16[256,256]{1,0:T(8,128)(2,1)S(1)}, bf16[256,256]{1,0:T(8,128)(2,1)S(1)}, u32[]{:S(2)}, u32[]{:S(2)}) collective-permute-start(bf16[256,256]{1,0:T(8,128)(2,1)S(1)} %get-tuple-element.48), channel_id=1, source_target_pairs={{0,17},{1,16},{2,19},{3,18},{4,21},{5,20},{6,23},{7,22},{8,25},{9,... | collective-permute-start | bytes 393224 | tf_op jit(solution)/shard_map/ppermute | solution.py:303
  57.4 0.0 collective-permute-done.13.y_ref
  57.4 1.9 %collective-permute-done.14.xy_ref = f32[256,256]{1,0:T(8,128)S(1)} collective-permute-done((f32[256,256]{1,0:T(8,128)S(1)}, f32[256,256]{1,0:T(8,128)S(1)}, u32[]{:S(2)}, u32[]{:S(2)}) %collective-permute-start.14) | collective-permute-done | bytes 262176 | tf_op jit(solution)/shard_map/ppermute | solution.py:303
  59.3 0.1 shard_map.79.refs_0_
  59.4 0.6 collective-permute-start.15
  60.0 1.1 %collective-permute-done.20.x_ref = bf16[256,256]{1,0:T(8,128)(2,1)S(1)} collective-permute-done((bf16[256,256]{1,0:T(8,128)(2,1)S(1)}, bf16[256,256]{1,0:T(8,128)(2,1)S(1)}, u32[]{:S(2)}, u32[]{:S(2)}) %collective-permute-start.20) | collective-permute-done | bytes 131104 | tf_op jit(solution)/shard_map/ppermute | solution.py:294
  61.2 3.5 %collective-permute-done.21.y_ref = bf16[256,256]{1,0:T(8,128)(2,1)S(1)} collective-permute-done((bf16[256,256]{1,0:T(8,128)(2,1)S(1)}, bf16[256,256]{1,0:T(8,128)(2,1)S(1)}, u32[]{:S(2)}, u32[]{:S(2)}) %collective-permute-start.21) | collective-permute-done | bytes 131104 | tf_op jit(solution)/shard_map/ppermute | solution.py:291
  64.7 0.1 shard_map.83.refs_0_
  64.7 0.8 %collective-permute-start.23 = (bf16[256,256]{1,0:T(8,128)(2,1)S(1)}, bf16[256,256]{1,0:T(8,128)(2,1)S(1)}, u32[]{:S(2)}, u32[]{:S(2)}) collective-permute-start(bf16[256,256]{1,0:T(8,128)(2,1)S(1)} %shard_map.83.refs_0_), channel_id=1, source_target_pairs={{0,16},{8,24},{16,0},{24,8},{1,17},{9,25},{17,1},{25,9},{2,18},{10... | collective-permute-start | bytes 393224 | tf_op jit(solution)/shard_map/ppermute | solution.py:306
  65.5 0.0 collective-permute-start.16
  65.5 2.0 %collective-permute-done.15.refs_1_ = bf16[256,256]{1,0:T(8,128)(2,1)S(1)} collective-permute-done((bf16[256,256]{1,0:T(8,128)(2,1)S(1)}, bf16[256,256]{1,0:T(8,128)(2,1)S(1)}, u32[]{:S(2)}, u32[]{:S(2)}) %collective-permute-start.15) | collective-permute-done | bytes 131104 | tf_op jit(solution)/shard_map/ppermute | solution.py:306
  67.5 0.0 collective-permute-start.17
  67.5 0.5 collective-permute-start.24
  68.0 1.8 %collective-permute-done.23.refs_1_ = bf16[256,256]{1,0:T(8,128)(2,1)S(1)} collective-permute-done((bf16[256,256]{1,0:T(8,128)(2,1)S(1)}, bf16[256,256]{1,0:T(8,128)(2,1)S(1)}, u32[]{:S(2)}, u32[]{:S(2)}) %collective-permute-start.23) | collective-permute-done | bytes 131104 | tf_op jit(solution)/shard_map/ppermute | solution.py:306
  69.8 0.0 collective-permute-start.25
  69.8 3.1 %shard_map.80 = (bf16[4,512,1024]{2,1,0:T(8,128)(2,1)S(1)}, f32[4,1,1024]{2,1,0:T(1,128)S(1)}) custom-call(s32[5]{0:T(128)S(1)} %stack.26.where, bf16[32,128,128]{2,1,0:T(8,128)(2,1)S(1)} %shard_map.75.q_ref, bf16[512,128]{1,0:T(8,128)(2,1)S(1)} %shard_map.76.bias_ref, bf16[256,256]{1,0:T(8,128)(2,1)S(1)} %shard_map.79.refs_0_, ...), custom_call_target="tpu_custom_call" | custom-call | flops 536870912 | bytes 5242880 | tf_op jit(solution)/shard_map/pallas_call | solution.py:400
  72.9 2.1 %shard_map.84 = bf16[128,4096]{1,0:T(8,128)(2,1)} custom-call(s32[5]{0:T(128)S(1)} %stack.26.where, bf16[4,512,1024]{2,1,0:T(8,128)(2,1)S(1)} %get-tuple-element.39.weight_ref, f32[4,1,1024]{2,1,0:T(1,128)S(1)} %get-tuple-element.40.total_ref, bf16[256,256]{1,0:T(8,128)(2,1)S(1)} %shard_map.83.refs_0_, bf16[256,256]{1,0:T(8,128)(2,1)S(1)} %collective-permute-done.23.refs_1_, ...), custom_call_target="tpu_custom_call" | custom-call | flops 536870912 | bytes 5242880 | tf_op jit(solution)/shard_map/pallas_call | solution.py:414
  (33 shorter events, 0.1 us)
Async XLA Ops:
  0.0 17.1 %copy-start.12 = (s32[64]{0:T(128)S(1)}, s32[64]{0:T(128)}, u32[]{:S(2)}) copy-start(s32[64]{0:T(128)} %constant.68) | copy-start | bytes 772
  0.0 17.1 %copy-start.11 = (s32[1,128]{1,0:T(1,128)S(1)}, s32[1,128]{1,0:T(1,128)}, u32[]{:S(2)}) copy-start(s32[1,128]{1,0:T(1,128)} %param.11) | copy-start | bytes 1540
  0.0 15.0 %copy-start.6 = (s32[1,2,6]{2,1,0:T(2,128)S(1)}, s32[1,2,6]{2,1,0:T(2,128)}, u32[]{:S(2)}) copy-start(s32[1,2,6]{2,1,0:T(2,128)} %param.12) | copy-start | bytes 148
  0.1 1.6 %copy-start = (bf16[1,128,8192]{2,1,0:T(8,128)(2,1)S(1)}, bf16[1,128,8192]{2,1,0:T(8,128)(2,1)}, u32[]{:S(2)}) copy-start(bf16[1,128,8192]{2,1,0:T(8,128)(2,1)} %param.7) | copy-start | bytes 6291460
  1.7 12.1 %copy-start.2 = (bf16[1024,512]{1,0:T(8,128)(2,1)S(1)}, bf16[1024,512]{1,0:T(8,128)(2,1)}, u32[]{:S(2)}) copy-start(bf16[1024,512]{1,0:T(8,128)(2,1)} %weight_ref.3) | copy-start | bytes 3145732
  3.4 8.9 %copy-start.7 = (bf16[4,128,512]{2,1,0:T(8,128)(2,1)}, bf16[4,128,512]{2,1,0:T(8,128)(2,1)S(1)}, u32[]{:S(2)}) copy-start(bf16[4,128,512]{2,1,0:T(8,128)(2,1)S(1)} %get-tuple-element.30) | copy-start | bytes 1572868
  3.4 1.4 %copy-start.1 = (bf16[1024,512]{1,0:T(8,128)(2,1)S(1)}, bf16[1024,512]{1,0:T(8,128)(2,1)}, u32[]{:S(2)}) copy-start(bf16[1024,512]{1,0:T(8,128)(2,1)} %weight_ref.2) | copy-start | bytes 3145732
  5.4 14.9 %collective-permute-start.5 = (bf16[512,256]{1,0:T(8,128)(2,1)S(1)}, bf16[512,256]{1,0:T(8,128)(2,1)}, u32[]{:S(2)}, u32[]{:S(2)}) collective-permute-start(bf16[512,256]{1,0:T(8,128)(2,1)S(1)} %shard_map.74.after_ref.refs_8_.refs_12_), channel_id=1, source_target_pairs={{0,2},{1,3},{2,4},{3,5},{4,6},{5,7},{6,0},{7,1},{8,10},{9,11},{10,... | collective-permute-start | bytes 786440 | tf_op jit(solution)/shard_map/ppermute | solution.py:297
  8.5 13.5 %collective-permute-start.6 = (bf16[512,256]{1,0:T(8,128)(2,1)S(1)}, bf16[512,256]{1,0:T(8,128)(2,1)}, u32[]{:S(2)}, u32[]{:S(2)}) collective-permute-start(bf16[512,256]{1,0:T(8,128)(2,1)S(1)} %shard_map.74.after_ref.refs_8_.refs_12_), channel_id=1, source_target_pairs={{0,6},{1,7},{2,0},{3,1},{4,2},{5,3},{6,4},{7,5},{8,14},{9,15},{10,... | collective-permute-start | bytes 786440 | tf_op jit(solution)/shard_map/ppermute | solution.py:297
  10.6 6.1 %collective-permute-start = (s32[1,128]{1,0:T(1,128)}, s32[1,128]{1,0:T(1,128)S(1)}, u32[]{:S(2)}, u32[]{:S(2)}) collective-permute-start(s32[1,128]{1,0:T(1,128)} %param.11), channel_id=1, source_target_pairs={{0,8},{8,0},{16,24},{24,16},{1,9},{9,1},{17,25},{25,17},{2,10},{10... | collective-permute-start | bytes 1544 | tf_op jit(solution)/shard_map/ppermute | solution.py:288
  10.6 25.2 %collective-permute-start.2 = (bf16[4,128,512]{2,1,0:T(8,128)(2,1)}, bf16[4,128,512]{2,1,0:T(8,128)(2,1)S(1)}, u32[]{:S(2)}, u32[]{:S(2)}) collective-permute-start(bf16[4,128,512]{2,1,0:T(8,128)(2,1)} %get-tuple-element.28), channel_id=1, source_target_pairs={{0,1},{1,0},{2,3},{3,2},{4,5},{5,4},{6,7},{7,6},{8,9},{9,8},{10,11... | collective-permute-start | bytes 1572872 | tf_op jit(solution)/shard_map/ppermute | solution.py:294
  12.2 25.5 %collective-permute-start.3 = (bf16[4,128,512]{2,1,0:T(8,128)(2,1)}, bf16[4,128,512]{2,1,0:T(8,128)(2,1)S(1)}, u32[]{:S(2)}, u32[]{:S(2)}) collective-permute-start(bf16[4,128,512]{2,1,0:T(8,128)(2,1)} %get-tuple-element.29), channel_id=1, source_target_pairs={{0,16},{8,24},{16,0},{24,8},{1,17},{9,25},{17,1},{25,9},{2,18},{10... | collective-permute-start | bytes 1572872 | tf_op jit(solution)/shard_map/ppermute | solution.py:291
  14.3 0.7 copy-start.4
  15.0 23.2 %copy-start.5 = (bf16[512,256]{1,0:T(8,128)(2,1)S(1)}, bf16[512,256]{1,0:T(8,128)(2,1)}, u32[]{:S(2)}) copy-start(bf16[512,256]{1,0:T(8,128)(2,1)} %copy-done.4) | copy-start | bytes 786436
  16.7 21.1 %collective-permute-start.4 = (bf16[4,128,512]{2,1,0:T(8,128)(2,1)}, bf16[4,128,512]{2,1,0:T(8,128)(2,1)S(1)}, u32[]{:S(2)}, u32[]{:S(2)}) collective-permute-start(bf16[4,128,512]{2,1,0:T(8,128)(2,1)} %copy-done.7), channel_id=1, source_target_pairs={{0,17},{1,16},{2,19},{3,18},{4,21},{5,20},{6,23},{7,22},{8,25},{9,... | collective-permute-start | bytes 1572872 | tf_op jit(solution)/shard_map/ppermute | solution.py:303
  19.6 0.7 copy-start.10
  19.6 2.3 %copy-start.8 = (f32[256,64]{1,0:T(8,128)}, f32[256,64]{1,0:T(8,128)S(1)}, u32[]{:S(2)}) copy-start(f32[256,64]{1,0:T(8,128)S(1)} %get-tuple-element.49) | copy-start | bytes 196612
  19.7 2.3 %copy-start.9 = (f32[256,64]{1,0:T(8,128)}, f32[256,64]{1,0:T(8,128)S(1)}, u32[]{:S(2)}) copy-start(f32[256,64]{1,0:T(8,128)S(1)} %get-tuple-element.50) | copy-start | bytes 196612
  20.3 11.4 %collective-permute-start.8 = (bf16[512,256]{1,0:T(8,128)(2,1)}, bf16[512,256]{1,0:T(8,128)(2,1)S(1)}, u32[]{:S(2)}, u32[]{:S(2)}) collective-permute-start(bf16[512,256]{1,0:T(8,128)(2,1)} %copy-done.4), channel_id=1, source_target_pairs={{0,2},{1,3},{2,4},{3,5},{4,6},{5,7},{6,0},{7,1},{8,10},{9,11},{10,... | collective-permute-start | bytes 786440 | tf_op jit(solution)/shard_map/ppermute | solution.py:297
  22.0 13.8 %collective-permute-start.7 = (bf16[512,256]{1,0:T(8,128)(2,1)}, bf16[512,256]{1,0:T(8,128)(2,1)S(1)}, u32[]{:S(2)}, u32[]{:S(2)}) collective-permute-start(bf16[512,256]{1,0:T(8,128)(2,1)} %collective-permute-done.5.refs_9_), channel_id=1, source_target_pairs={{0,2},{1,3},{2,4},{3,5},{4,6},{5,7},{6,0},{7,1},{8,10},{9,11},{10,... | collective-permute-start | bytes 786440 | tf_op jit(solution)/shard_map/ppermute | solution.py:297
  24.9 1.2 %copy-start.3 = (bf16[1,128,4096]{2,1,0:T(8,128)(2,1)S(1)}, bf16[1,128,4096]{2,1,0:T(8,128)(2,1)}, u32[]{:S(2)}) copy-start(bf16[1,128,4096]{2,1,0:T(8,128)(2,1)} %param.8) | copy-start | bytes 3145732
  31.7 8.3 %collective-permute-start.1 = (bf16[4,128,512]{2,1,0:T(8,128)(2,1)S(1)}, bf16[4,128,512]{2,1,0:T(8,128)(2,1)S(1)}, u32[]{:S(2)}, u32[]{:S(2)}) collective-permute-start(bf16[4,128,512]{2,1,0:T(8,128)(2,1)S(1)} %get-tuple-element.27.refs_0_), channel_id=1, source_target_pairs={{0,8},{8,0},{16,24},{24,16},{1,9},{9,1},{17,25},{25,17},{2,10},{10... | collective-permute-start | bytes 1572872 | tf_op jit(solution)/shard_map/ppermute | solution.py:288
  37.7 2.6 %collective-permute-start.10 = (bf16[4,128,512]{2,1,0:T(8,128)(2,1)S(1)}, bf16[4,128,512]{2,1,0:T(8,128)(2,1)S(1)}, u32[]{:S(2)}, u32[]{:S(2)}) collective-permute-start(bf16[4,128,512]{2,1,0:T(8,128)(2,1)S(1)} %collective-permute-done.3.refs_4_), channel_id=1, source_target_pairs={{0,8},{8,0},{16,24},{24,16},{1,9},{9,1},{17,25},{25,17},{2,10},{10... | collective-permute-start | bytes 1572872 | tf_op jit(solution)/shard_map/ppermute | solution.py:288
  37.7 2.7 %collective-permute-start.11 = (bf16[4,128,512]{2,1,0:T(8,128)(2,1)S(1)}, bf16[4,128,512]{2,1,0:T(8,128)(2,1)S(1)}, u32[]{:S(2)}, u32[]{:S(2)}) collective-permute-start(bf16[4,128,512]{2,1,0:T(8,128)(2,1)S(1)} %collective-permute-done.4.refs_6_), channel_id=1, source_target_pairs={{0,8},{8,0},{16,24},{24,16},{1,9},{9,1},{17,25},{25,17},{2,10},{10... | collective-permute-start | bytes 1572872 | tf_op jit(solution)/shard_map/ppermute | solution.py:288
  38.3 2.9 %collective-permute-start.9 = (bf16[4,128,512]{2,1,0:T(8,128)(2,1)S(1)}, bf16[4,128,512]{2,1,0:T(8,128)(2,1)S(1)}, u32[]{:S(2)}, u32[]{:S(2)}) collective-permute-start(bf16[4,128,512]{2,1,0:T(8,128)(2,1)S(1)} %collective-permute-done.2.refs_2_), channel_id=1, source_target_pairs={{0,8},{8,0},{16,24},{24,16},{1,9},{9,1},{17,25},{25,17},{2,10},{10... | collective-permute-start | bytes 1572872 | tf_op jit(solution)/shard_map/ppermute | solution.py:288
  38.3 8.9 %collective-permute-start.19 = (bf16[512,256]{1,0:T(8,128)(2,1)S(1)}, bf16[512,256]{1,0:T(8,128)(2,1)S(1)}, u32[]{:S(2)}, u32[]{:S(2)}) collective-permute-start(bf16[512,256]{1,0:T(8,128)(2,1)S(1)} %copy-done.5), channel_id=1, source_target_pairs={{0,6},{1,7},{2,0},{3,1},{4,2},{5,3},{6,4},{7,5},{8,14},{9,15},{10,... | collective-permute-start | bytes 786440 | tf_op jit(solution)/shard_map/ppermute | solution.py:297
  40.1 12.8 %collective-permute-start.18 = (bf16[512,256]{1,0:T(8,128)(2,1)S(1)}, bf16[512,256]{1,0:T(8,128)(2,1)S(1)}, u32[]{:S(2)}, u32[]{:S(2)}) collective-permute-start(bf16[512,256]{1,0:T(8,128)(2,1)S(1)} %collective-permute-done.8.refs_9_), channel_id=1, source_target_pairs={{0,2},{1,3},{2,4},{3,5},{4,6},{5,7},{6,0},{7,1},{8,10},{9,11},{10,... | collective-permute-start | bytes 786440 | tf_op jit(solution)/shard_map/ppermute | solution.py:297
  43.5 12.5 %collective-permute-start.12 = (f32[256,256]{1,0:T(8,128)S(1)}, f32[256,256]{1,0:T(8,128)S(1)}, u32[]{:S(2)}, u32[]{:S(2)}) collective-permute-start(f32[256,256]{1,0:T(8,128)S(1)} %get-tuple-element.36), channel_id=1, source_target_pairs={{0,1},{1,0},{2,3},{3,2},{4,5},{5,4},{6,7},{7,6},{8,9},{9,8},{10,11... | collective-permute-start | bytes 786440 | tf_op jit(solution)/shard_map/ppermute | solution.py:294
  44.8 12.6 %collective-permute-start.13 = (f32[256,256]{1,0:T(8,128)S(1)}, f32[256,256]{1,0:T(8,128)S(1)}, u32[]{:S(2)}, u32[]{:S(2)}) collective-permute-start(f32[256,256]{1,0:T(8,128)S(1)} %get-tuple-element.37), channel_id=1, source_target_pairs={{0,16},{8,24},{16,0},{24,8},{1,17},{9,25},{17,1},{25,9},{2,18},{10... | collective-permute-start | bytes 786440 | tf_op jit(solution)/shard_map/ppermute | solution.py:291
  45.6 13.7 %collective-permute-start.14 = (f32[256,256]{1,0:T(8,128)S(1)}, f32[256,256]{1,0:T(8,128)S(1)}, u32[]{:S(2)}, u32[]{:S(2)}) collective-permute-start(f32[256,256]{1,0:T(8,128)S(1)} %get-tuple-element.38), channel_id=1, source_target_pairs={{0,17},{1,16},{2,19},{3,18},{4,21},{5,20},{6,23},{7,22},{8,25},{9,... | collective-permute-start | bytes 786440 | tf_op jit(solution)/shard_map/ppermute | solution.py:303
  53.8 7.3 %collective-permute-start.20 = (bf16[256,256]{1,0:T(8,128)(2,1)S(1)}, bf16[256,256]{1,0:T(8,128)(2,1)S(1)}, u32[]{:S(2)}, u32[]{:S(2)}) collective-permute-start(bf16[256,256]{1,0:T(8,128)(2,1)S(1)} %get-tuple-element.46), channel_id=1, source_target_pairs={{0,1},{1,0},{2,3},{3,2},{4,5},{5,4},{6,7},{7,6},{8,9},{9,8},{10,11... | collective-permute-start | bytes 393224 | tf_op jit(solution)/shard_map/ppermute | solution.py:294
  55.1 9.5 %collective-permute-start.21 = (bf16[256,256]{1,0:T(8,128)(2,1)S(1)}, bf16[256,256]{1,0:T(8,128)(2,1)S(1)}, u32[]{:S(2)}, u32[]{:S(2)}) collective-permute-start(bf16[256,256]{1,0:T(8,128)(2,1)S(1)} %get-tuple-element.47), channel_id=1, source_target_pairs={{0,16},{8,24},{16,0},{24,8},{1,17},{9,25},{17,1},{25,9},{2,18},{10... | collective-permute-start | bytes 393224 | tf_op jit(solution)/shard_map/ppermute | solution.py:291
  55.9 8.7 %collective-permute-start.22 = (bf16[256,256]{1,0:T(8,128)(2,1)S(1)}, bf16[256,256]{1,0:T(8,128)(2,1)S(1)}, u32[]{:S(2)}, u32[]{:S(2)}) collective-permute-start(bf16[256,256]{1,0:T(8,128)(2,1)S(1)} %get-tuple-element.48), channel_id=1, source_target_pairs={{0,17},{1,16},{2,19},{3,18},{4,21},{5,20},{6,23},{7,22},{8,25},{9,... | collective-permute-start | bytes 393224 | tf_op jit(solution)/shard_map/ppermute | solution.py:303
  59.4 8.1 %collective-permute-start.15 = (bf16[256,256]{1,0:T(8,128)(2,1)S(1)}, bf16[256,256]{1,0:T(8,128)(2,1)S(1)}, u32[]{:S(2)}, u32[]{:S(2)}) collective-permute-start(bf16[256,256]{1,0:T(8,128)(2,1)S(1)} %shard_map.79.refs_0_), channel_id=1, source_target_pairs={{0,16},{8,24},{16,0},{24,8},{1,17},{9,25},{17,1},{25,9},{2,18},{10... | collective-permute-start | bytes 393224 | tf_op jit(solution)/shard_map/ppermute | solution.py:306
  64.7 5.0 %collective-permute-start.23 = (bf16[256,256]{1,0:T(8,128)(2,1)S(1)}, bf16[256,256]{1,0:T(8,128)(2,1)S(1)}, u32[]{:S(2)}, u32[]{:S(2)}) collective-permute-start(bf16[256,256]{1,0:T(8,128)(2,1)S(1)} %shard_map.83.refs_0_), channel_id=1, source_target_pairs={{0,16},{8,24},{16,0},{24,8},{1,17},{9,25},{17,1},{25,9},{2,18},{10... | collective-permute-start | bytes 393224 | tf_op jit(solution)/shard_map/ppermute | solution.py:306
  65.5 4.3 %collective-permute-start.16 = (bf16[256,256]{1,0:T(8,128)(2,1)S(1)}, bf16[256,256]{1,0:T(8,128)(2,1)S(1)}, u32[]{:S(2)}, u32[]{:S(2)}) collective-permute-start(bf16[256,256]{1,0:T(8,128)(2,1)S(1)} %shard_map.79.refs_0_), channel_id=1, source_target_pairs={{0,8},{8,0},{16,24},{24,16},{1,9},{9,1},{17,25},{25,17},{2,10},{10... | collective-permute-start | bytes 393224 | tf_op jit(solution)/shard_map/ppermute | solution.py:288
  67.5 2.3 %collective-permute-start.17 = (bf16[256,256]{1,0:T(8,128)(2,1)S(1)}, bf16[256,256]{1,0:T(8,128)(2,1)S(1)}, u32[]{:S(2)}, u32[]{:S(2)}) collective-permute-start(bf16[256,256]{1,0:T(8,128)(2,1)S(1)} %collective-permute-done.15.refs_1_), channel_id=1, source_target_pairs={{0,8},{8,0},{16,24},{24,16},{1,9},{9,1},{17,25},{25,17},{2,10},{10... | collective-permute-start | bytes 393224 | tf_op jit(solution)/shard_map/ppermute | solution.py:288
  67.5 5.4 %collective-permute-start.24 = (bf16[256,256]{1,0:T(8,128)(2,1)S(1)}, bf16[256,256]{1,0:T(8,128)(2,1)S(1)}, u32[]{:S(2)}, u32[]{:S(2)}) collective-permute-start(bf16[256,256]{1,0:T(8,128)(2,1)S(1)} %shard_map.83.refs_0_), channel_id=1, source_target_pairs={{0,8},{8,0},{16,24},{24,16},{1,9},{9,1},{17,25},{25,17},{2,10},{10... | collective-permute-start | bytes 393224 | tf_op jit(solution)/shard_map/ppermute | solution.py:288
  69.8 3.1 %collective-permute-start.25 = (bf16[256,256]{1,0:T(8,128)(2,1)S(1)}, bf16[256,256]{1,0:T(8,128)(2,1)S(1)}, u32[]{:S(2)}, u32[]{:S(2)}) collective-permute-start(bf16[256,256]{1,0:T(8,128)(2,1)S(1)} %collective-permute-done.23.refs_1_), channel_id=1, source_target_pairs={{0,8},{8,0},{16,24},{24,16},{1,9},{9,1},{17,25},{25,17},{2,10},{10... | collective-permute-start | bytes 393224 | tf_op jit(solution)/shard_map/ppermute | solution.py:288

commit v4 on v3

--- a/solution.py
+++ b/solution.py
@@ -169,35 +169,40 @@
     out_ref[...] = add_up((own_ref, x_ref, y_ref, xy_ref)).astype(jnp.bfloat16)
 
 
-def turn_queries_kernel(q_ref, cosine_ref, sine_ref, after_ref, out_ref):
-    for h in range(out_ref.shape[0]):
-        query = q_ref[:, h * HD : (h + 1) * HD].astype(jnp.float32)
+def turn_queries_kernel(where, q_ref, cosine_ref, sine_ref, after_ref, out_ref):
+    half = out_ref.shape[0] // 2
+    core = where[3]
+    for h in range(2 * half):
+        side = 1 - core if h // half else core
+        start = pl.multiple_of((side * half + h % half) * HD, HD)
+        query = q_ref[:, pl.ds(start, HD)].astype(jnp.float32)
         out_ref[h] = turn(query, cosine_ref[...], sine_ref[...]).astype(jnp.bfloat16)
 
 
-def mask_kernel(chip_rows, n_chips, where, lists_ref, out_ref):
-    span_rows, tokens = out_ref.shape
+def mask_kernel(chip_rows, n_chips, where, lists_ref, *refs):
+    out_ref = refs[-1]
+    tokens = out_ref.shape[1]
     chip, core = where[4], where[3]
+    shape = (BLOCK, tokens)
+    row, column = (lax.broadcasted_iota(jnp.int32, shape, axis) for axis in range(2))
+    ahead = row - column
+    first_query = chip * chip_rows + core * tokens
     for j in range(n_chips):
-        first_key = lax.rem(chip - j + n_chips, n_chips) * chip_rows
-        shape = (chip_rows, tokens)
-        key = first_key + lax.broadcasted_iota(jnp.int32, shape, 0)
-        column = lax.broadcasted_iota(jnp.int32, shape, 1)
-        query = chip * chip_rows + core * tokens + column
-        key_block, query_row = key // BLOCK, column // BLOCK
-        listed = key < 0
-        for row in range(lists_ref.shape[0]):
-            for entry in range(lists_ref.shape[1]):
-                listed = listed | ((key_block == lists_ref[row, entry]) & (query_row == row))
-        out_ref[j * chip_rows : (j + 1) * chip_rows, :] = jnp.where(
-            listed & (key <= query), 0.0, neg_large
-        ).astype(jnp.bfloat16)
-
-
-def weigh_kernel(n_chips, group, where, q_ref, bias_ref, *refs):
-    key_refs, (weight_ref, total_ref, scores) = refs[: 2 * n_chips], refs[2 * n_chips :]
-    core = where[3]
-    heads_here = key_refs[0].shape[1] // HD
+        for b in range(chip_rows // BLOCK):
+            first_key = lax.rem(chip - j + n_chips, n_chips) * chip_rows + b * BLOCK
+            listed = ahead > tokens + BLOCK
+            for q in range(lists_ref.shape[0]):
+                found = lists_ref[q, 0] == first_key // BLOCK
+                for entry in range(1, lists_ref.shape[1]):
+                    found = found | (lists_ref[q, entry] == first_key // BLOCK)
+                limit = jnp.where(found, first_query - first_key, -tokens - BLOCK)
+                listed = listed | ((column // BLOCK == q) & (ahead <= limit))
+            rows = slice(j * chip_rows + b * BLOCK, j * chip_rows + (b + 1) * BLOCK)
+            out_ref[rows, :] = jnp.where(listed, 0.0, neg_large).astype(jnp.bfloat16)
+
+
+def weigh_kernel(first, group, q_ref, bias_ref, *refs):
+    key_refs, (weight_ref, total_ref, scores) = refs[:-3], refs[-3:]
     tokens = q_ref.shape[1]
     span_rows, lanes = scores.shape
     together = lanes // tokens
@@ -205,40 +210,55 @@
     square = (tokens, tokens)
     row, column = (lax.broadcasted_iota(jnp.int32, square, axis) for axis in range(2))
     pick = (row == column).astype(jnp.float32).astype(jnp.bfloat16)
-    for side in range(2):
-        first_head = (1 - core if side else core) * heads_here
-        for i in range(heads_here):
-            span = slice(i * HD, (i + 1) * HD)
-            keys = jnp.concatenate(
-                [ref[:, span] for ref in key_refs[side * n_chips : (side + 1) * n_chips]], axis=0
+    for pair in range(weight_ref.shape[0]):
+        span = slice(pair * HD, (pair + 1) * HD)
+        keys = jnp.concatenate([ref[:, span] for ref in key_refs], axis=0)
+        keys = jnp.concatenate([keys, bias_ref[...]], axis=1)
+        for g in range(0, group, together):
+            head = first + pair * group + g
+            query = jnp.concatenate(
+                [jnp.concatenate([q_ref[head + t], pick], axis=1) for t in range(together)],
+                axis=0,
             )
-            keys = jnp.concatenate([keys, bias_ref[...]], axis=1)
-            pair = side * heads_here + i
-            for g in range(0, group, together):
-                query = jnp.concatenate(
-                    [
-                        jnp.concatenate([q_ref[(first_head + i) * group + g + t], pick], axis=1)
-                        for t in range(together)
-                    ],
-                    axis=0,
-                )
-                scores[...] = lax.dot_general(
-                    keys, query, (((1,), (1,)), ((), ())), preferred_element_type=jnp.float32
-                )
-                top = scores[:8]
-                for r in range(8, span_rows, 8):
-                    top = jnp.maximum(top, scores[r : r + 8])
-                top = jnp.max(top, axis=0, keepdims=True)
-                total = jnp.zeros((16, lanes), jnp.float32)
-                columns = slice(g * tokens, g * tokens + lanes)
-                for r in range(0, span_rows, 16):
-                    probabilities = jnp.exp2((scores[r : r + 16] - top) * scale)
-                    total = total + probabilities
-                    weight_ref[pair, r : r + 16, columns] = probabilities.astype(jnp.bfloat16)
-                total_ref[pair, :, columns] = jnp.sum(total, axis=0, keepdims=True)
-
-
-def mix_kernel(n_chips, group, where, weight_ref, total_ref, *refs):
+            scores[...] = lax.dot_general(
+                keys, query, (((1,), (1,)), ((), ())), preferred_element_type=jnp.float32
+            )
+            top = scores[:8]
+            for r in range(8, span_rows, 8):
+                top = jnp.maximum(top, scores[r : r + 8])
+            top = jnp.max(top, axis=0, keepdims=True)
+            total = jnp.zeros((16, lanes), jnp.float32)
+            columns = slice(g * tokens, g * tokens + lanes)
+            for r in range(0, span_rows, 16):
+                probabilities = jnp.exp2((scores[r : r + 16] - top) * scale)
+                total = total + probabilities
+                weight_ref[pair, r : r + 16, columns] = probabilities.astype(jnp.bfloat16)
+            total_ref[pair, :, columns] = jnp.sum(total, axis=0, keepdims=True)
+
+
+def weigh(query_rot, bias, keys, first, group):
+    _, tokens, _ = query_rot.shape
+    span_rows = bias.shape[0]
+    pairs, lanes = keys[0].shape[1] // HD, group * tokens
+    held = 2 * query_rot.size + 10 * bias.size + 2 * pairs * span_rows * lanes
+    return pl.pallas_call(
+        functools.partial(weigh_kernel, first, group),
+        out_shape=(
+            jax.ShapeDtypeStruct((pairs, span_rows, lanes), jnp.bfloat16),
+            jax.ShapeDtypeStruct((pairs, 1, lanes), jnp.float32),
+        ),
+        in_specs=[VMEM] * (2 + len(keys)),
+        out_specs=(VMEM, VMEM),
+        scratch_shapes=[pltpu.VMEM((span_rows, 2 * tokens), jnp.float32)],
+        compiler_params=params(held + 4 * len(keys) * keys[0].size),
+        cost_estimate=cost(
+            2 * pairs * span_rows * lanes * HD, held, pairs * span_rows * lanes
+        ),
+    )(query_rot, bias, *keys)
+
+
+def mix_kernel(n_chips, group, where, *refs):
+    weight_refs, total_refs, refs = refs[:2], refs[2:4], refs[4:]
     value_refs, out_ref, buf, sems = refs[: 2 * n_chips], refs[-3], refs[-2], refs[-1]
     core = where[3]
     heads_here = value_refs[0].shape[1] // HD
@@ -255,8 +275,8 @@
             )
             pair = side * heads_here + i
             mixed = jnp.dot(
-                values.T, weight_ref[pair], preferred_element_type=jnp.float32
-            ) * (1.0 / total_ref[pair])
+                values.T, weight_refs[side][i], preferred_element_type=jnp.float32
+            ) * (1.0 / total_refs[side][i])
             for g in range(group):
                 buf[pair, :, g * HD : (g + 1) * HD] = mixed[
                     :, g * tokens : (g + 1) * tokens
@@ -322,8 +342,14 @@
             came[j] = over_z(before, 1)
         return came
 
-    cuts = cut_tokens(where, tokens_local, n_line)
-    key_own = cut_weight(where, key_weight, cuts[0])
+    key_own = cut_weight(where, key_weight)
+    cuts = cut_tokens(where, tokens_local, n_line, key_own)
+    key_pieces = gather_pieces(key_own, True, [])
+    held = [cuts[0], over_x(cuts[1]), over_y(cuts[2]), over_xy(cuts[3])]
+    value_own = cut_weight(where, value_weight, cuts[0])
+    value_pieces = gather_pieces(value_own, False, [])
+
+    positions = lax.optimization_barrier((positions, key_pieces[1]))[0]
     token_pos = positions[0]
     pos_pair = jnp.stack([token_pos, over_core(positions)[0]])
     pos_chip = jnp.where(core == 0, pos_pair, pos_pair[::-1]).reshape(-1)
@@ -335,37 +361,33 @@
     query_rot = pl.pallas_call(
         turn_queries_kernel,
         out_shape=jax.ShapeDtypeStruct((n_heads, tok_rows, HD), jnp.bfloat16),
-        in_specs=[VMEM] * 3 + [ANY],
+        in_specs=[SMEM] + [VMEM] * 3 + [ANY],
         out_specs=VMEM,
         compiler_params=params(4 * query_local.size),
         cost_estimate=cost(3 * query_local.size, 4 * query_local.size),
-    )(query_local, query_cosine, query_sine, key_own)
+    )(where, query_local, query_cosine, query_sine, key_pieces[1])
 
     chip_rows = 2 * tok_rows
     bias = pl.pallas_call(
         functools.partial(mask_kernel, chip_rows, n_chips),
         out_shape=jax.ShapeDtypeStruct((n_chips * chip_rows, tok_rows), jnp.bfloat16),
-        in_specs=[SMEM, SMEM],
+        in_specs=[SMEM, SMEM, ANY],
         out_specs=VMEM,
         compiler_params=params(16 * chip_rows * tok_rows),
         cost_estimate=cost(20 * n_chips * chip_rows * tok_rows, 0),
-    )(where, block_lists[0])
-
-    key_pieces = gather_pieces(key_own, True, [bias, cosine, sine_part])
-    held = [cuts[0], over_x(cuts[1]), over_y(cuts[2]), over_xy(cuts[3])]
-    value_own = cut_weight(where, value_weight, cuts[0])
-    value_pieces = gather_pieces(value_own, False, [])
-
-    held[1:] = lax.optimization_barrier(
-        (*held[1:], key_pieces[up], value_pieces[1], query_rot)
-    )[:3]
-    sets = [(array, over_core(array)) for array in held]
-
+    )(where, block_lists[0], key_pieces[up])
+
+    held[1:3] = lax.optimization_barrier((*held[1:3], key_pieces[up], value_pieces[1], query_rot, bias, cosine, sine_part))[:2]
     f32, bf16 = jnp.float32, jnp.bfloat16
     every = list(range(n_line))
-    key_parts = project(
-        where, sets, every, key_pieces, None, (f32,), key_own
-    )
+    sets = [(array, over_core(array)) for array in held[:3]]
+    key_x, key_y = project(where, sets[1:], every, key_pieces, None, (f32,), bias, cosine, sine_part)
+    *held[3:], _ = lax.optimization_barrier((held[3], held[1], value_pieces[-1]))
+    sets.append((held[3], over_core(held[3])))
+    key_own_part, key_xy = project(
+        where, [sets[0], sets[3]], every, key_pieces, None, (f32,), key_x
+    )
+    key_parts = (key_own_part, key_x, key_y, key_xy)
     key_here = pl.pallas_call(
         finish_keys_kernel,
         out_shape=jax.ShapeDtypeStruct(key_parts[0].shape, bf16),
@@ -378,7 +400,7 @@
         cosine, sine_part,
     )
     keys = [key_here] + [from_chip(key_here, j) for j in range(1, n_chips)]
-    keys += [over_core(array) for array in keys]
+    keys_other = [over_core(array) for array in keys]
 
     early = [j for j in every if j != up]
     early_values = project(where, sets, early, value_pieces, None, (f32,), key_parts[0])
@@ -391,30 +413,19 @@
         compiler_params=params(10 * value_parts[0].size),
         cost_estimate=cost(3 * value_parts[0].size, 10 * value_parts[0].size),
     )(value_parts[0], over_x(value_parts[1]), over_y(value_parts[2]), over_xy(value_parts[3]))
+    weights, totals = weigh(query_rot, bias, keys, 0, group)
     values = [value_here] + [from_chip(value_here, j) for j in range(1, n_chips)]
+    *values, weights = lax.optimization_barrier((*values, weights))
     values += [over_core(array) for array in values]
+    weights_other, totals_other = weigh(query_rot, bias, keys_other, n_heads // 2, group)
 
     span_rows = n_chips * chip_rows
-    pairs, lanes = 2 * (keys[0].shape[1] // HD), group * tok_rows
+    pairs = n_heads // group
     held = 2 * tok_rows * (query_width + n_heads * span_rows)
-    weights, totals = pl.pallas_call(
-        functools.partial(weigh_kernel, n_chips, group),
-        out_shape=(
-            jax.ShapeDtypeStruct((pairs, span_rows, lanes), bf16),
-            jax.ShapeDtypeStruct((pairs, 1, lanes), f32),
-        ),
-        in_specs=[SMEM] + [VMEM] * (2 + len(keys)),
-        out_specs=(VMEM, VMEM),
-        scratch_shapes=[pltpu.VMEM((span_rows, 2 * tok_rows), f32)],
-        compiler_params=params(held + 10 * bias.size + 4 * span_rows * key_width),
-        cost_estimate=cost(
-            2 * tok_rows * query_width * span_rows, held, tok_rows * n_heads * span_rows
-        ),
-    )(where, query_rot, bias, *keys)
     mixed = pl.pallas_call(
         functools.partial(mix_kernel, n_chips, group),
         out_shape=jax.ShapeDtypeStruct((tok_rows, query_width), bf16),
-        in_specs=[SMEM] + [VMEM] * (2 + len(values)),
+        in_specs=[SMEM] + [VMEM] * (4 + len(values)),
         out_specs=ANY,
         scratch_shapes=[
             pltpu.VMEM((pairs, tok_rows, group * HD), bf16),
@@ -422,7 +433,7 @@
         ],
         compiler_params=params(held + 4 * span_rows * key_width),
         cost_estimate=cost(2 * tok_rows * query_width * span_rows, held),
-    )(where, weights, totals, *values)
+    )(where, weights, weights_other, totals, totals_other, *values)
     return mixed[None]
 
 

time: 75.4 us -> 70.9 us (0.940)
  waiting for transfers between devices: 28.2 us -> 22.8 us
  starting transfers between devices: 22.2 us -> 26.1 us
  other arithmetic: 3.68 us -> 2.09 us
  local copies, waits for them, and re-layouts: 5.55 us -> 4.17 us
    ppermute x6, waiting for transfers between devices: 15.1 us -> 10.2 us  [over_z(): lax.ppermute(array, 'dp', [(i, (i + 2 * step) % n_dp) for i in range(n_dp)])]
    ppermute x3, starting transfers between devices: 3.16 us -> 4.72 us  [over_y(): return lax.ppermute(array, 'ctx', [(i, i ^ 2) for i in range(n_ctx)])]
    unnamed x26 -> x18, local copies, waits for them, and re-layouts: 5.44 us -> 4.06 us
    ppermute x3, waiting for transfers between devices: 1.88 us -> 3.14 us  [over_xy(): return lax.ppermute(array, ('ctx', 'dp'), pairs)]
    ppermute x3, waiting for transfers between devices: 5.44 us -> 4.41 us  [over_y(): return lax.ppermute(array, 'ctx', [(i, i ^ 2) for i in range(n_ctx)])]
    ppermute x3, starting transfers between devices: 3.26 us -> 4.22 us  [over_xy(): return lax.ppermute(array, ('ctx', 'dp'), pairs)]
    pallas_call x1, Pallas kernels: 1.62 us -> 0.68 us  [on_device(): pl.pallas_call(functools.partial(mask_kernel, chip_rows, n_chips), out_sh...]
    concatenate x1, other arithmetic: 1.04 us -> 0.1 us  [rope_tables(): jnp.concatenate([-sine_part, sine_part], axis=1)]
  transfers between devices with their start and end apart: 26 -> 26, of which waited for: 13 -> 12; matrix products, arithmetic and copies ran while one was open for 5% -> 3% of each run, Pallas kernels for 14% -> 18%
where the time goes in v4:
time: 70.9 us; the launch traced here: 70.6 us
  starting transfers between devices  26.1 us (37%)
  waiting for transfers between devices  22.8 us (32%)
  Pallas kernels  15.1 us (21%)
  local copies, waits for them, and re-layouts  4.17 us (6%)
  other arithmetic  2.09 us (3%)
    ppermute x6, waiting for transfers between devices, over_z(): lax.ppermute(array, 'dp', [(i, (i + 2 * step) % n_dp) for i in range(n_dp)])  10.2 us
    ppermute x6, starting transfers between devices, over_z(): lax.ppermute(array, 'dp', [(i, (i + 2 * step) % n_dp) for i in range(n_dp)])  9.2 us
    pallas_call x4, Pallas kernels, project(): pl.pallas_call(functools.partial(project_kernel, n_sets, lines, bool(star...  5.48 us
    ppermute x3, starting transfers between devices, over_y(): return lax.ppermute(array, 'ctx', [(i, i ^ 2) for i in range(n_ctx)])  4.72 us
    ppermute x3, starting transfers between devices, over_x(): return lax.ppermute(array, 'dp', [(i, i ^ 1) for i in range(n_dp)])  4.6 us
    ppermute x3, waiting for transfers between devices, over_y(): return lax.ppermute(array, 'ctx', [(i, i ^ 2) for i in range(n_ctx)])  4.41 us
    ppermute x3, starting transfers between devices, over_xy(): return lax.ppermute(array, ('ctx', 'dp'), pairs)  4.22 us
    unnamed x18, local copies, waits for them, and re-layouts  4.06 us
  transfers between devices with their start and end apart: 26, of which 12 were waited for; matrix products, arithmetic and copies ran while one was open for 3% of the time, Pallas kernels for 18%

profile of v4, /device:TPU:0, one launch (start us, length us, event | category | flops | bytes accessed | tf_op | source)
XLA Modules:
  0.0 70.6 jit_solution(3072925771617326044)
XLA Ops:
  0.0 0.1 stack.26.where
  0.1 1.2 %copy-done.1 = bf16[1024,512]{1,0:T(8,128)(2,1)S(1)} copy-done((bf16[1024,512]{1,0:T(8,128)(2,1)S(1)}, bf16[1024,512]{1,0:T(8,128)(2,1)}, u32[]{:S(2)}) %copy-start.1) | copy-done | bytes 1048600
  1.3 0.6 shard_map.73.refs_0_.refs_4_
  1.9 3.1 %collective-permute-start.3 = (bf16[512,256]{1,0:T(8,128)(2,1)S(1)}, bf16[512,256]{1,0:T(8,128)(2,1)S(1)}, u32[]{:S(2)}, u32[]{:S(2)}) collective-permute-start(bf16[512,256]{1,0:T(8,128)(2,1)S(1)} %shard_map.73.refs_0_.refs_4_), channel_id=1, source_target_pairs={{0,2},{1,3},{2,4},{3,5},{4,6},{5,7},{6,0},{7,1},{8,10},{9,11},{10,... | collective-permute-start | bytes 786440 | tf_op jit(solution)/shard_map/ppermute | solution.py:317
  5.0 2.1 %collective-permute-start.4 = (bf16[512,256]{1,0:T(8,128)(2,1)S(1)}, bf16[512,256]{1,0:T(8,128)(2,1)S(1)}, u32[]{:S(2)}, u32[]{:S(2)}) collective-permute-start(bf16[512,256]{1,0:T(8,128)(2,1)S(1)} %shard_map.73.refs_0_.refs_4_), channel_id=1, source_target_pairs={{0,6},{1,7},{2,0},{3,1},{4,2},{5,3},{6,4},{7,5},{8,14},{9,15},{10,... | collective-permute-start | bytes 786440 | tf_op jit(solution)/shard_map/ppermute | solution.py:317
  7.1 1.6 %copy-done = bf16[1,128,8192]{2,1,0:T(8,128)(2,1)S(1)} copy-done((bf16[1,128,8192]{2,1,0:T(8,128)(2,1)S(1)}, bf16[1,128,8192]{2,1,0:T(8,128)(2,1)}, u32[]{:S(2)}) %copy-start) | copy-done | bytes 2097176
  8.7 1.7 %shard_map.74 = (bf16[4,128,512]{2,1,0:T(8,128)(2,1)S(1)}, bf16[4,128,512]{2,1,0:T(8,128)(2,1)}, bf16[4,128,512]{2,1,0:T(8,128)(2,1)}, bf16[4,128,512]{2,1,0:T(8,128)(2,1)S(1)}) custom-call(s32[5]{0:T(128)S(1)} %stack.26.where, bf16[128,8192]{1,0:T(8,128)(2,1)S(1)} %bitcast.11, bf16[512,256]{1,0:T(8,128)(2,1)S(1)} %shard_map.73.refs_0_.refs_4_), custom_call_target="tpu_custom_call" | custom-call | bytes 4194304 | tf_op jit(solution)/shard_map/pallas_call | solution.py:99
  10.3 1.6 %collective-permute-start.1 = (bf16[4,128,512]{2,1,0:T(8,128)(2,1)}, bf16[4,128,512]{2,1,0:T(8,128)(2,1)S(1)}, u32[]{:S(2)}, u32[]{:S(2)}) collective-permute-start(bf16[4,128,512]{2,1,0:T(8,128)(2,1)} %get-tuple-element.34), channel_id=1, source_target_pairs={{0,1},{1,0},{2,3},{3,2},{4,5},{5,4},{6,7},{7,6},{8,9},{9,8},{10,11... | collective-permute-start | bytes 1572872 | tf_op jit(solution)/shard_map/ppermute | solution.py:314
  12.0 1.5 %collective-permute-start.2 = (bf16[4,128,512]{2,1,0:T(8,128)(2,1)}, bf16[4,128,512]{2,1,0:T(8,128)(2,1)S(1)}, u32[]{:S(2)}, u32[]{:S(2)}) collective-permute-start(bf16[4,128,512]{2,1,0:T(8,128)(2,1)} %get-tuple-element.35), channel_id=1, source_target_pairs={{0,16},{8,24},{16,0},{24,8},{1,17},{9,25},{17,1},{25,9},{2,18},{10... | collective-permute-start | bytes 1572872 | tf_op jit(solution)/shard_map/ppermute | solution.py:311
  13.5 0.6 shard_map.75.refs_8_
  14.1 0.0 copy-start.4
  14.1 0.1 collective-permute-start.6
  14.2 0.1 collective-permute-start.7
  14.3 4.3 %collective-permute-done.4.refs_7_ = bf16[512,256]{1,0:T(8,128)(2,1)S(1)} collective-permute-done((bf16[512,256]{1,0:T(8,128)(2,1)S(1)}, bf16[512,256]{1,0:T(8,128)(2,1)S(1)}, u32[]{:S(2)}, u32[]{:S(2)}) %collective-permute-start.4) | collective-permute-done | bytes 262176 | tf_op jit(solution)/shard_map/ppermute | solution.py:317
  18.6 2.7 %collective-permute-start.10 = (bf16[4,128,512]{2,1,0:T(8,128)(2,1)}, bf16[4,128,512]{2,1,0:T(8,128)(2,1)S(1)}, u32[]{:S(2)}, u32[]{:S(2)}) collective-permute-start(bf16[4,128,512]{2,1,0:T(8,128)(2,1)} %copy-done.5), channel_id=1, source_target_pairs={{0,17},{1,16},{2,19},{3,18},{4,21},{5,20},{6,23},{7,22},{8,25},{9,... | collective-permute-start | bytes 1572872 | tf_op jit(solution)/shard_map/ppermute | solution.py:323
  21.3 0.0 collective-permute-done.7
  21.3 1.7 %collective-permute-start.5 = (bf16[512,256]{1,0:T(8,128)(2,1)S(1)}, bf16[512,256]{1,0:T(8,128)(2,1)S(1)}, u32[]{:S(2)}, u32[]{:S(2)}) collective-permute-start(bf16[512,256]{1,0:T(8,128)(2,1)S(1)} %collective-permute-done.3.after_ref.refs_5_), channel_id=1, source_target_pairs={{0,2},{1,3},{2,4},{3,5},{4,6},{5,7},{6,0},{7,1},{8,10},{9,11},{10,... | collective-permute-start | bytes 786440 | tf_op jit(solution)/shard_map/ppermute | solution.py:317
  23.0 1.8 %fusion.3 = (f32[256,64]{1,0:T(8,128)S(1)}, f32[256,64]{1,0:T(8,128)S(1)}, f32[256,64]{1,0:T(8,128)S(1)}) fusion(f32[64]{0:T(128)S(1)} %copy-done.7, s32[64]{0:T(128)S(1)} %copy-done.8, s32[256]{0:T(256)S(1)} %select_bitcast_fusion), kind=kLoop, calls=%fused_computation.7 | loop fusion | flops 163840 | bytes 198144 | tf_op jit(solution)/shard_map/sin | solution.py:48
  24.9 5.3 %collective-permute-done.5.refs_0_.refs_6_ = bf16[512,256]{1,0:T(8,128)(2,1)S(1)} collective-permute-done((bf16[512,256]{1,0:T(8,128)(2,1)S(1)}, bf16[512,256]{1,0:T(8,128)(2,1)S(1)}, u32[]{:S(2)}, u32[]{:S(2)}) %collective-permute-start.5) | collective-permute-done | bytes 262176 | tf_op jit(solution)/shard_map/ppermute | solution.py:317
  30.2 1.7 %collective-permute-start.11 = (bf16[512,256]{1,0:T(8,128)(2,1)S(1)}, bf16[512,256]{1,0:T(8,128)(2,1)S(1)}, u32[]{:S(2)}, u32[]{:S(2)}) collective-permute-start(bf16[512,256]{1,0:T(8,128)(2,1)S(1)} %shard_map.75.refs_8_), channel_id=1, source_target_pairs={{0,6},{1,7},{2,0},{3,1},{4,2},{5,3},{6,4},{7,5},{8,14},{9,15},{10,... | collective-permute-start | bytes 786440 | tf_op jit(solution)/shard_map/ppermute | solution.py:317
  31.9 0.1 fusion.6
  32.0 0.0 copy-start.3
  32.0 1.2 %copy-done.3 = bf16[1,128,4096]{2,1,0:T(8,128)(2,1)S(1)} copy-done((bf16[1,128,4096]{2,1,0:T(8,128)(2,1)S(1)}, bf16[1,128,4096]{2,1,0:T(8,128)(2,1)}, u32[]{:S(2)}) %copy-start.3) | copy-done | bytes 1048600
  33.2 1.1 %shard_map.76.q_ref = bf16[32,128,128]{2,1,0:T(8,128)(2,1)S(1)} custom-call(s32[5]{0:T(128)S(1)} %stack.26.where, bf16[128,4096]{1,0:T(8,128)(2,1)S(1)} %bitcast.12, f32[128,128]{1,0:T(8,128)S(1)} %get-tuple-element.65.cosine_ref, f32[128,128]{1,0:T(8,128)S(1)} %get-tuple-element.64.sine_ref, bf16[512,256]{1,0:T(8,128)(2,1)S(1)} %collective-permute-done.3.after_ref.refs_5_), custom_call_target="tpu_custom_call" | custom-call | flops 1572864 | bytes 2097152 | tf_op jit(solution)/shard_map/pallas_call | solution.py:361
  34.3 0.1 pad_maximum_fusion
  34.5 0.7 shard_map.77.refs_8_.bias_ref
  35.2 0.0 collective-permute-done.6.refs_9_
  35.2 1.2 %collective-permute-done.2.refs_2_.refs_4_ = bf16[4,128,512]{2,1,0:T(8,128)(2,1)S(1)} collective-permute-done((bf16[4,128,512]{2,1,0:T(8,128)(2,1)}, bf16[4,128,512]{2,1,0:T(8,128)(2,1)S(1)}, u32[]{:S(2)}, u32[]{:S(2)}) %collective-permute-start.2) | collective-permute-done | bytes 524320 | tf_op jit(solution)/shard_map/ppermute | solution.py:311
  36.4 0.5 collective-permute-start.9
  36.9 0.0 collective-permute-start
  36.9 0.0 collective-permute-done.11.refs_10_
  36.9 0.0 collective-permute-done.10.refs_2_.refs_6_
  36.9 0.5 collective-permute-start.12
  37.4 0.6 collective-permute-start.13
  38.0 0.3 collective-permute-done.8.refs_1_.refs_3_
  38.3 0.7 %collective-permute-done.9.refs_3_.refs_5_ = bf16[4,128,512]{2,1,0:T(8,128)(2,1)S(1)} collective-permute-done((bf16[4,128,512]{2,1,0:T(8,128)(2,1)S(1)}, bf16[4,128,512]{2,1,0:T(8,128)(2,1)S(1)}, u32[]{:S(2)}, u32[]{:S(2)}) %collective-permute-start.9) | collective-permute-done | bytes 524320 | tf_op jit(solution)/shard_map/ppermute | solution.py:308
  39.0 1.3 %shard_map.78 = (f32[256,256]{1,0:T(8,128)S(1)}, f32[256,256]{1,0:T(8,128)S(1)}) custom-call(s32[5]{0:T(128)S(1)} %stack.26.where, bf16[4,128,512]{2,1,0:T(8,128)(2,1)S(1)} %collective-permute-done.1.refs_0_.refs_2_, bf16[4,128,512]{2,1,0:T(8,128)(2,1)S(1)} %collective-permute-done.8.refs_1_.refs_3_, ...), custom_call_target="tpu_custom_call" | custom-call | flops 536870912 | bytes 4194304 | tf_op jit(solution)/shard_map/pallas_call | solution.py:141
  40.3 0.4 collective-permute-start.18
  40.7 1.7 %collective-permute-start.19 = (f32[256,256]{1,0:T(8,128)S(1)}, f32[256,256]{1,0:T(8,128)S(1)}, u32[]{:S(2)}, u32[]{:S(2)}) collective-permute-start(f32[256,256]{1,0:T(8,128)S(1)} %get-tuple-element.52), channel_id=1, source_target_pairs={{0,16},{8,24},{16,0},{24,8},{1,17},{9,25},{17,1},{25,9},{2,18},{10... | collective-permute-start | bytes 786440 | tf_op jit(solution)/shard_map/ppermute | solution.py:311
  42.4 0.0 collective-permute-done.refs_1_
  42.4 0.0 collective-permute-done.12.refs_3_.refs_7_
  42.4 1.3 %shard_map.79 = (f32[256,256]{1,0:T(8,128)S(1)}, f32[256,256]{1,0:T(8,128)S(1)}) custom-call(s32[5]{0:T(128)S(1)} %stack.26.where, bf16[4,128,512]{2,1,0:T(8,128)(2,1)S(1)} %get-tuple-element.33.refs_0_, bf16[4,128,512]{2,1,0:T(8,128)(2,1)S(1)} %collective-permute-done.refs_1_, bf16[4,128,512]{2,1,0:T(8,128)(2,1)S(1)} %collective-permute-done.10.refs_2_.refs_6_, ...), custom_call_target="tpu_custom_call" | custom-call | flops 536870912 | bytes 4194304 | tf_op jit(solution)/shard_map/pallas_call | solution.py:141
  43.7 1.5 %collective-permute-start.20 = (f32[256,256]{1,0:T(8,128)S(1)}, f32[256,256]{1,0:T(8,128)S(1)}, u32[]{:S(2)}, u32[]{:S(2)}) collective-permute-start(f32[256,256]{1,0:T(8,128)S(1)} %get-tuple-element.53), channel_id=1, source_target_pairs={{0,17},{1,16},{2,19},{3,18},{4,21},{5,20},{6,23},{7,22},{8,25},{9,... | collective-permute-start | bytes 786440 | tf_op jit(solution)/shard_map/ppermute | solution.py:323
  45.2 2.0 %shard_map.80 = (f32[256,256]{1,0:T(8,128)S(1)}, f32[256,256]{1,0:T(8,128)S(1)}, f32[256,256]{1,0:T(8,128)S(1)}, f32[256,256]{1,0:T(8,128)S(1)}) custom-call(s32[5]{0:T(128)S(1)} %stack.26.where, bf16[4,128,512]{2,1,0:T(8,128)(2,1)S(1)} %get-tuple-element.33.refs_0_, bf16[4,128,512]{2,1,0:T(8,128)(2,1)S(1)} %collective-permute-done.refs_1_, ...), custom_call_target="tpu_custom_call" | custom-call | flops 805306368 | bytes 7077888 | tf_op jit(solution)/shard_map/pallas_call | solution.py:141
  47.2 0.6 collective-permute-done.13.refs_8_
  47.8 1.0 %shard_map.81 = (bf16[256,256]{1,0:T(8,128)(2,1)S(1)}, bf16[256,256]{1,0:T(8,128)(2,1)S(1)}, bf16[256,256]{1,0:T(8,128)(2,1)S(1)}, bf16[256,256]{1,0:T(8,128)(2,1)S(1)}) custom-call(s32[5]{0:T(128)S(1)} %stack.26.where, bf16[4,128,512]{2,1,0:T(8,128)(2,1)S(1)} %get-tuple-element.33.refs_0_, bf16[4,128,512]{2,1,0:T(8,128)(2,1)S(1)} %collective-permute-done.refs_1_, ...), custom_call_target="tpu_custom_call" | custom-call | flops 268435456 | bytes 6553600 | tf_op jit(solution)/shard_map/pallas_call | solution.py:141
  48.8 2.5 %collective-permute-start.14 = (bf16[256,256]{1,0:T(8,128)(2,1)S(1)}, bf16[256,256]{1,0:T(8,128)(2,1)S(1)}, u32[]{:S(2)}, u32[]{:S(2)}) collective-permute-start(bf16[256,256]{1,0:T(8,128)(2,1)S(1)} %get-tuple-element.49), channel_id=1, source_target_pairs={{0,1},{1,0},{2,3},{3,2},{4,5},{5,4},{6,7},{7,6},{8,9},{9,8},{10,11... | collective-permute-start | bytes 393224 | tf_op jit(solution)/shard_map/ppermute | solution.py:314
  51.3 1.5 %collective-permute-start.15 = (bf16[256,256]{1,0:T(8,128)(2,1)S(1)}, bf16[256,256]{1,0:T(8,128)(2,1)S(1)}, u32[]{:S(2)}, u32[]{:S(2)}) collective-permute-start(bf16[256,256]{1,0:T(8,128)(2,1)S(1)} %get-tuple-element.50), channel_id=1, source_target_pairs={{0,16},{8,24},{16,0},{24,8},{1,17},{9,25},{17,1},{25,9},{2,18},{10... | collective-permute-start | bytes 393224 | tf_op jit(solution)/shard_map/ppermute | solution.py:311
  52.8 0.0 collective-permute-done.18.x_ref
  52.8 0.0 collective-permute-start.16
  52.8 0.1 collective-permute-done.19.y_ref
  53.0 3.1 %collective-permute-done.20.xy_ref = f32[256,256]{1,0:T(8,128)S(1)} collective-permute-done((f32[256,256]{1,0:T(8,128)S(1)}, f32[256,256]{1,0:T(8,128)S(1)}, u32[]{:S(2)}, u32[]{:S(2)}) %collective-permute-start.20) | collective-permute-done | bytes 262176 | tf_op jit(solution)/shard_map/ppermute | solution.py:323
  56.1 0.2 shard_map.83.refs_0_
  56.2 0.6 collective-permute-start.21
  56.9 1.1 %collective-permute-done.14.x_ref = bf16[256,256]{1,0:T(8,128)(2,1)S(1)} collective-permute-done((bf16[256,256]{1,0:T(8,128)(2,1)S(1)}, bf16[256,256]{1,0:T(8,128)(2,1)S(1)}, u32[]{:S(2)}, u32[]{:S(2)}) %collective-permute-start.14) | collective-permute-done | bytes 131104 | tf_op jit(solution)/shard_map/ppermute | solution.py:314
  58.0 3.1 %collective-permute-done.15.y_ref = bf16[256,256]{1,0:T(8,128)(2,1)S(1)} collective-permute-done((bf16[256,256]{1,0:T(8,128)(2,1)S(1)}, bf16[256,256]{1,0:T(8,128)(2,1)S(1)}, u32[]{:S(2)}, u32[]{:S(2)}) %collective-permute-start.15) | collective-permute-done | bytes 131104 | tf_op jit(solution)/shard_map/ppermute | solution.py:311
  61.1 0.1 shard_map.82.refs_4_
  61.2 1.1 %collective-permute-start.17 = (bf16[256,256]{1,0:T(8,128)(2,1)S(1)}, bf16[256,256]{1,0:T(8,128)(2,1)S(1)}, u32[]{:S(2)}, u32[]{:S(2)}) collective-permute-start(bf16[256,256]{1,0:T(8,128)(2,1)S(1)} %shard_map.82.refs_4_), channel_id=1, source_target_pairs={{0,16},{8,24},{16,0},{24,8},{1,17},{9,25},{17,1},{25,9},{2,18},{10... | collective-permute-start | bytes 393224 | tf_op jit(solution)/shard_map/ppermute | solution.py:326
  62.3 1.6 %collective-permute-done.21.refs_1_ = bf16[256,256]{1,0:T(8,128)(2,1)S(1)} collective-permute-done((bf16[256,256]{1,0:T(8,128)(2,1)S(1)}, bf16[256,256]{1,0:T(8,128)(2,1)S(1)}, u32[]{:S(2)}, u32[]{:S(2)}) %collective-permute-start.21) | collective-permute-done | bytes 131104 | tf_op jit(solution)/shard_map/ppermute | solution.py:326
  63.9 1.3 %shard_map.84 = (bf16[2,512,1024]{2,1,0:T(8,128)(2,1)S(1)}, f32[2,1,1024]{2,1,0:T(1,128)S(1)}) custom-call(bf16[32,128,128]{2,1,0:T(8,128)(2,1)S(1)} %shard_map.76.q_ref, bf16[512,128]{1,0:T(8,128)(2,1)S(1)} %shard_map.77.refs_8_.bias_ref, bf16[256,256]{1,0:T(8,128)(2,1)S(1)} %shard_map.83.refs_0_, bf16[256,256]{1,0:T(8,128)(2,1)S(1)} %collective-permute-done.21.refs_1_), custom_call_target="tpu_custom_call" | custom-call | flops 268435456 | bytes 3801088 | tf_op jit(solution)/shard_map/pallas_call | solution.py:244
  65.2 1.3 %collective-permute-done.17.refs_5_ = bf16[256,256]{1,0:T(8,128)(2,1)S(1)} collective-permute-done((bf16[256,256]{1,0:T(8,128)(2,1)S(1)}, bf16[256,256]{1,0:T(8,128)(2,1)S(1)}, u32[]{:S(2)}, u32[]{:S(2)}) %collective-permute-start.17) | collective-permute-done | bytes 131104 | tf_op jit(solution)/shard_map/ppermute | solution.py:326
  66.5 0.5 collective-permute-start.25
  67.0 1.3 %shard_map.85 = (bf16[2,512,1024]{2,1,0:T(8,128)(2,1)S(1)}, f32[2,1,1024]{2,1,0:T(1,128)S(1)}) custom-call(bf16[32,128,128]{2,1,0:T(8,128)(2,1)S(1)} %shard_map.76.q_ref, bf16[512,128]{1,0:T(8,128)(2,1)S(1)} %shard_map.77.refs_8_.bias_ref, bf16[256,256]{1,0:T(8,128)(2,1)S(1)} %collective-permute-done.22.refs_0_, ...), custom_call_target="tpu_custom_call" | custom-call | flops 268435456 | bytes 3801088 | tf_op jit(solution)/shard_map/pallas_call | solution.py:244
  68.4 2.1 %shard_map.86 = bf16[128,4096]{1,0:T(8,128)(2,1)} custom-call(s32[5]{0:T(128)S(1)} %stack.26.where, bf16[2,512,1024]{2,1,0:T(8,128)(2,1)S(1)} %get-tuple-element.55.refs_0_, bf16[2,512,1024]{2,1,0:T(8,128)(2,1)S(1)} %get-tuple-element.56.refs_1_, f32[2,1,1024]{2,1,0:T(1,128)S(1)} %get-tuple-element.57.refs_2_, f32[2,1,1024]{2,1,0:T(1,128)S(1)} %get-tuple-element.58.refs_3_, ...), custom_call_target="tpu_custom_call" | custom-call | flops 536870912 | bytes 5242880 | tf_op jit(solution)/shard_map/pallas_call | solution.py:425
  (27 shorter events, 0.1 us)
Async XLA Ops:
  0.1 1.2 %copy-start.1 = (bf16[1024,512]{1,0:T(8,128)(2,1)S(1)}, bf16[1024,512]{1,0:T(8,128)(2,1)}, u32[]{:S(2)}) copy-start(bf16[1024,512]{1,0:T(8,128)(2,1)} %weight_ref.2) | copy-start | bytes 3145732
  1.3 12.2 %copy-start.2 = (bf16[1024,512]{1,0:T(8,128)(2,1)S(1)}, bf16[1024,512]{1,0:T(8,128)(2,1)}, u32[]{:S(2)}) copy-start(bf16[1024,512]{1,0:T(8,128)(2,1)} %weight_ref.3) | copy-start | bytes 3145732
  1.9 12.3 %collective-permute-start.3 = (bf16[512,256]{1,0:T(8,128)(2,1)S(1)}, bf16[512,256]{1,0:T(8,128)(2,1)S(1)}, u32[]{:S(2)}, u32[]{:S(2)}) collective-permute-start(bf16[512,256]{1,0:T(8,128)(2,1)S(1)} %shard_map.73.refs_0_.refs_4_), channel_id=1, source_target_pairs={{0,2},{1,3},{2,4},{3,5},{4,6},{5,7},{6,0},{7,1},{8,10},{9,11},{10,... | collective-permute-start | bytes 786440 | tf_op jit(solution)/shard_map/ppermute | solution.py:317
  5.0 13.6 %collective-permute-start.4 = (bf16[512,256]{1,0:T(8,128)(2,1)S(1)}, bf16[512,256]{1,0:T(8,128)(2,1)S(1)}, u32[]{:S(2)}, u32[]{:S(2)}) collective-permute-start(bf16[512,256]{1,0:T(8,128)(2,1)S(1)} %shard_map.73.refs_0_.refs_4_), channel_id=1, source_target_pairs={{0,6},{1,7},{2,0},{3,1},{4,2},{5,3},{6,4},{7,5},{8,14},{9,15},{10,... | collective-permute-start | bytes 786440 | tf_op jit(solution)/shard_map/ppermute | solution.py:317
  7.1 1.6 %copy-start = (bf16[1,128,8192]{2,1,0:T(8,128)(2,1)S(1)}, bf16[1,128,8192]{2,1,0:T(8,128)(2,1)}, u32[]{:S(2)}) copy-start(bf16[1,128,8192]{2,1,0:T(8,128)(2,1)} %param.7) | copy-start | bytes 6291460
  8.6 5.5 %copy-start.6 = (s32[1,128]{1,0:T(1,128)S(1)}, s32[1,128]{1,0:T(1,128)}, u32[]{:S(2)}) copy-start(s32[1,128]{1,0:T(1,128)} %param.11) | copy-start | bytes 1540
  8.6 14.4 %copy-start.7 = (f32[64]{0:T(128)S(1)}, f32[64]{0:T(128)}, u32[]{:S(2)}) copy-start(f32[64]{0:T(128)} %constant.72) | copy-start | bytes 772
  8.6 14.4 %copy-start.8 = (s32[64]{0:T(128)S(1)}, s32[64]{0:T(128)}, u32[]{:S(2)}) copy-start(s32[64]{0:T(128)} %constant.68) | copy-start | bytes 772
  10.3 3.7 %copy-start.5 = (bf16[4,128,512]{2,1,0:T(8,128)(2,1)}, bf16[4,128,512]{2,1,0:T(8,128)(2,1)S(1)}, u32[]{:S(2)}) copy-start(bf16[4,128,512]{2,1,0:T(8,128)(2,1)S(1)} %get-tuple-element.40) | copy-start | bytes 1572868
  10.3 24.8 %collective-permute-start.1 = (bf16[4,128,512]{2,1,0:T(8,128)(2,1)}, bf16[4,128,512]{2,1,0:T(8,128)(2,1)S(1)}, u32[]{:S(2)}, u32[]{:S(2)}) collective-permute-start(bf16[4,128,512]{2,1,0:T(8,128)(2,1)} %get-tuple-element.34), channel_id=1, source_target_pairs={{0,1},{1,0},{2,3},{3,2},{4,5},{5,4},{6,7},{7,6},{8,9},{9,8},{10,11... | collective-permute-start | bytes 1572872 | tf_op jit(solution)/shard_map/ppermute | solution.py:314
  12.0 24.4 %collective-permute-start.2 = (bf16[4,128,512]{2,1,0:T(8,128)(2,1)}, bf16[4,128,512]{2,1,0:T(8,128)(2,1)S(1)}, u32[]{:S(2)}, u32[]{:S(2)}) collective-permute-start(bf16[4,128,512]{2,1,0:T(8,128)(2,1)} %get-tuple-element.35), channel_id=1, source_target_pairs={{0,16},{8,24},{16,0},{24,8},{1,17},{9,25},{17,1},{25,9},{2,18},{10... | collective-permute-start | bytes 1572872 | tf_op jit(solution)/shard_map/ppermute | solution.py:311
  14.1 20.4 %copy-start.4 = (s32[1,2,6]{2,1,0:T(2,128)S(1)}, s32[1,2,6]{2,1,0:T(2,128)}, u32[]{:S(2)}) copy-start(s32[1,2,6]{2,1,0:T(2,128)} %param.12) | copy-start | bytes 148
  14.1 21.1 %collective-permute-start.6 = (bf16[512,256]{1,0:T(8,128)(2,1)S(1)}, bf16[512,256]{1,0:T(8,128)(2,1)}, u32[]{:S(2)}, u32[]{:S(2)}) collective-permute-start(bf16[512,256]{1,0:T(8,128)(2,1)S(1)} %shard_map.75.refs_8_), channel_id=1, source_target_pairs={{0,2},{1,3},{2,4},{3,5},{4,6},{5,7},{6,0},{7,1},{8,10},{9,11},{10,... | collective-permute-start | bytes 786440 | tf_op jit(solution)/shard_map/ppermute | solution.py:317
  14.2 7.1 %collective-permute-start.7 = (s32[1,128]{1,0:T(1,128)S(1)}, s32[1,128]{1,0:T(1,128)S(1)}, u32[]{:S(2)}, u32[]{:S(2)}) collective-permute-start(s32[1,128]{1,0:T(1,128)S(1)} %copy-done.6), channel_id=1, source_target_pairs={{0,8},{8,0},{16,24},{24,16},{1,9},{9,1},{17,25},{25,17},{2,10},{10... | collective-permute-start | bytes 1544 | tf_op jit(solution)/shard_map/ppermute | solution.py:308
  18.6 18.3 %collective-permute-start.10 = (bf16[4,128,512]{2,1,0:T(8,128)(2,1)}, bf16[4,128,512]{2,1,0:T(8,128)(2,1)S(1)}, u32[]{:S(2)}, u32[]{:S(2)}) collective-permute-start(bf16[4,128,512]{2,1,0:T(8,128)(2,1)} %copy-done.5), channel_id=1, source_target_pairs={{0,17},{1,16},{2,19},{3,18},{4,21},{5,20},{6,23},{7,22},{8,25},{9,... | collective-permute-start | bytes 1572872 | tf_op jit(solution)/shard_map/ppermute | solution.py:323
  21.3 8.9 %collective-permute-start.5 = (bf16[512,256]{1,0:T(8,128)(2,1)S(1)}, bf16[512,256]{1,0:T(8,128)(2,1)S(1)}, u32[]{:S(2)}, u32[]{:S(2)}) collective-permute-start(bf16[512,256]{1,0:T(8,128)(2,1)S(1)} %collective-permute-done.3.after_ref.refs_5_), channel_id=1, source_target_pairs={{0,2},{1,3},{2,4},{3,5},{4,6},{5,7},{6,0},{7,1},{8,10},{9,11},{10,... | collective-permute-start | bytes 786440 | tf_op jit(solution)/shard_map/ppermute | solution.py:317
  30.2 6.7 %collective-permute-start.11 = (bf16[512,256]{1,0:T(8,128)(2,1)S(1)}, bf16[512,256]{1,0:T(8,128)(2,1)S(1)}, u32[]{:S(2)}, u32[]{:S(2)}) collective-permute-start(bf16[512,256]{1,0:T(8,128)(2,1)S(1)} %shard_map.75.refs_8_), channel_id=1, source_target_pairs={{0,6},{1,7},{2,0},{3,1},{4,2},{5,3},{6,4},{7,5},{8,14},{9,15},{10,... | collective-permute-start | bytes 786440 | tf_op jit(solution)/shard_map/ppermute | solution.py:317
  32.0 1.2 %copy-start.3 = (bf16[1,128,4096]{2,1,0:T(8,128)(2,1)S(1)}, bf16[1,128,4096]{2,1,0:T(8,128)(2,1)}, u32[]{:S(2)}) copy-start(bf16[1,128,4096]{2,1,0:T(8,128)(2,1)} %param.8) | copy-start | bytes 3145732
  36.4 1.9 %collective-permute-start.8 = (bf16[4,128,512]{2,1,0:T(8,128)(2,1)S(1)}, bf16[4,128,512]{2,1,0:T(8,128)(2,1)S(1)}, u32[]{:S(2)}, u32[]{:S(2)}) collective-permute-start(bf16[4,128,512]{2,1,0:T(8,128)(2,1)S(1)} %collective-permute-done.1.refs_0_.refs_2_), channel_id=1, source_target_pairs={{0,8},{8,0},{16,24},{24,16},{1,9},{9,1},{17,25},{25,17},{2,10},{10... | collective-permute-start | bytes 1572872 | tf_op jit(solution)/shard_map/ppermute | solution.py:308
  36.4 2.7 %collective-permute-start.9 = (bf16[4,128,512]{2,1,0:T(8,128)(2,1)S(1)}, bf16[4,128,512]{2,1,0:T(8,128)(2,1)S(1)}, u32[]{:S(2)}, u32[]{:S(2)}) collective-permute-start(bf16[4,128,512]{2,1,0:T(8,128)(2,1)S(1)} %collective-permute-done.2.refs_2_.refs_4_), channel_id=1, source_target_pairs={{0,8},{8,0},{16,24},{24,16},{1,9},{9,1},{17,25},{25,17},{2,10},{10... | collective-permute-start | bytes 1572872 | tf_op jit(solution)/shard_map/ppermute | solution.py:308
  36.9 5.5 %collective-permute-start = (bf16[4,128,512]{2,1,0:T(8,128)(2,1)S(1)}, bf16[4,128,512]{2,1,0:T(8,128)(2,1)S(1)}, u32[]{:S(2)}, u32[]{:S(2)}) collective-permute-start(bf16[4,128,512]{2,1,0:T(8,128)(2,1)S(1)} %get-tuple-element.33.refs_0_), channel_id=1, source_target_pairs={{0,8},{8,0},{16,24},{24,16},{1,9},{9,1},{17,25},{25,17},{2,10},{10... | collective-permute-start | bytes 1572872 | tf_op jit(solution)/shard_map/ppermute | solution.py:308
  36.9 5.5 %collective-permute-start.12 = (bf16[4,128,512]{2,1,0:T(8,128)(2,1)S(1)}, bf16[4,128,512]{2,1,0:T(8,128)(2,1)S(1)}, u32[]{:S(2)}, u32[]{:S(2)}) collective-permute-start(bf16[4,128,512]{2,1,0:T(8,128)(2,1)S(1)} %collective-permute-done.10.refs_2_.refs_6_), channel_id=1, source_target_pairs={{0,8},{8,0},{16,24},{24,16},{1,9},{9,1},{17,25},{25,17},{2,10},{10... | collective-permute-start | bytes 1572872 | tf_op jit(solution)/shard_map/ppermute | solution.py:308
  37.4 10.4 %collective-permute-start.13 = (bf16[512,256]{1,0:T(8,128)(2,1)}, bf16[512,256]{1,0:T(8,128)(2,1)S(1)}, u32[]{:S(2)}, u32[]{:S(2)}) collective-permute-start(bf16[512,256]{1,0:T(8,128)(2,1)} %collective-permute-done.6.refs_9_), channel_id=1, source_target_pairs={{0,2},{1,3},{2,4},{3,5},{4,6},{5,7},{6,0},{7,1},{8,10},{9,11},{10,... | collective-permute-start | bytes 786440 | tf_op jit(solution)/shard_map/ppermute | solution.py:317
  40.3 12.5 %collective-permute-start.18 = (f32[256,256]{1,0:T(8,128)S(1)}, f32[256,256]{1,0:T(8,128)S(1)}, u32[]{:S(2)}, u32[]{:S(2)}) collective-permute-start(f32[256,256]{1,0:T(8,128)S(1)} %get-tuple-element.42.refs_8_), channel_id=1, source_target_pairs={{0,1},{1,0},{2,3},{3,2},{4,5},{5,4},{6,7},{7,6},{8,9},{9,8},{10,11... | collective-permute-start | bytes 786440 | tf_op jit(solution)/shard_map/ppermute | solution.py:314
  40.7 12.2 %collective-permute-start.19 = (f32[256,256]{1,0:T(8,128)S(1)}, f32[256,256]{1,0:T(8,128)S(1)}, u32[]{:S(2)}, u32[]{:S(2)}) collective-permute-start(f32[256,256]{1,0:T(8,128)S(1)} %get-tuple-element.52), channel_id=1, source_target_pairs={{0,16},{8,24},{16,0},{24,8},{1,17},{9,25},{17,1},{25,9},{2,18},{10... | collective-permute-start | bytes 786440 | tf_op jit(solution)/shard_map/ppermute | solution.py:311
  43.7 12.4 %collective-permute-start.20 = (f32[256,256]{1,0:T(8,128)S(1)}, f32[256,256]{1,0:T(8,128)S(1)}, u32[]{:S(2)}, u32[]{:S(2)}) collective-permute-start(f32[256,256]{1,0:T(8,128)S(1)} %get-tuple-element.53), channel_id=1, source_target_pairs={{0,17},{1,16},{2,19},{3,18},{4,21},{5,20},{6,23},{7,22},{8,25},{9,... | collective-permute-start | bytes 786440 | tf_op jit(solution)/shard_map/ppermute | solution.py:323
  48.8 9.2 %collective-permute-start.14 = (bf16[256,256]{1,0:T(8,128)(2,1)S(1)}, bf16[256,256]{1,0:T(8,128)(2,1)S(1)}, u32[]{:S(2)}, u32[]{:S(2)}) collective-permute-start(bf16[256,256]{1,0:T(8,128)(2,1)S(1)} %get-tuple-element.49), channel_id=1, source_target_pairs={{0,1},{1,0},{2,3},{3,2},{4,5},{5,4},{6,7},{7,6},{8,9},{9,8},{10,11... | collective-permute-start | bytes 393224 | tf_op jit(solution)/shard_map/ppermute | solution.py:314
  51.3 9.8 %collective-permute-start.15 = (bf16[256,256]{1,0:T(8,128)(2,1)S(1)}, bf16[256,256]{1,0:T(8,128)(2,1)S(1)}, u32[]{:S(2)}, u32[]{:S(2)}) collective-permute-start(bf16[256,256]{1,0:T(8,128)(2,1)S(1)} %get-tuple-element.50), channel_id=1, source_target_pairs={{0,16},{8,24},{16,0},{24,8},{1,17},{9,25},{17,1},{25,9},{2,18},{10... | collective-permute-start | bytes 393224 | tf_op jit(solution)/shard_map/ppermute | solution.py:311
  52.8 8.3 %collective-permute-start.16 = (bf16[256,256]{1,0:T(8,128)(2,1)S(1)}, bf16[256,256]{1,0:T(8,128)(2,1)S(1)}, u32[]{:S(2)}, u32[]{:S(2)}) collective-permute-start(bf16[256,256]{1,0:T(8,128)(2,1)S(1)} %get-tuple-element.51), channel_id=1, source_target_pairs={{0,17},{1,16},{2,19},{3,18},{4,21},{5,20},{6,23},{7,22},{8,25},{9,... | collective-permute-start | bytes 393224 | tf_op jit(solution)/shard_map/ppermute | solution.py:323
  56.2 7.6 %collective-permute-start.21 = (bf16[256,256]{1,0:T(8,128)(2,1)S(1)}, bf16[256,256]{1,0:T(8,128)(2,1)S(1)}, u32[]{:S(2)}, u32[]{:S(2)}) collective-permute-start(bf16[256,256]{1,0:T(8,128)(2,1)S(1)} %shard_map.83.refs_0_), channel_id=1, source_target_pairs={{0,16},{8,24},{16,0},{24,8},{1,17},{9,25},{17,1},{25,9},{2,18},{10... | collective-permute-start | bytes 393224 | tf_op jit(solution)/shard_map/ppermute | solution.py:326
  61.2 5.4 %collective-permute-start.17 = (bf16[256,256]{1,0:T(8,128)(2,1)S(1)}, bf16[256,256]{1,0:T(8,128)(2,1)S(1)}, u32[]{:S(2)}, u32[]{:S(2)}) collective-permute-start(bf16[256,256]{1,0:T(8,128)(2,1)S(1)} %shard_map.82.refs_4_), channel_id=1, source_target_pairs={{0,16},{8,24},{16,0},{24,8},{1,17},{9,25},{17,1},{25,9},{2,18},{10... | collective-permute-start | bytes 393224 | tf_op jit(solution)/shard_map/ppermute | solution.py:326
  62.3 4.7 %collective-permute-start.22 = (bf16[256,256]{1,0:T(8,128)(2,1)S(1)}, bf16[256,256]{1,0:T(8,128)(2,1)S(1)}, u32[]{:S(2)}, u32[]{:S(2)}) collective-permute-start(bf16[256,256]{1,0:T(8,128)(2,1)S(1)} %shard_map.83.refs_0_), channel_id=1, source_target_pairs={{0,8},{8,0},{16,24},{24,16},{1,9},{9,1},{17,25},{25,17},{2,10},{10... | collective-permute-start | bytes 393224 | tf_op jit(solution)/shard_map/ppermute | solution.py:308
  63.9 3.1 %collective-permute-start.23 = (bf16[256,256]{1,0:T(8,128)(2,1)S(1)}, bf16[256,256]{1,0:T(8,128)(2,1)S(1)}, u32[]{:S(2)}, u32[]{:S(2)}) collective-permute-start(bf16[256,256]{1,0:T(8,128)(2,1)S(1)} %collective-permute-done.21.refs_1_), channel_id=1, source_target_pairs={{0,8},{8,0},{16,24},{24,16},{1,9},{9,1},{17,25},{25,17},{2,10},{10... | collective-permute-start | bytes 393224 | tf_op jit(solution)/shard_map/ppermute | solution.py:308
  66.5 1.9 %collective-permute-start.24 = (bf16[256,256]{1,0:T(8,128)(2,1)S(1)}, bf16[256,256]{1,0:T(8,128)(2,1)S(1)}, u32[]{:S(2)}, u32[]{:S(2)}) collective-permute-start(bf16[256,256]{1,0:T(8,128)(2,1)S(1)} %shard_map.82.refs_4_), channel_id=1, source_target_pairs={{0,8},{8,0},{16,24},{24,16},{1,9},{9,1},{17,25},{25,17},{2,10},{10... | collective-permute-start | bytes 393224 | tf_op jit(solution)/shard_map/ppermute | solution.py:308
  66.5 1.9 %collective-permute-start.25 = (bf16[256,256]{1,0:T(8,128)(2,1)S(1)}, bf16[256,256]{1,0:T(8,128)(2,1)S(1)}, u32[]{:S(2)}, u32[]{:S(2)}) collective-permute-start(bf16[256,256]{1,0:T(8,128)(2,1)S(1)} %collective-permute-done.17.refs_5_), channel_id=1, source_target_pairs={{0,8},{8,0},{16,24},{24,16},{1,9},{9,1},{17,25},{25,17},{2,10},{10... | collective-permute-start | bytes 393224 | tf_op jit(solution)/shard_map/ppermute | solution.py:308

commit v5 on v4

--- a/solution.py
+++ b/solution.py
@@ -101,7 +101,7 @@
         out_shape=(jax.ShapeDtypeStruct(shape, jnp.bfloat16),) * 4,
         in_specs=[SMEM, VMEM] + [ANY] * len(after),
         out_specs=(VMEM,) * 4,
-        compiler_params=params(4 * tokens.size),
+        compiler_params=pltpu.CompilerParams(vmem_limit_bytes=52 * 1024 * 1024),
         cost_estimate=cost(0, 4 * tokens.size),
     )(where, tokens, *after)
 
@@ -325,6 +325,9 @@
     def from_chip(array, step):
         return lax.ppermute(array, "ctx", [(i, (i + 2 * step) % n_ctx) for i in range(n_ctx)])
 
+    def spread_out(arrays):
+        return over_x(arrays[1]), over_y(arrays[2]), over_xy(arrays[3])
+
     up = n_line // 2
 
     def gather_pieces(own, late, after):
@@ -375,7 +378,7 @@
         out_specs=VMEM,
         compiler_params=params(16 * chip_rows * tok_rows),
         cost_estimate=cost(20 * n_chips * chip_rows * tok_rows, 0),
-    )(where, block_lists[0], key_pieces[up])
+    )(where, block_lists[0], key_pieces[1])
 
     held[1:3] = lax.optimization_barrier((*held[1:3], key_pieces[up], value_pieces[1], query_rot, bias, cosine, sine_part))[:2]
     f32, bf16 = jnp.float32, jnp.bfloat16
@@ -396,8 +399,7 @@
         compiler_params=params(26 * key_parts[0].size),
         cost_estimate=cost(6 * key_parts[0].size, 26 * key_parts[0].size),
     )(
-        key_parts[0], over_x(key_parts[1]), over_y(key_parts[2]), over_xy(key_parts[3]),
-        cosine, sine_part,
+        key_parts[0], *spread_out(key_parts), cosine, sine_part,
     )
     keys = [key_here] + [from_chip(key_here, j) for j in range(1, n_chips)]
     keys_other = [over_core(array) for array in keys]
@@ -412,7 +414,7 @@
         out_specs=VMEM,
         compiler_params=params(10 * value_parts[0].size),
         cost_estimate=cost(3 * value_parts[0].size, 10 * value_parts[0].size),
-    )(value_parts[0], over_x(value_parts[1]), over_y(value_parts[2]), over_xy(value_parts[3]))
+    )(value_parts[0], *spread_out(value_parts))
     weights, totals = weigh(query_rot, bias, keys, 0, group)
     values = [value_here] + [from_chip(value_here, j) for j in range(1, n_chips)]
     *values, weights = lax.optimization_barrier((*values, weights))

time: 70.9 us -> 70.5 us (level)
  local copies, waits for them, and re-layouts: 4.17 us -> 2.57 us
  other arithmetic: 2.09 us -> 3.39 us
  Pallas kernels: 15.1 us -> 16.4 us
  starting transfers between devices: 26.1 us -> 25.2 us
    ppermute x6, waiting for transfers between devices: 10.2 us -> 5.31 us  [over_z(): lax.ppermute(array, 'dp', [(i, (i + 2 * step) % n_dp) for i in range(n_dp)])]
    ppermute x3, starting transfers between devices: 4.6 us -> 2.47 us  [over_x(): return lax.ppermute(array, 'dp', [(i, i ^ 1) for i in range(n_dp)])]
    ppermute x3, waiting for transfers between devices: 3.14 us -> 5.22 us  [over_xy(): return lax.ppermute(array, ('ctx', 'dp'), pairs)]
    ppermute x3, waiting for transfers between devices: 4.41 us -> 6.05 us  [over_y(): return lax.ppermute(array, 'ctx', [(i, i ^ 2) for i in range(n_ctx)])]
    unnamed x18 -> x12, local copies, waits for them, and re-layouts: 4.06 us -> 2.46 us
    ppermute x3, starting transfers between devices: 4.22 us -> 5.47 us  [over_xy(): return lax.ppermute(array, ('ctx', 'dp'), pairs)]
    pallas_call x1, Pallas kernels: 1.68 us -> 2.92 us  [cut_tokens(): pl.pallas_call(functools.partial(cut_tokens_kernel, n_line), out_shape=(j...]
  transfers between devices with their start and end apart: 26 -> 26, of which waited for: 12 -> 13; matrix products, arithmetic and copies ran while one was open for 3% -> 5% of each run, Pallas kernels for 18% -> 19%
where the time goes in v5:
time: 70.5 us; the launch traced here: 70.2 us
  starting transfers between devices  25.2 us (36%)
  waiting for transfers between devices  22.4 us (32%)
  Pallas kernels  16.4 us (23%)
  other arithmetic  3.39 us (5%)
  local copies, waits for them, and re-layouts  2.57 us (4%)
    ppermute x6, starting transfers between devices, over_z(): lax.ppermute(array, 'dp', [(i, (i + 2 * step) % n_dp) for i in range(n_dp)])  9.23 us
    ppermute x3, waiting for transfers between devices, over_y(): return lax.ppermute(array, 'ctx', [(i, i ^ 2) for i in range(n_ctx)])  6.05 us
    pallas_call x4, Pallas kernels, project(): pl.pallas_call(functools.partial(project_kernel, n_sets, lines, bool(star...  5.47 us
    ppermute x3, starting transfers between devices, over_xy(): return lax.ppermute(array, ('ctx', 'dp'), pairs)  5.47 us
    ppermute x6, waiting for transfers between devices, over_z(): lax.ppermute(array, 'dp', [(i, (i + 2 * step) % n_dp) for i in range(n_dp)])  5.31 us
    ppermute x3, waiting for transfers between devices, over_xy(): return lax.ppermute(array, ('ctx', 'dp'), pairs)  5.22 us
    ppermute x3, starting transfers between devices, over_y(): return lax.ppermute(array, 'ctx', [(i, i ^ 2) for i in range(n_ctx)])  5.08 us
    ppermute x2, waiting for transfers between devices, from_chip(): lax.ppermute(array, 'ctx', [(i, (i + 2 * step) % n_ctx) for i in range(n_...  3.14 us
  transfers between devices with their start and end apart: 26, of which 13 were waited for; matrix products, arithmetic and copies ran while one was open for 5% of the time, Pallas kernels for 19%

profile of v5, /device:TPU:0, one launch (start us, length us, event | category | flops | bytes accessed | tf_op | source)
XLA Modules:
  0.0 70.2 jit_solution(9095261169733828217)
XLA Ops:
  0.0 0.1 stack.26.where
  0.1 1.2 %copy-done = bf16[1024,512]{1,0:T(8,128)(2,1)S(1)} copy-done((bf16[1024,512]{1,0:T(8,128)(2,1)S(1)}, bf16[1024,512]{1,0:T(8,128)(2,1)}, u32[]{:S(2)}) %copy-start) | copy-done | bytes 1048600
  1.3 0.6 shard_map.73.refs_0_.refs_4_
  1.9 3.1 %collective-permute-start.3 = (bf16[512,256]{1,0:T(8,128)(2,1)S(1)}, bf16[512,256]{1,0:T(8,128)(2,1)S(1)}, u32[]{:S(2)}, u32[]{:S(2)}) collective-permute-start(bf16[512,256]{1,0:T(8,128)(2,1)S(1)} %shard_map.73.refs_0_.refs_4_), channel_id=1, source_target_pairs={{0,2},{1,3},{2,4},{3,5},{4,6},{5,7},{6,0},{7,1},{8,10},{9,11},{10,... | collective-permute-start | bytes 786440 | tf_op jit(solution)/shard_map/ppermute | solution.py:317
  5.0 2.1 %collective-permute-start.4 = (bf16[512,256]{1,0:T(8,128)(2,1)S(1)}, bf16[512,256]{1,0:T(8,128)(2,1)S(1)}, u32[]{:S(2)}, u32[]{:S(2)}) collective-permute-start(bf16[512,256]{1,0:T(8,128)(2,1)S(1)} %shard_map.73.refs_0_.refs_4_), channel_id=1, source_target_pairs={{0,6},{1,7},{2,0},{3,1},{4,2},{5,3},{6,4},{7,5},{8,14},{9,15},{10,... | collective-permute-start | bytes 786440 | tf_op jit(solution)/shard_map/ppermute | solution.py:317
  7.1 2.9 %shard_map.74 = (bf16[4,128,512]{2,1,0:T(8,128)(2,1)S(1)}, bf16[4,128,512]{2,1,0:T(8,128)(2,1)}, bf16[4,128,512]{2,1,0:T(8,128)(2,1)}, bf16[4,128,512]{2,1,0:T(8,128)(2,1)}) custom-call(s32[5]{0:T(128)S(1)} %stack.26.where, bf16[128,8192]{1,0:T(8,128)(2,1)} %bitcast.13, bf16[512,256]{1,0:T(8,128)(2,1)S(1)} %shard_map.73.refs_0_.refs_4_), custom_call_target="tpu_custom_call" | custom-call | bytes 4194304 | tf_op jit(solution)/shard_map/pallas_call | solution.py:99
  10.0 1.6 %collective-permute-start.1 = (bf16[4,128,512]{2,1,0:T(8,128)(2,1)}, bf16[4,128,512]{2,1,0:T(8,128)(2,1)S(1)}, u32[]{:S(2)}, u32[]{:S(2)}) collective-permute-start(bf16[4,128,512]{2,1,0:T(8,128)(2,1)} %get-tuple-element.34), channel_id=1, source_target_pairs={{0,1},{1,0},{2,3},{3,2},{4,5},{5,4},{6,7},{7,6},{8,9},{9,8},{10,11... | collective-permute-start | bytes 1572872 | tf_op jit(solution)/shard_map/ppermute | solution.py:314
  11.6 1.5 %collective-permute-start.2 = (bf16[4,128,512]{2,1,0:T(8,128)(2,1)}, bf16[4,128,512]{2,1,0:T(8,128)(2,1)S(1)}, u32[]{:S(2)}, u32[]{:S(2)}) collective-permute-start(bf16[4,128,512]{2,1,0:T(8,128)(2,1)} %get-tuple-element.35), channel_id=1, source_target_pairs={{0,16},{8,24},{16,0},{24,8},{1,17},{9,25},{17,1},{25,9},{2,18},{10... | collective-permute-start | bytes 1572872 | tf_op jit(solution)/shard_map/ppermute | solution.py:311
  13.1 0.6 shard_map.75.refs_8_
  13.7 0.1 collective-permute-start.6
  13.8 0.4 collective-permute-done.3.after_ref.refs_0_.refs_5_
  14.2 0.0 collective-permute-start.7
  14.2 4.4 %collective-permute-done.4.refs_7_ = bf16[512,256]{1,0:T(8,128)(2,1)S(1)} collective-permute-done((bf16[512,256]{1,0:T(8,128)(2,1)S(1)}, bf16[512,256]{1,0:T(8,128)(2,1)S(1)}, u32[]{:S(2)}, u32[]{:S(2)}) %collective-permute-start.4) | collective-permute-done | bytes 262176 | tf_op jit(solution)/shard_map/ppermute | solution.py:317
  18.6 2.7 %collective-permute-start.10 = (bf16[4,128,512]{2,1,0:T(8,128)(2,1)}, bf16[4,128,512]{2,1,0:T(8,128)(2,1)S(1)}, u32[]{:S(2)}, u32[]{:S(2)}) collective-permute-start(bf16[4,128,512]{2,1,0:T(8,128)(2,1)} %get-tuple-element.40), channel_id=1, source_target_pairs={{0,17},{1,16},{2,19},{3,18},{4,21},{5,20},{6,23},{7,22},{8,25},{9,... | collective-permute-start | bytes 1572872 | tf_op jit(solution)/shard_map/ppermute | solution.py:323
  21.3 0.7 shard_map.77.refs_8_.bias_ref
  21.9 0.0 collective-permute-done.7
  22.0 1.7 %collective-permute-start.5 = (bf16[512,256]{1,0:T(8,128)(2,1)S(1)}, bf16[512,256]{1,0:T(8,128)(2,1)S(1)}, u32[]{:S(2)}, u32[]{:S(2)}) collective-permute-start(bf16[512,256]{1,0:T(8,128)(2,1)S(1)} %collective-permute-done.3.after_ref.refs_0_.refs_5_), channel_id=1, source_target_pairs={{0,2},{1,3},{2,4},{3,5},{4,6},{5,7},{6,0},{7,1},{8,10},{9,11},{10,... | collective-permute-start | bytes 786440 | tf_op jit(solution)/shard_map/ppermute | solution.py:317
  23.8 0.6 select_bitcast_fusion
  24.4 2.5 %fusion.3 = (f32[256,64]{1,0:T(8,128)S(1)}, f32[256,64]{1,0:T(8,128)S(1)}, f32[256,64]{1,0:T(8,128)S(1)}) fusion(f32[64]{0:T(128)} %constant.72, s32[64]{0:T(128)} %constant.68, s32[256]{0:T(256)S(1)} %select_bitcast_fusion), kind=kLoop, calls=%fused_computation.7 | loop fusion | flops 163840 | bytes 198144 | tf_op jit(solution)/shard_map/sin | solution.py:48
  26.9 2.2 %collective-permute-start.11 = (bf16[512,256]{1,0:T(8,128)(2,1)S(1)}, bf16[512,256]{1,0:T(8,128)(2,1)S(1)}, u32[]{:S(2)}, u32[]{:S(2)}) collective-permute-start(bf16[512,256]{1,0:T(8,128)(2,1)S(1)} %shard_map.75.refs_8_), channel_id=1, source_target_pairs={{0,6},{1,7},{2,0},{3,1},{4,2},{5,3},{6,4},{7,5},{8,14},{9,15},{10,... | collective-permute-start | bytes 786440 | tf_op jit(solution)/shard_map/ppermute | solution.py:317
  29.1 0.1 fusion.6
  29.2 0.0 copy-start.2
  29.2 1.2 %copy-done.2 = bf16[1,128,4096]{2,1,0:T(8,128)(2,1)S(1)} copy-done((bf16[1,128,4096]{2,1,0:T(8,128)(2,1)S(1)}, bf16[1,128,4096]{2,1,0:T(8,128)(2,1)}, u32[]{:S(2)}) %copy-start.2) | copy-done | bytes 1048600
  30.4 1.1 %shard_map.76.q_ref = bf16[32,128,128]{2,1,0:T(8,128)(2,1)S(1)} custom-call(s32[5]{0:T(128)S(1)} %stack.26.where, bf16[128,4096]{1,0:T(8,128)(2,1)S(1)} %bitcast.11, f32[128,128]{1,0:T(8,128)S(1)} %get-tuple-element.65.cosine_ref, f32[128,128]{1,0:T(8,128)S(1)} %get-tuple-element.64.sine_ref, ...), custom_call_target="tpu_custom_call" | custom-call | flops 1572864 | bytes 2097152 | tf_op jit(solution)/shard_map/pallas_call | solution.py:364
  31.5 0.1 pad_maximum_fusion
  31.7 4.3 %collective-permute-done.2.refs_2_.refs_4_ = bf16[4,128,512]{2,1,0:T(8,128)(2,1)S(1)} collective-permute-done((bf16[4,128,512]{2,1,0:T(8,128)(2,1)}, bf16[4,128,512]{2,1,0:T(8,128)(2,1)S(1)}, u32[]{:S(2)}, u32[]{:S(2)}) %collective-permute-start.2) | collective-permute-done | bytes 524320 | tf_op jit(solution)/shard_map/ppermute | solution.py:311
  36.0 0.5 collective-permute-start.9
  36.5 0.0 collective-permute-start
  36.5 0.0 collective-permute-done.11.refs_10_
  36.6 0.0 collective-permute-done.10.refs_2_.refs_6_
  36.6 0.5 collective-permute-start.12
  37.1 0.1 collective-permute-start.13
  37.1 0.8 %collective-permute-done.8.refs_1_.refs_3_ = bf16[4,128,512]{2,1,0:T(8,128)(2,1)S(1)} collective-permute-done((bf16[4,128,512]{2,1,0:T(8,128)(2,1)S(1)}, bf16[4,128,512]{2,1,0:T(8,128)(2,1)S(1)}, u32[]{:S(2)}, u32[]{:S(2)}) %collective-permute-start.8) | collective-permute-done | bytes 524320 | tf_op jit(solution)/shard_map/ppermute | solution.py:308
  37.9 0.7 %collective-permute-done.9.refs_3_.refs_5_ = bf16[4,128,512]{2,1,0:T(8,128)(2,1)S(1)} collective-permute-done((bf16[4,128,512]{2,1,0:T(8,128)(2,1)S(1)}, bf16[4,128,512]{2,1,0:T(8,128)(2,1)S(1)}, u32[]{:S(2)}, u32[]{:S(2)}) %collective-permute-start.9) | collective-permute-done | bytes 524320 | tf_op jit(solution)/shard_map/ppermute | solution.py:308
  38.7 1.3 %shard_map.78 = (f32[256,256]{1,0:T(8,128)S(1)}, f32[256,256]{1,0:T(8,128)S(1)}) custom-call(s32[5]{0:T(128)S(1)} %stack.26.where, bf16[4,128,512]{2,1,0:T(8,128)(2,1)S(1)} %collective-permute-done.1.refs_0_.refs_2_, bf16[4,128,512]{2,1,0:T(8,128)(2,1)S(1)} %collective-permute-done.8.refs_1_.refs_3_, ...), custom_call_target="tpu_custom_call" | custom-call | flops 536870912 | bytes 4194304 | tf_op jit(solution)/shard_map/pallas_call | solution.py:141
  39.9 0.1 collective-permute-start.18
  40.0 2.0 %collective-permute-start.19 = (f32[256,256]{1,0:T(8,128)S(1)}, f32[256,256]{1,0:T(8,128)S(1)}, u32[]{:S(2)}, u32[]{:S(2)}) collective-permute-start(f32[256,256]{1,0:T(8,128)S(1)} %get-tuple-element.52), channel_id=1, source_target_pairs={{0,16},{8,24},{16,0},{24,8},{1,17},{9,25},{17,1},{25,9},{2,18},{10... | collective-permute-start | bytes 786440 | tf_op jit(solution)/shard_map/ppermute | solution.py:311
  42.1 0.0 collective-permute-done.refs_1_
  42.1 1.3 %shard_map.79 = (f32[256,256]{1,0:T(8,128)S(1)}, f32[256,256]{1,0:T(8,128)S(1)}) custom-call(s32[5]{0:T(128)S(1)} %stack.26.where, bf16[4,128,512]{2,1,0:T(8,128)(2,1)S(1)} %get-tuple-element.33.refs_0_, bf16[4,128,512]{2,1,0:T(8,128)(2,1)S(1)} %collective-permute-done.refs_1_, bf16[4,128,512]{2,1,0:T(8,128)(2,1)S(1)} %collective-permute-done.10.refs_2_.refs_6_, ...), custom_call_target="tpu_custom_call" | custom-call | flops 536870912 | bytes 4194304 | tf_op jit(solution)/shard_map/pallas_call | solution.py:141
  43.3 1.5 %collective-permute-start.20 = (f32[256,256]{1,0:T(8,128)S(1)}, f32[256,256]{1,0:T(8,128)S(1)}, u32[]{:S(2)}, u32[]{:S(2)}) collective-permute-start(f32[256,256]{1,0:T(8,128)S(1)} %get-tuple-element.53), channel_id=1, source_target_pairs={{0,17},{1,16},{2,19},{3,18},{4,21},{5,20},{6,23},{7,22},{8,25},{9,... | collective-permute-start | bytes 786440 | tf_op jit(solution)/shard_map/ppermute | solution.py:323
  44.8 2.0 %shard_map.80 = (f32[256,256]{1,0:T(8,128)S(1)}, f32[256,256]{1,0:T(8,128)S(1)}, f32[256,256]{1,0:T(8,128)S(1)}, f32[256,256]{1,0:T(8,128)S(1)}) custom-call(s32[5]{0:T(128)S(1)} %stack.26.where, bf16[4,128,512]{2,1,0:T(8,128)(2,1)S(1)} %get-tuple-element.33.refs_0_, bf16[4,128,512]{2,1,0:T(8,128)(2,1)S(1)} %collective-permute-done.refs_1_, ...), custom_call_target="tpu_custom_call" | custom-call | flops 805306368 | bytes 7077888 | tf_op jit(solution)/shard_map/pallas_call | solution.py:141
  46.8 0.5 collective-permute-done.13.refs_8_
  47.3 1.0 %shard_map.81 = (bf16[256,256]{1,0:T(8,128)(2,1)S(1)}, bf16[256,256]{1,0:T(8,128)(2,1)S(1)}, bf16[256,256]{1,0:T(8,128)(2,1)S(1)}, bf16[256,256]{1,0:T(8,128)(2,1)S(1)}) custom-call(s32[5]{0:T(128)S(1)} %stack.26.where, bf16[4,128,512]{2,1,0:T(8,128)(2,1)S(1)} %get-tuple-element.33.refs_0_, bf16[4,128,512]{2,1,0:T(8,128)(2,1)S(1)} %collective-permute-done.refs_1_, ...), custom_call_target="tpu_custom_call" | custom-call | flops 268435456 | bytes 6553600 | tf_op jit(solution)/shard_map/pallas_call | solution.py:141
  48.3 0.8 %collective-permute-start.14 = (bf16[256,256]{1,0:T(8,128)(2,1)S(1)}, bf16[256,256]{1,0:T(8,128)(2,1)S(1)}, u32[]{:S(2)}, u32[]{:S(2)}) collective-permute-start(bf16[256,256]{1,0:T(8,128)(2,1)S(1)} %get-tuple-element.49), channel_id=1, source_target_pairs={{0,1},{1,0},{2,3},{3,2},{4,5},{5,4},{6,7},{7,6},{8,9},{9,8},{10,11... | collective-permute-start | bytes 393224 | tf_op jit(solution)/shard_map/ppermute | solution.py:314
  49.1 1.5 %collective-permute-start.15 = (bf16[256,256]{1,0:T(8,128)(2,1)S(1)}, bf16[256,256]{1,0:T(8,128)(2,1)S(1)}, u32[]{:S(2)}, u32[]{:S(2)}) collective-permute-start(bf16[256,256]{1,0:T(8,128)(2,1)S(1)} %get-tuple-element.50), channel_id=1, source_target_pairs={{0,16},{8,24},{16,0},{24,8},{1,17},{9,25},{17,1},{25,9},{2,18},{10... | collective-permute-start | bytes 393224 | tf_op jit(solution)/shard_map/ppermute | solution.py:311
  50.6 0.0 collective-permute-done.18.x_ref
  50.6 1.3 %collective-permute-start.16 = (bf16[256,256]{1,0:T(8,128)(2,1)S(1)}, bf16[256,256]{1,0:T(8,128)(2,1)S(1)}, u32[]{:S(2)}, u32[]{:S(2)}) collective-permute-start(bf16[256,256]{1,0:T(8,128)(2,1)S(1)} %get-tuple-element.51), channel_id=1, source_target_pairs={{0,17},{1,16},{2,19},{3,18},{4,21},{5,20},{6,23},{7,22},{8,25},{9,... | collective-permute-start | bytes 393224 | tf_op jit(solution)/shard_map/ppermute | solution.py:323
  51.9 0.7 %collective-permute-done.19.y_ref = f32[256,256]{1,0:T(8,128)S(1)} collective-permute-done((f32[256,256]{1,0:T(8,128)S(1)}, f32[256,256]{1,0:T(8,128)S(1)}, u32[]{:S(2)}, u32[]{:S(2)}) %collective-permute-start.19) | collective-permute-done | bytes 262176 | tf_op jit(solution)/shard_map/ppermute | solution.py:311
  52.6 3.2 %collective-permute-done.20.xy_ref = f32[256,256]{1,0:T(8,128)S(1)} collective-permute-done((f32[256,256]{1,0:T(8,128)S(1)}, f32[256,256]{1,0:T(8,128)S(1)}, u32[]{:S(2)}, u32[]{:S(2)}) %collective-permute-start.20) | collective-permute-done | bytes 262176 | tf_op jit(solution)/shard_map/ppermute | solution.py:323
  55.8 0.2 shard_map.83.refs_0_
  55.9 0.6 collective-permute-start.21
  56.5 1.1 %collective-permute-done.14.x_ref = bf16[256,256]{1,0:T(8,128)(2,1)S(1)} collective-permute-done((bf16[256,256]{1,0:T(8,128)(2,1)S(1)}, bf16[256,256]{1,0:T(8,128)(2,1)S(1)}, u32[]{:S(2)}, u32[]{:S(2)}) %collective-permute-start.14) | collective-permute-done | bytes 131104 | tf_op jit(solution)/shard_map/ppermute | solution.py:314
  57.6 1.0 %collective-permute-done.15.y_ref = bf16[256,256]{1,0:T(8,128)(2,1)S(1)} collective-permute-done((bf16[256,256]{1,0:T(8,128)(2,1)S(1)}, bf16[256,256]{1,0:T(8,128)(2,1)S(1)}, u32[]{:S(2)}, u32[]{:S(2)}) %collective-permute-start.15) | collective-permute-done | bytes 131104 | tf_op jit(solution)/shard_map/ppermute | solution.py:311
  58.7 2.1 %collective-permute-done.16.xy_ref = bf16[256,256]{1,0:T(8,128)(2,1)S(1)} collective-permute-done((bf16[256,256]{1,0:T(8,128)(2,1)S(1)}, bf16[256,256]{1,0:T(8,128)(2,1)S(1)}, u32[]{:S(2)}, u32[]{:S(2)}) %collective-permute-start.16) | collective-permute-done | bytes 131104 | tf_op jit(solution)/shard_map/ppermute | solution.py:323
  60.7 0.1 shard_map.82.refs_4_
  60.8 0.9 %collective-permute-start.17 = (bf16[256,256]{1,0:T(8,128)(2,1)S(1)}, bf16[256,256]{1,0:T(8,128)(2,1)S(1)}, u32[]{:S(2)}, u32[]{:S(2)}) collective-permute-start(bf16[256,256]{1,0:T(8,128)(2,1)S(1)} %shard_map.82.refs_4_), channel_id=1, source_target_pairs={{0,16},{8,24},{16,0},{24,8},{1,17},{9,25},{17,1},{25,9},{2,18},{10... | collective-permute-start | bytes 393224 | tf_op jit(solution)/shard_map/ppermute | solution.py:326
  61.7 1.9 %collective-permute-done.21.refs_1_ = bf16[256,256]{1,0:T(8,128)(2,1)S(1)} collective-permute-done((bf16[256,256]{1,0:T(8,128)(2,1)S(1)}, bf16[256,256]{1,0:T(8,128)(2,1)S(1)}, u32[]{:S(2)}, u32[]{:S(2)}) %collective-permute-start.21) | collective-permute-done | bytes 131104 | tf_op jit(solution)/shard_map/ppermute | solution.py:326
  63.6 0.0 collective-permute-start.23
  63.6 1.4 %shard_map.84 = (bf16[2,512,1024]{2,1,0:T(8,128)(2,1)S(1)}, f32[2,1,1024]{2,1,0:T(1,128)S(1)}) custom-call(bf16[32,128,128]{2,1,0:T(8,128)(2,1)S(1)} %shard_map.76.q_ref, bf16[512,128]{1,0:T(8,128)(2,1)S(1)} %shard_map.77.refs_8_.bias_ref, bf16[256,256]{1,0:T(8,128)(2,1)S(1)} %shard_map.83.refs_0_, bf16[256,256]{1,0:T(8,128)(2,1)S(1)} %collective-permute-done.21.refs_1_), custom_call_target="tpu_custom_call" | custom-call | flops 268435456 | bytes 3801088 | tf_op jit(solution)/shard_map/pallas_call | solution.py:244
  64.9 1.2 %collective-permute-done.17.refs_5_ = bf16[256,256]{1,0:T(8,128)(2,1)S(1)} collective-permute-done((bf16[256,256]{1,0:T(8,128)(2,1)S(1)}, bf16[256,256]{1,0:T(8,128)(2,1)S(1)}, u32[]{:S(2)}, u32[]{:S(2)}) %collective-permute-start.17) | collective-permute-done | bytes 131104 | tf_op jit(solution)/shard_map/ppermute | solution.py:326
  66.2 0.5 collective-permute-start.25
  66.7 0.0 collective-permute-done.22.refs_0_
  66.7 1.3 %shard_map.85 = (bf16[2,512,1024]{2,1,0:T(8,128)(2,1)S(1)}, f32[2,1,1024]{2,1,0:T(1,128)S(1)}) custom-call(bf16[32,128,128]{2,1,0:T(8,128)(2,1)S(1)} %shard_map.76.q_ref, bf16[512,128]{1,0:T(8,128)(2,1)S(1)} %shard_map.77.refs_8_.bias_ref, bf16[256,256]{1,0:T(8,128)(2,1)S(1)} %collective-permute-done.22.refs_0_, ...), custom_call_target="tpu_custom_call" | custom-call | flops 268435456 | bytes 3801088 | tf_op jit(solution)/shard_map/pallas_call | solution.py:244
  68.1 2.2 %shard_map.86 = bf16[128,4096]{1,0:T(8,128)(2,1)} custom-call(s32[5]{0:T(128)S(1)} %stack.26.where, bf16[2,512,1024]{2,1,0:T(8,128)(2,1)S(1)} %get-tuple-element.55.refs_0_, bf16[2,512,1024]{2,1,0:T(8,128)(2,1)S(1)} %get-tuple-element.56.refs_1_, f32[2,1,1024]{2,1,0:T(1,128)S(1)} %get-tuple-element.57.refs_2_, f32[2,1,1024]{2,1,0:T(1,128)S(1)} %get-tuple-element.58.refs_3_, ...), custom_call_target="tpu_custom_call" | custom-call | flops 536870912 | bytes 5242880 | tf_op jit(solution)/shard_map/pallas_call | solution.py:427
  (21 shorter events, 0.1 us)
Async XLA Ops:
  0.1 1.2 %copy-start = (bf16[1024,512]{1,0:T(8,128)(2,1)S(1)}, bf16[1024,512]{1,0:T(8,128)(2,1)}, u32[]{:S(2)}) copy-start(bf16[1024,512]{1,0:T(8,128)(2,1)} %weight_ref.2) | copy-start | bytes 3145732
  1.3 11.8 %copy-start.1 = (bf16[1024,512]{1,0:T(8,128)(2,1)S(1)}, bf16[1024,512]{1,0:T(8,128)(2,1)}, u32[]{:S(2)}) copy-start(bf16[1024,512]{1,0:T(8,128)(2,1)} %weight_ref.3) | copy-start | bytes 3145732
  1.9 12.3 %collective-permute-start.3 = (bf16[512,256]{1,0:T(8,128)(2,1)S(1)}, bf16[512,256]{1,0:T(8,128)(2,1)S(1)}, u32[]{:S(2)}, u32[]{:S(2)}) collective-permute-start(bf16[512,256]{1,0:T(8,128)(2,1)S(1)} %shard_map.73.refs_0_.refs_4_), channel_id=1, source_target_pairs={{0,2},{1,3},{2,4},{3,5},{4,6},{5,7},{6,0},{7,1},{8,10},{9,11},{10,... | collective-permute-start | bytes 786440 | tf_op jit(solution)/shard_map/ppermute | solution.py:317
  5.0 13.6 %collective-permute-start.4 = (bf16[512,256]{1,0:T(8,128)(2,1)S(1)}, bf16[512,256]{1,0:T(8,128)(2,1)S(1)}, u32[]{:S(2)}, u32[]{:S(2)}) collective-permute-start(bf16[512,256]{1,0:T(8,128)(2,1)S(1)} %shard_map.73.refs_0_.refs_4_), channel_id=1, source_target_pairs={{0,6},{1,7},{2,0},{3,1},{4,2},{5,3},{6,4},{7,5},{8,14},{9,15},{10,... | collective-permute-start | bytes 786440 | tf_op jit(solution)/shard_map/ppermute | solution.py:317
  7.1 7.1 %copy-start.4 = (s32[1,128]{1,0:T(1,128)S(1)}, s32[1,128]{1,0:T(1,128)}, u32[]{:S(2)}) copy-start(s32[1,128]{1,0:T(1,128)} %param.11) | copy-start | bytes 1540
  7.1 14.2 %copy-start.3 = (s32[1,2,6]{2,1,0:T(2,128)S(1)}, s32[1,2,6]{2,1,0:T(2,128)}, u32[]{:S(2)}) copy-start(s32[1,2,6]{2,1,0:T(2,128)} %param.12) | copy-start | bytes 148
  10.0 21.7 %collective-permute-start.1 = (bf16[4,128,512]{2,1,0:T(8,128)(2,1)}, bf16[4,128,512]{2,1,0:T(8,128)(2,1)S(1)}, u32[]{:S(2)}, u32[]{:S(2)}) collective-permute-start(bf16[4,128,512]{2,1,0:T(8,128)(2,1)} %get-tuple-element.34), channel_id=1, source_target_pairs={{0,1},{1,0},{2,3},{3,2},{4,5},{5,4},{6,7},{7,6},{8,9},{9,8},{10,11... | collective-permute-start | bytes 1572872 | tf_op jit(solution)/shard_map/ppermute | solution.py:314
  11.6 24.4 %collective-permute-start.2 = (bf16[4,128,512]{2,1,0:T(8,128)(2,1)}, bf16[4,128,512]{2,1,0:T(8,128)(2,1)S(1)}, u32[]{:S(2)}, u32[]{:S(2)}) collective-permute-start(bf16[4,128,512]{2,1,0:T(8,128)(2,1)} %get-tuple-element.35), channel_id=1, source_target_pairs={{0,16},{8,24},{16,0},{24,8},{1,17},{9,25},{17,1},{25,9},{2,18},{10... | collective-permute-start | bytes 1572872 | tf_op jit(solution)/shard_map/ppermute | solution.py:311
  13.7 13.2 %collective-permute-start.6 = (bf16[512,256]{1,0:T(8,128)(2,1)S(1)}, bf16[512,256]{1,0:T(8,128)(2,1)}, u32[]{:S(2)}, u32[]{:S(2)}) collective-permute-start(bf16[512,256]{1,0:T(8,128)(2,1)S(1)} %shard_map.75.refs_8_), channel_id=1, source_target_pairs={{0,2},{1,3},{2,4},{3,5},{4,6},{5,7},{6,0},{7,1},{8,10},{9,11},{10,... | collective-permute-start | bytes 786440 | tf_op jit(solution)/shard_map/ppermute | solution.py:317
  14.2 7.8 %collective-permute-start.7 = (s32[1,128]{1,0:T(1,128)S(1)}, s32[1,128]{1,0:T(1,128)S(1)}, u32[]{:S(2)}, u32[]{:S(2)}) collective-permute-start(s32[1,128]{1,0:T(1,128)S(1)} %copy-done.4), channel_id=1, source_target_pairs={{0,8},{8,0},{16,24},{24,16},{1,9},{9,1},{17,25},{25,17},{2,10},{10... | collective-permute-start | bytes 1544 | tf_op jit(solution)/shard_map/ppermute | solution.py:308
  18.6 18.0 %collective-permute-start.10 = (bf16[4,128,512]{2,1,0:T(8,128)(2,1)}, bf16[4,128,512]{2,1,0:T(8,128)(2,1)S(1)}, u32[]{:S(2)}, u32[]{:S(2)}) collective-permute-start(bf16[4,128,512]{2,1,0:T(8,128)(2,1)} %get-tuple-element.40), channel_id=1, source_target_pairs={{0,17},{1,16},{2,19},{3,18},{4,21},{5,20},{6,23},{7,22},{8,25},{9,... | collective-permute-start | bytes 1572872 | tf_op jit(solution)/shard_map/ppermute | solution.py:323
  22.0 1.8 %copy-start.5 = (s32[1,128]{1,0:T(1,128)}, s32[1,128]{1,0:T(1,128)S(1)}, u32[]{:S(2)}) copy-start(s32[1,128]{1,0:T(1,128)S(1)} %collective-permute-done.7) | copy-start | bytes 1540
  22.0 14.1 %collective-permute-start.5 = (bf16[512,256]{1,0:T(8,128)(2,1)S(1)}, bf16[512,256]{1,0:T(8,128)(2,1)S(1)}, u32[]{:S(2)}, u32[]{:S(2)}) collective-permute-start(bf16[512,256]{1,0:T(8,128)(2,1)S(1)} %collective-permute-done.3.after_ref.refs_0_.refs_5_), channel_id=1, source_target_pairs={{0,2},{1,3},{2,4},{3,5},{4,6},{5,7},{6,0},{7,1},{8,10},{9,11},{10,... | collective-permute-start | bytes 786440 | tf_op jit(solution)/shard_map/ppermute | solution.py:317
  26.9 9.6 %collective-permute-start.11 = (bf16[512,256]{1,0:T(8,128)(2,1)S(1)}, bf16[512,256]{1,0:T(8,128)(2,1)S(1)}, u32[]{:S(2)}, u32[]{:S(2)}) collective-permute-start(bf16[512,256]{1,0:T(8,128)(2,1)S(1)} %shard_map.75.refs_8_), channel_id=1, source_target_pairs={{0,6},{1,7},{2,0},{3,1},{4,2},{5,3},{6,4},{7,5},{8,14},{9,15},{10,... | collective-permute-start | bytes 786440 | tf_op jit(solution)/shard_map/ppermute | solution.py:317
  29.2 1.2 %copy-start.2 = (bf16[1,128,4096]{2,1,0:T(8,128)(2,1)S(1)}, bf16[1,128,4096]{2,1,0:T(8,128)(2,1)}, u32[]{:S(2)}) copy-start(bf16[1,128,4096]{2,1,0:T(8,128)(2,1)} %param.8) | copy-start | bytes 3145732
  36.0 1.9 %collective-permute-start.8 = (bf16[4,128,512]{2,1,0:T(8,128)(2,1)S(1)}, bf16[4,128,512]{2,1,0:T(8,128)(2,1)S(1)}, u32[]{:S(2)}, u32[]{:S(2)}) collective-permute-start(bf16[4,128,512]{2,1,0:T(8,128)(2,1)S(1)} %collective-permute-done.1.refs_0_.refs_2_), channel_id=1, source_target_pairs={{0,8},{8,0},{16,24},{24,16},{1,9},{9,1},{17,25},{25,17},{2,10},{10... | collective-permute-start | bytes 1572872 | tf_op jit(solution)/shard_map/ppermute | solution.py:308
  36.0 2.7 %collective-permute-start.9 = (bf16[4,128,512]{2,1,0:T(8,128)(2,1)S(1)}, bf16[4,128,512]{2,1,0:T(8,128)(2,1)S(1)}, u32[]{:S(2)}, u32[]{:S(2)}) collective-permute-start(bf16[4,128,512]{2,1,0:T(8,128)(2,1)S(1)} %collective-permute-done.2.refs_2_.refs_4_), channel_id=1, source_target_pairs={{0,8},{8,0},{16,24},{24,16},{1,9},{9,1},{17,25},{25,17},{2,10},{10... | collective-permute-start | bytes 1572872 | tf_op jit(solution)/shard_map/ppermute | solution.py:308
  36.5 5.5 %collective-permute-start = (bf16[4,128,512]{2,1,0:T(8,128)(2,1)S(1)}, bf16[4,128,512]{2,1,0:T(8,128)(2,1)S(1)}, u32[]{:S(2)}, u32[]{:S(2)}) collective-permute-start(bf16[4,128,512]{2,1,0:T(8,128)(2,1)S(1)} %get-tuple-element.33.refs_0_), channel_id=1, source_target_pairs={{0,8},{8,0},{16,24},{24,16},{1,9},{9,1},{17,25},{25,17},{2,10},{10... | collective-permute-start | bytes 1572872 | tf_op jit(solution)/shard_map/ppermute | solution.py:308
  36.6 5.5 %collective-permute-start.12 = (bf16[4,128,512]{2,1,0:T(8,128)(2,1)S(1)}, bf16[4,128,512]{2,1,0:T(8,128)(2,1)S(1)}, u32[]{:S(2)}, u32[]{:S(2)}) collective-permute-start(bf16[4,128,512]{2,1,0:T(8,128)(2,1)S(1)} %collective-permute-done.10.refs_2_.refs_6_), channel_id=1, source_target_pairs={{0,8},{8,0},{16,24},{24,16},{1,9},{9,1},{17,25},{25,17},{2,10},{10... | collective-permute-start | bytes 1572872 | tf_op jit(solution)/shard_map/ppermute | solution.py:308
  37.1 10.3 %collective-permute-start.13 = (bf16[512,256]{1,0:T(8,128)(2,1)}, bf16[512,256]{1,0:T(8,128)(2,1)S(1)}, u32[]{:S(2)}, u32[]{:S(2)}) collective-permute-start(bf16[512,256]{1,0:T(8,128)(2,1)} %collective-permute-done.6.refs_9_), channel_id=1, source_target_pairs={{0,2},{1,3},{2,4},{3,5},{4,6},{5,7},{6,0},{7,1},{8,10},{9,11},{10,... | collective-permute-start | bytes 786440 | tf_op jit(solution)/shard_map/ppermute | solution.py:317
  39.9 10.7 %collective-permute-start.18 = (f32[256,256]{1,0:T(8,128)S(1)}, f32[256,256]{1,0:T(8,128)S(1)}, u32[]{:S(2)}, u32[]{:S(2)}) collective-permute-start(f32[256,256]{1,0:T(8,128)S(1)} %get-tuple-element.42.refs_8_), channel_id=1, source_target_pairs={{0,1},{1,0},{2,3},{3,2},{4,5},{5,4},{6,7},{7,6},{8,9},{9,8},{10,11... | collective-permute-start | bytes 786440 | tf_op jit(solution)/shard_map/ppermute | solution.py:314
  40.0 12.6 %collective-permute-start.19 = (f32[256,256]{1,0:T(8,128)S(1)}, f32[256,256]{1,0:T(8,128)S(1)}, u32[]{:S(2)}, u32[]{:S(2)}) collective-permute-start(f32[256,256]{1,0:T(8,128)S(1)} %get-tuple-element.52), channel_id=1, source_target_pairs={{0,16},{8,24},{16,0},{24,8},{1,17},{9,25},{17,1},{25,9},{2,18},{10... | collective-permute-start | bytes 786440 | tf_op jit(solution)/shard_map/ppermute | solution.py:311
  43.3 12.4 %collective-permute-start.20 = (f32[256,256]{1,0:T(8,128)S(1)}, f32[256,256]{1,0:T(8,128)S(1)}, u32[]{:S(2)}, u32[]{:S(2)}) collective-permute-start(f32[256,256]{1,0:T(8,128)S(1)} %get-tuple-element.53), channel_id=1, source_target_pairs={{0,17},{1,16},{2,19},{3,18},{4,21},{5,20},{6,23},{7,22},{8,25},{9,... | collective-permute-start | bytes 786440 | tf_op jit(solution)/shard_map/ppermute | solution.py:323
  48.3 9.3 %collective-permute-start.14 = (bf16[256,256]{1,0:T(8,128)(2,1)S(1)}, bf16[256,256]{1,0:T(8,128)(2,1)S(1)}, u32[]{:S(2)}, u32[]{:S(2)}) collective-permute-start(bf16[256,256]{1,0:T(8,128)(2,1)S(1)} %get-tuple-element.49), channel_id=1, source_target_pairs={{0,1},{1,0},{2,3},{3,2},{4,5},{5,4},{6,7},{7,6},{8,9},{9,8},{10,11... | collective-permute-start | bytes 393224 | tf_op jit(solution)/shard_map/ppermute | solution.py:314
  49.1 9.6 %collective-permute-start.15 = (bf16[256,256]{1,0:T(8,128)(2,1)S(1)}, bf16[256,256]{1,0:T(8,128)(2,1)S(1)}, u32[]{:S(2)}, u32[]{:S(2)}) collective-permute-start(bf16[256,256]{1,0:T(8,128)(2,1)S(1)} %get-tuple-element.50), channel_id=1, source_target_pairs={{0,16},{8,24},{16,0},{24,8},{1,17},{9,25},{17,1},{25,9},{2,18},{10... | collective-permute-start | bytes 393224 | tf_op jit(solution)/shard_map/ppermute | solution.py:311
  50.6 10.1 %collective-permute-start.16 = (bf16[256,256]{1,0:T(8,128)(2,1)S(1)}, bf16[256,256]{1,0:T(8,128)(2,1)S(1)}, u32[]{:S(2)}, u32[]{:S(2)}) collective-permute-start(bf16[256,256]{1,0:T(8,128)(2,1)S(1)} %get-tuple-element.51), channel_id=1, source_target_pairs={{0,17},{1,16},{2,19},{3,18},{4,21},{5,20},{6,23},{7,22},{8,25},{9,... | collective-permute-start | bytes 393224 | tf_op jit(solution)/shard_map/ppermute | solution.py:323
  55.9 7.6 %collective-permute-start.21 = (bf16[256,256]{1,0:T(8,128)(2,1)S(1)}, bf16[256,256]{1,0:T(8,128)(2,1)S(1)}, u32[]{:S(2)}, u32[]{:S(2)}) collective-permute-start(bf16[256,256]{1,0:T(8,128)(2,1)S(1)} %shard_map.83.refs_0_), channel_id=1, source_target_pairs={{0,16},{8,24},{16,0},{24,8},{1,17},{9,25},{17,1},{25,9},{2,18},{10... | collective-permute-start | bytes 393224 | tf_op jit(solution)/shard_map/ppermute | solution.py:326
  60.8 5.4 %collective-permute-start.17 = (bf16[256,256]{1,0:T(8,128)(2,1)S(1)}, bf16[256,256]{1,0:T(8,128)(2,1)S(1)}, u32[]{:S(2)}, u32[]{:S(2)}) collective-permute-start(bf16[256,256]{1,0:T(8,128)(2,1)S(1)} %shard_map.82.refs_4_), channel_id=1, source_target_pairs={{0,16},{8,24},{16,0},{24,8},{1,17},{9,25},{17,1},{25,9},{2,18},{10... | collective-permute-start | bytes 393224 | tf_op jit(solution)/shard_map/ppermute | solution.py:326
  61.7 5.0 %collective-permute-start.22 = (bf16[256,256]{1,0:T(8,128)(2,1)S(1)}, bf16[256,256]{1,0:T(8,128)(2,1)S(1)}, u32[]{:S(2)}, u32[]{:S(2)}) collective-permute-start(bf16[256,256]{1,0:T(8,128)(2,1)S(1)} %shard_map.83.refs_0_), channel_id=1, source_target_pairs={{0,8},{8,0},{16,24},{24,16},{1,9},{9,1},{17,25},{25,17},{2,10},{10... | collective-permute-start | bytes 393224 | tf_op jit(solution)/shard_map/ppermute | solution.py:308
  63.6 3.1 %collective-permute-start.23 = (bf16[256,256]{1,0:T(8,128)(2,1)S(1)}, bf16[256,256]{1,0:T(8,128)(2,1)S(1)}, u32[]{:S(2)}, u32[]{:S(2)}) collective-permute-start(bf16[256,256]{1,0:T(8,128)(2,1)S(1)} %collective-permute-done.21.refs_1_), channel_id=1, source_target_pairs={{0,8},{8,0},{16,24},{24,16},{1,9},{9,1},{17,25},{25,17},{2,10},{10... | collective-permute-start | bytes 393224 | tf_op jit(solution)/shard_map/ppermute | solution.py:308
  66.2 1.9 %collective-permute-start.24 = (bf16[256,256]{1,0:T(8,128)(2,1)S(1)}, bf16[256,256]{1,0:T(8,128)(2,1)S(1)}, u32[]{:S(2)}, u32[]{:S(2)}) collective-permute-start(bf16[256,256]{1,0:T(8,128)(2,1)S(1)} %shard_map.82.refs_4_), channel_id=1, source_target_pairs={{0,8},{8,0},{16,24},{24,16},{1,9},{9,1},{17,25},{25,17},{2,10},{10... | collective-permute-start | bytes 393224 | tf_op jit(solution)/shard_map/ppermute | solution.py:308
  66.2 1.9 %collective-permute-start.25 = (bf16[256,256]{1,0:T(8,128)(2,1)S(1)}, bf16[256,256]{1,0:T(8,128)(2,1)S(1)}, u32[]{:S(2)}, u32[]{:S(2)}) collective-permute-start(bf16[256,256]{1,0:T(8,128)(2,1)S(1)} %collective-permute-done.17.refs_5_), channel_id=1, source_target_pairs={{0,8},{8,0},{16,24},{24,16},{1,9},{9,1},{17,25},{25,17},{2,10},{10... | collective-permute-start | bytes 393224 | tf_op jit(solution)/shard_map/ppermute | solution.py:308

commit v6 on v5

--- a/solution.py
+++ b/solution.py
@@ -274,20 +274,26 @@
                 axis=0,
             )
             pair = side * heads_here + i
-            mixed = jnp.dot(
-                values.T, weight_refs[side][i], preferred_element_type=jnp.float32
-            ) * (1.0 / total_refs[side][i])
-            for g in range(group):
-                buf[pair, :, g * HD : (g + 1) * HD] = mixed[
-                    :, g * tokens : (g + 1) * tokens
-                ].T.astype(jnp.bfloat16)
-            start = pl.multiple_of((first_head + i) * width, width)
-            copies.append(
-                pltpu.make_async_copy(
-                    buf.at[pair], out_ref.at[:, pl.ds(start, width)], sems.at[pair]
+            columns = values.T
+            step = group // 2
+            for g in range(0, group, step):
+                lanes = slice(g * tokens, (g + step) * tokens)
+                mixed = jnp.dot(
+                    columns, weight_refs[side][i, :, lanes], preferred_element_type=jnp.float32
+                ) * (1.0 / total_refs[side][i, :, lanes])
+                for t in range(step):
+                    buf[pair, :, (g + t) * HD : (g + t + 1) * HD] = mixed[
+                        :, t * tokens : (t + 1) * tokens
+                    ].T.astype(jnp.bfloat16)
+                start = pl.multiple_of((first_head + i) * width + g * HD, step * HD)
+                copies.append(
+                    pltpu.make_async_copy(
+                        buf.at[pair, :, pl.ds(g * HD, step * HD)],
+                        out_ref.at[:, pl.ds(start, step * HD)],
+                        sems.at[pair, g // step],
+                    )
                 )
-            )
-            copies[-1].start()
+                copies[-1].start()
     for copy in copies:
         copy.wait()
 
@@ -326,7 +332,8 @@
         return lax.ppermute(array, "ctx", [(i, (i + 2 * step) % n_ctx) for i in range(n_ctx)])
 
     def spread_out(arrays):
-        return over_x(arrays[1]), over_y(arrays[2]), over_xy(arrays[3])
+        came_y, came_xy = over_y(arrays[2]), over_xy(arrays[3])
+        return over_x(arrays[1]), came_y, came_xy
 
     up = n_line // 2
 
@@ -384,7 +391,8 @@
     f32, bf16 = jnp.float32, jnp.bfloat16
     every = list(range(n_line))
     sets = [(array, over_core(array)) for array in held[:3]]
-    key_x, key_y = project(where, sets[1:], every, key_pieces, None, (f32,), bias, cosine, sine_part)
+    (key_y,) = project(where, sets[2:], every, key_pieces, None, (f32,), bias, cosine, sine_part)
+    (key_x,) = project(where, sets[1:2], every, key_pieces, None, (f32,), key_y)
     *held[3:], _ = lax.optimization_barrier((held[3], held[1], value_pieces[-1]))
     sets.append((held[3], over_core(held[3])))
     key_own_part, key_xy = project(
@@ -431,7 +439,7 @@
         out_specs=ANY,
         scratch_shapes=[
             pltpu.VMEM((pairs, tok_rows, group * HD), bf16),
-            pltpu.SemaphoreType.DMA((pairs,)),
+            pltpu.SemaphoreType.DMA((pairs, 2)),
         ],
         compiler_params=params(held + 4 * span_rows * key_width),
         cost_estimate=cost(2 * tok_rows * query_width * span_rows, held),

time: 70.5 us -> 70.5 us (level)
  Pallas kernels: 16.4 us -> 17.2 us
  waiting for transfers between devices: 22.4 us -> 21.6 us
    ppermute x9, waiting for transfers between devices: 1.57 us -> 0.8 us  [over_core(): return lax.ppermute(array, 'ctx', [(i, i ^ 1) for i in range(n_ctx)])]
    pallas_call x4 -> x5, Pallas kernels: 5.47 us -> 6.22 us  [project(): pl.pallas_call(functools.partial(project_kernel, n_sets, lines, bool(star...]
  transfers between devices with their start and end apart: 26 -> 26, of which waited for: 13 -> 12; matrix products, arithmetic and copies ran while one was open for 5% -> 5% of each run, Pallas kernels for 19% -> 21%
where the time goes in v6:
time: 70.5 us; the launch traced here: 70.2 us
  starting transfers between devices  25.2 us (36%)
  waiting for transfers between devices  21.6 us (31%)
  Pallas kernels  17.2 us (24%)
  other arithmetic  3.42 us (5%)
  local copies, waits for them, and re-layouts  2.57 us (4%)
    ppermute x6, starting transfers between devices, over_z(): lax.ppermute(array, 'dp', [(i, (i + 2 * step) % n_dp) for i in range(n_dp)])  9.25 us
    pallas_call x5, Pallas kernels, project(): pl.pallas_call(functools.partial(project_kernel, n_sets, lines, bool(star...  6.22 us
    ppermute x3, waiting for transfers between devices, over_y(): return lax.ppermute(array, 'ctx', [(i, i ^ 2) for i in range(n_ctx)])  5.98 us
    ppermute x3, starting transfers between devices, over_xy(): return lax.ppermute(array, ('ctx', 'dp'), pairs)  5.46 us
    ppermute x6, waiting for transfers between devices, over_z(): lax.ppermute(array, 'dp', [(i, (i + 2 * step) % n_dp) for i in range(n_dp)])  5.35 us
    ppermute x3, waiting for transfers between devices, over_xy(): return lax.ppermute(array, ('ctx', 'dp'), pairs)  5.24 us
    ppermute x3, starting transfers between devices, over_y(): return lax.ppermute(array, 'ctx', [(i, i ^ 2) for i in range(n_ctx)])  5.08 us
    ppermute x2, waiting for transfers between devices, from_chip(): lax.ppermute(array, 'ctx', [(i, (i + 2 * step) % n_ctx) for i in range(n_...  3.12 us
  transfers between devices with their start and end apart: 26, of which 12 were waited for; matrix products, arithmetic and copies ran while one was open for 5% of the time, Pallas kernels for 21%

profile of v6, /device:TPU:0, one launch (start us, length us, event | category | flops | bytes accessed | tf_op | source)
XLA Modules:
  0.0 70.2 jit_solution(6668234076563304488)
XLA Ops:
  0.0 0.1 stack.26.where
  0.1 1.2 %copy-done = bf16[1024,512]{1,0:T(8,128)(2,1)S(1)} copy-done((bf16[1024,512]{1,0:T(8,128)(2,1)S(1)}, bf16[1024,512]{1,0:T(8,128)(2,1)}, u32[]{:S(2)}) %copy-start) | copy-done | bytes 1048600
  1.3 0.6 shard_map.73.refs_0_.refs_2_.refs_4_
  1.9 3.1 %collective-permute-start.3 = (bf16[512,256]{1,0:T(8,128)(2,1)S(1)}, bf16[512,256]{1,0:T(8,128)(2,1)S(1)}, u32[]{:S(2)}, u32[]{:S(2)}) collective-permute-start(bf16[512,256]{1,0:T(8,128)(2,1)S(1)} %shard_map.73.refs_0_.refs_2_.refs_4_), channel_id=1, source_target_pairs={{0,2},{1,3},{2,4},{3,5},{4,6},{5,7},{6,0},{7,1},{8,10},{9,11},{10,... | collective-permute-start | bytes 786440 | tf_op jit(solution)/shard_map/ppermute | solution.py:323
  5.0 2.1 %collective-permute-start.4 = (bf16[512,256]{1,0:T(8,128)(2,1)S(1)}, bf16[512,256]{1,0:T(8,128)(2,1)S(1)}, u32[]{:S(2)}, u32[]{:S(2)}) collective-permute-start(bf16[512,256]{1,0:T(8,128)(2,1)S(1)} %shard_map.73.refs_0_.refs_2_.refs_4_), channel_id=1, source_target_pairs={{0,6},{1,7},{2,0},{3,1},{4,2},{5,3},{6,4},{7,5},{8,14},{9,15},{10,... | collective-permute-start | bytes 786440 | tf_op jit(solution)/shard_map/ppermute | solution.py:323
  7.1 2.9 %shard_map.74 = (bf16[4,128,512]{2,1,0:T(8,128)(2,1)S(1)}, bf16[4,128,512]{2,1,0:T(8,128)(2,1)}, bf16[4,128,512]{2,1,0:T(8,128)(2,1)}, bf16[4,128,512]{2,1,0:T(8,128)(2,1)}) custom-call(s32[5]{0:T(128)S(1)} %stack.26.where, bf16[128,8192]{1,0:T(8,128)(2,1)} %bitcast.13, bf16[512,256]{1,0:T(8,128)(2,1)S(1)} %shard_map.73.refs_0_.refs_2_.refs_4_), custom_call_target="tpu_custom_call" | custom-call | bytes 4194304 | tf_op jit(solution)/shard_map/pallas_call | solution.py:99
  10.0 1.6 %collective-permute-start.1 = (bf16[4,128,512]{2,1,0:T(8,128)(2,1)}, bf16[4,128,512]{2,1,0:T(8,128)(2,1)S(1)}, u32[]{:S(2)}, u32[]{:S(2)}) collective-permute-start(bf16[4,128,512]{2,1,0:T(8,128)(2,1)} %get-tuple-element.32), channel_id=1, source_target_pairs={{0,1},{1,0},{2,3},{3,2},{4,5},{5,4},{6,7},{7,6},{8,9},{9,8},{10,11... | collective-permute-start | bytes 1572872 | tf_op jit(solution)/shard_map/ppermute | solution.py:320
  11.6 1.5 %collective-permute-start.2 = (bf16[4,128,512]{2,1,0:T(8,128)(2,1)}, bf16[4,128,512]{2,1,0:T(8,128)(2,1)S(1)}, u32[]{:S(2)}, u32[]{:S(2)}) collective-permute-start(bf16[4,128,512]{2,1,0:T(8,128)(2,1)} %get-tuple-element.33), channel_id=1, source_target_pairs={{0,16},{8,24},{16,0},{24,8},{1,17},{9,25},{17,1},{25,9},{2,18},{10... | collective-permute-start | bytes 1572872 | tf_op jit(solution)/shard_map/ppermute | solution.py:317
  13.1 0.6 shard_map.75.refs_8_
  13.7 0.1 collective-permute-start.6
  13.8 0.4 collective-permute-done.3.after_ref.refs_0_.refs_3_.refs_5_
  14.2 0.0 collective-permute-start.7
  14.2 4.4 %collective-permute-done.4.refs_5_.refs_7_ = bf16[512,256]{1,0:T(8,128)(2,1)S(1)} collective-permute-done((bf16[512,256]{1,0:T(8,128)(2,1)S(1)}, bf16[512,256]{1,0:T(8,128)(2,1)S(1)}, u32[]{:S(2)}, u32[]{:S(2)}) %collective-permute-start.4) | collective-permute-done | bytes 262176 | tf_op jit(solution)/shard_map/ppermute | solution.py:323
  18.6 2.7 %collective-permute-start.10 = (bf16[4,128,512]{2,1,0:T(8,128)(2,1)}, bf16[4,128,512]{2,1,0:T(8,128)(2,1)S(1)}, u32[]{:S(2)}, u32[]{:S(2)}) collective-permute-start(bf16[4,128,512]{2,1,0:T(8,128)(2,1)} %get-tuple-element.38), channel_id=1, source_target_pairs={{0,17},{1,16},{2,19},{3,18},{4,21},{5,20},{6,23},{7,22},{8,25},{9,... | collective-permute-start | bytes 1572872 | tf_op jit(solution)/shard_map/ppermute | solution.py:329
  21.3 0.7 shard_map.77.refs_6_.bias_ref
  21.9 0.0 collective-permute-done.7
  22.0 1.7 %collective-permute-start.5 = (bf16[512,256]{1,0:T(8,128)(2,1)S(1)}, bf16[512,256]{1,0:T(8,128)(2,1)S(1)}, u32[]{:S(2)}, u32[]{:S(2)}) collective-permute-start(bf16[512,256]{1,0:T(8,128)(2,1)S(1)} %collective-permute-done.3.after_ref.refs_0_.refs_3_.refs_5_), channel_id=1, source_target_pairs={{0,2},{1,3},{2,4},{3,5},{4,6},{5,7},{6,0},{7,1},{8,10},{9,11},{10,... | collective-permute-start | bytes 786440 | tf_op jit(solution)/shard_map/ppermute | solution.py:323
  23.8 0.7 select_bitcast_fusion
  24.4 2.5 %fusion.3 = (f32[256,64]{1,0:T(8,128)S(1)}, f32[256,64]{1,0:T(8,128)S(1)}, f32[256,64]{1,0:T(8,128)S(1)}) fusion(f32[64]{0:T(128)} %constant.72, s32[64]{0:T(128)} %constant.68, s32[256]{0:T(256)S(1)} %select_bitcast_fusion), kind=kLoop, calls=%fused_computation.7 | loop fusion | flops 163840 | bytes 198144 | tf_op jit(solution)/shard_map/sin | solution.py:48
  26.9 0.0 collective-permute-done.6.refs_9_
  26.9 2.2 %collective-permute-start.11 = (bf16[512,256]{1,0:T(8,128)(2,1)S(1)}, bf16[512,256]{1,0:T(8,128)(2,1)S(1)}, u32[]{:S(2)}, u32[]{:S(2)}) collective-permute-start(bf16[512,256]{1,0:T(8,128)(2,1)S(1)} %shard_map.75.refs_8_), channel_id=1, source_target_pairs={{0,6},{1,7},{2,0},{3,1},{4,2},{5,3},{6,4},{7,5},{8,14},{9,15},{10,... | collective-permute-start | bytes 786440 | tf_op jit(solution)/shard_map/ppermute | solution.py:323
  29.1 0.1 fusion.6
  29.2 0.0 copy-start.2
  29.3 1.2 %copy-done.2 = bf16[1,128,4096]{2,1,0:T(8,128)(2,1)S(1)} copy-done((bf16[1,128,4096]{2,1,0:T(8,128)(2,1)S(1)}, bf16[1,128,4096]{2,1,0:T(8,128)(2,1)}, u32[]{:S(2)}) %copy-start.2) | copy-done | bytes 1048600
  30.5 1.1 %shard_map.76.q_ref = bf16[32,128,128]{2,1,0:T(8,128)(2,1)S(1)} custom-call(s32[5]{0:T(128)S(1)} %stack.26.where, bf16[128,4096]{1,0:T(8,128)(2,1)S(1)} %bitcast.11, f32[128,128]{1,0:T(8,128)S(1)} %get-tuple-element.61.cosine_ref, f32[128,128]{1,0:T(8,128)S(1)} %get-tuple-element.60.sine_ref, ...), custom_call_target="tpu_custom_call" | custom-call | flops 1572864 | bytes 2097152 | tf_op jit(solution)/shard_map/pallas_call | solution.py:371
  31.6 0.1 pad_maximum_fusion
  31.7 0.0 collective-permute-done.1.refs_0_.refs_2_
  31.7 4.3 %collective-permute-done.2.refs_0_.refs_4_ = bf16[4,128,512]{2,1,0:T(8,128)(2,1)S(1)} collective-permute-done((bf16[4,128,512]{2,1,0:T(8,128)(2,1)}, bf16[4,128,512]{2,1,0:T(8,128)(2,1)S(1)}, u32[]{:S(2)}, u32[]{:S(2)}) %collective-permute-start.2) | collective-permute-done | bytes 524320 | tf_op jit(solution)/shard_map/ppermute | solution.py:317
  36.0 0.5 collective-permute-start.8
  36.5 0.0 collective-permute-start
  36.5 0.0 collective-permute-done.11.refs_10_
  36.6 0.0 collective-permute-done.10.refs_2_.refs_6_
  36.6 0.5 collective-permute-start.12
  37.0 0.1 collective-permute-start.13
  37.1 0.8 %collective-permute-done.9.refs_1_.refs_5_ = bf16[4,128,512]{2,1,0:T(8,128)(2,1)S(1)} collective-permute-done((bf16[4,128,512]{2,1,0:T(8,128)(2,1)S(1)}, bf16[4,128,512]{2,1,0:T(8,128)(2,1)S(1)}, u32[]{:S(2)}, u32[]{:S(2)}) %collective-permute-start.9) | collective-permute-done | bytes 524320 | tf_op jit(solution)/shard_map/ppermute | solution.py:314
  37.9 1.0 %shard_map.78.refs_6_ = f32[256,256]{1,0:T(8,128)S(1)} custom-call(s32[5]{0:T(128)S(1)} %stack.26.where, bf16[4,128,512]{2,1,0:T(8,128)(2,1)S(1)} %collective-permute-done.2.refs_0_.refs_4_, bf16[4,128,512]{2,1,0:T(8,128)(2,1)S(1)} %collective-permute-done.9.refs_1_.refs_5_, bf16[512,256]{1,0:T(8,128)(2,1)S(1)} %shard_map.73.refs_0_.refs_2_.refs_4_, ...), custom_call_target="tpu_custom_call" | custom-call | flops 268435456 | bytes 2621440 | tf_op jit(solution)/shard_map/pallas_call | solution.py:141
  38.9 0.0 collective-permute-done.8.refs_1_.refs_3_
  38.9 1.0 %shard_map.79.refs_8_ = f32[256,256]{1,0:T(8,128)S(1)} custom-call(s32[5]{0:T(128)S(1)} %stack.26.where, bf16[4,128,512]{2,1,0:T(8,128)(2,1)S(1)} %collective-permute-done.1.refs_0_.refs_2_, bf16[4,128,512]{2,1,0:T(8,128)(2,1)S(1)} %collective-permute-done.8.refs_1_.refs_3_, bf16[512,256]{1,0:T(8,128)(2,1)S(1)} %shard_map.73.refs_0_.refs_2_.refs_4_, ...), custom_call_target="tpu_custom_call" | custom-call | flops 268435456 | bytes 2621440 | tf_op jit(solution)/shard_map/pallas_call | solution.py:141
  39.9 0.1 collective-permute-start.18
  40.0 2.0 %collective-permute-start.19 = (f32[256,256]{1,0:T(8,128)S(1)}, f32[256,256]{1,0:T(8,128)S(1)}, u32[]{:S(2)}, u32[]{:S(2)}) collective-permute-start(f32[256,256]{1,0:T(8,128)S(1)} %shard_map.78.refs_6_), channel_id=1, source_target_pairs={{0,16},{8,24},{16,0},{24,8},{1,17},{9,25},{17,1},{25,9},{2,18},{10... | collective-permute-start | bytes 786440 | tf_op jit(solution)/shard_map/ppermute | solution.py:317
  42.0 0.0 collective-permute-done.refs_1_
  42.1 1.3 %shard_map.80 = (f32[256,256]{1,0:T(8,128)S(1)}, f32[256,256]{1,0:T(8,128)S(1)}) custom-call(s32[5]{0:T(128)S(1)} %stack.26.where, bf16[4,128,512]{2,1,0:T(8,128)(2,1)S(1)} %get-tuple-element.31.refs_0_, bf16[4,128,512]{2,1,0:T(8,128)(2,1)S(1)} %collective-permute-done.refs_1_, bf16[4,128,512]{2,1,0:T(8,128)(2,1)S(1)} %collective-permute-done.10.refs_2_.refs_6_, ...), custom_call_target="tpu_custom_call" | custom-call | flops 536870912 | bytes 4194304 | tf_op jit(solution)/shard_map/pallas_call | solution.py:141
  43.3 1.5 %collective-permute-start.20 = (f32[256,256]{1,0:T(8,128)S(1)}, f32[256,256]{1,0:T(8,128)S(1)}, u32[]{:S(2)}, u32[]{:S(2)}) collective-permute-start(f32[256,256]{1,0:T(8,128)S(1)} %get-tuple-element.49), channel_id=1, source_target_pairs={{0,17},{1,16},{2,19},{3,18},{4,21},{5,20},{6,23},{7,22},{8,25},{9,... | collective-permute-start | bytes 786440 | tf_op jit(solution)/shard_map/ppermute | solution.py:329
  44.8 2.0 %shard_map.81 = (f32[256,256]{1,0:T(8,128)S(1)}, f32[256,256]{1,0:T(8,128)S(1)}, f32[256,256]{1,0:T(8,128)S(1)}, f32[256,256]{1,0:T(8,128)S(1)}) custom-call(s32[5]{0:T(128)S(1)} %stack.26.where, bf16[4,128,512]{2,1,0:T(8,128)(2,1)S(1)} %get-tuple-element.31.refs_0_, bf16[4,128,512]{2,1,0:T(8,128)(2,1)S(1)} %collective-permute-done.refs_1_, ...), custom_call_target="tpu_custom_call" | custom-call | flops 805306368 | bytes 7077888 | tf_op jit(solution)/shard_map/pallas_call | solution.py:141
  46.8 0.5 collective-permute-done.13.refs_8_
  47.3 1.0 %shard_map.82 = (bf16[256,256]{1,0:T(8,128)(2,1)S(1)}, bf16[256,256]{1,0:T(8,128)(2,1)S(1)}, bf16[256,256]{1,0:T(8,128)(2,1)S(1)}, bf16[256,256]{1,0:T(8,128)(2,1)S(1)}) custom-call(s32[5]{0:T(128)S(1)} %stack.26.where, bf16[4,128,512]{2,1,0:T(8,128)(2,1)S(1)} %get-tuple-element.31.refs_0_, bf16[4,128,512]{2,1,0:T(8,128)(2,1)S(1)} %collective-permute-done.refs_1_, ...), custom_call_target="tpu_custom_call" | custom-call | flops 268435456 | bytes 6553600 | tf_op jit(solution)/shard_map/pallas_call | solution.py:141
  48.3 0.8 %collective-permute-start.14 = (bf16[256,256]{1,0:T(8,128)(2,1)S(1)}, bf16[256,256]{1,0:T(8,128)(2,1)S(1)}, u32[]{:S(2)}, u32[]{:S(2)}) collective-permute-start(bf16[256,256]{1,0:T(8,128)(2,1)S(1)} %get-tuple-element.46), channel_id=1, source_target_pairs={{0,1},{1,0},{2,3},{3,2},{4,5},{5,4},{6,7},{7,6},{8,9},{9,8},{10,11... | collective-permute-start | bytes 393224 | tf_op jit(solution)/shard_map/ppermute | solution.py:320
  49.1 1.5 %collective-permute-start.15 = (bf16[256,256]{1,0:T(8,128)(2,1)S(1)}, bf16[256,256]{1,0:T(8,128)(2,1)S(1)}, u32[]{:S(2)}, u32[]{:S(2)}) collective-permute-start(bf16[256,256]{1,0:T(8,128)(2,1)S(1)} %get-tuple-element.47), channel_id=1, source_target_pairs={{0,16},{8,24},{16,0},{24,8},{1,17},{9,25},{17,1},{25,9},{2,18},{10... | collective-permute-start | bytes 393224 | tf_op jit(solution)/shard_map/ppermute | solution.py:317
  50.6 1.3 %collective-permute-start.16 = (bf16[256,256]{1,0:T(8,128)(2,1)S(1)}, bf16[256,256]{1,0:T(8,128)(2,1)S(1)}, u32[]{:S(2)}, u32[]{:S(2)}) collective-permute-start(bf16[256,256]{1,0:T(8,128)(2,1)S(1)} %get-tuple-element.48), channel_id=1, source_target_pairs={{0,17},{1,16},{2,19},{3,18},{4,21},{5,20},{6,23},{7,22},{8,25},{9,... | collective-permute-start | bytes 393224 | tf_op jit(solution)/shard_map/ppermute | solution.py:329
  51.9 0.7 collective-permute-done.19.y_ref
  52.6 3.2 %collective-permute-done.20.xy_ref = f32[256,256]{1,0:T(8,128)S(1)} collective-permute-done((f32[256,256]{1,0:T(8,128)S(1)}, f32[256,256]{1,0:T(8,128)S(1)}, u32[]{:S(2)}, u32[]{:S(2)}) %collective-permute-start.20) | collective-permute-done | bytes 262176 | tf_op jit(solution)/shard_map/ppermute | solution.py:329
  55.8 0.2 shard_map.84.refs_0_
  55.9 0.6 collective-permute-start.21
  56.5 1.1 %collective-permute-done.14.x_ref = bf16[256,256]{1,0:T(8,128)(2,1)S(1)} collective-permute-done((bf16[256,256]{1,0:T(8,128)(2,1)S(1)}, bf16[256,256]{1,0:T(8,128)(2,1)S(1)}, u32[]{:S(2)}, u32[]{:S(2)}) %collective-permute-start.14) | collective-permute-done | bytes 131104 | tf_op jit(solution)/shard_map/ppermute | solution.py:320
  57.6 1.0 %collective-permute-done.15.y_ref = bf16[256,256]{1,0:T(8,128)(2,1)S(1)} collective-permute-done((bf16[256,256]{1,0:T(8,128)(2,1)S(1)}, bf16[256,256]{1,0:T(8,128)(2,1)S(1)}, u32[]{:S(2)}, u32[]{:S(2)}) %collective-permute-start.15) | collective-permute-done | bytes 131104 | tf_op jit(solution)/shard_map/ppermute | solution.py:317
  58.6 2.0 %collective-permute-done.16.xy_ref = bf16[256,256]{1,0:T(8,128)(2,1)S(1)} collective-permute-done((bf16[256,256]{1,0:T(8,128)(2,1)S(1)}, bf16[256,256]{1,0:T(8,128)(2,1)S(1)}, u32[]{:S(2)}, u32[]{:S(2)}) %collective-permute-start.16) | collective-permute-done | bytes 131104 | tf_op jit(solution)/shard_map/ppermute | solution.py:329
  60.7 0.1 shard_map.83.refs_4_
  60.7 0.9 %collective-permute-start.17 = (bf16[256,256]{1,0:T(8,128)(2,1)S(1)}, bf16[256,256]{1,0:T(8,128)(2,1)S(1)}, u32[]{:S(2)}, u32[]{:S(2)}) collective-permute-start(bf16[256,256]{1,0:T(8,128)(2,1)S(1)} %shard_map.83.refs_4_), channel_id=1, source_target_pairs={{0,16},{8,24},{16,0},{24,8},{1,17},{9,25},{17,1},{25,9},{2,18},{10... | collective-permute-start | bytes 393224 | tf_op jit(solution)/shard_map/ppermute | solution.py:332
  61.6 1.9 %collective-permute-done.21.refs_1_ = bf16[256,256]{1,0:T(8,128)(2,1)S(1)} collective-permute-done((bf16[256,256]{1,0:T(8,128)(2,1)S(1)}, bf16[256,256]{1,0:T(8,128)(2,1)S(1)}, u32[]{:S(2)}, u32[]{:S(2)}) %collective-permute-start.21) | collective-permute-done | bytes 131104 | tf_op jit(solution)/shard_map/ppermute | solution.py:332
  63.5 1.4 %shard_map.85 = (bf16[2,512,1024]{2,1,0:T(8,128)(2,1)S(1)}, f32[2,1,1024]{2,1,0:T(1,128)S(1)}) custom-call(bf16[32,128,128]{2,1,0:T(8,128)(2,1)S(1)} %shard_map.76.q_ref, bf16[512,128]{1,0:T(8,128)(2,1)S(1)} %shard_map.77.refs_6_.bias_ref, bf16[256,256]{1,0:T(8,128)(2,1)S(1)} %shard_map.84.refs_0_, bf16[256,256]{1,0:T(8,128)(2,1)S(1)} %collective-permute-done.21.refs_1_), custom_call_target="tpu_custom_call" | custom-call | flops 268435456 | bytes 3801088 | tf_op jit(solution)/shard_map/pallas_call | solution.py:244
  64.9 1.2 %collective-permute-done.17.refs_5_ = bf16[256,256]{1,0:T(8,128)(2,1)S(1)} collective-permute-done((bf16[256,256]{1,0:T(8,128)(2,1)S(1)}, bf16[256,256]{1,0:T(8,128)(2,1)S(1)}, u32[]{:S(2)}, u32[]{:S(2)}) %collective-permute-start.17) | collective-permute-done | bytes 131104 | tf_op jit(solution)/shard_map/ppermute | solution.py:332
  66.2 0.5 collective-permute-start.25
  66.7 1.4 %shard_map.86 = (bf16[2,512,1024]{2,1,0:T(8,128)(2,1)S(1)}, f32[2,1,1024]{2,1,0:T(1,128)S(1)}) custom-call(bf16[32,128,128]{2,1,0:T(8,128)(2,1)S(1)} %shard_map.76.q_ref, bf16[512,128]{1,0:T(8,128)(2,1)S(1)} %shard_map.77.refs_6_.bias_ref, bf16[256,256]{1,0:T(8,128)(2,1)S(1)} %collective-permute-done.22.refs_0_, ...), custom_call_target="tpu_custom_call" | custom-call | flops 268435456 | bytes 3801088 | tf_op jit(solution)/shard_map/pallas_call | solution.py:244
  68.0 2.2 %shard_map.87 = bf16[128,4096]{1,0:T(8,128)(2,1)} custom-call(s32[5]{0:T(128)S(1)} %stack.26.where, bf16[2,512,1024]{2,1,0:T(8,128)(2,1)S(1)} %get-tuple-element.51.refs_0_, bf16[2,512,1024]{2,1,0:T(8,128)(2,1)S(1)} %get-tuple-element.52.refs_1_, f32[2,1,1024]{2,1,0:T(1,128)S(1)} %get-tuple-element.53.refs_2_, f32[2,1,1024]{2,1,0:T(1,128)S(1)} %get-tuple-element.54.refs_3_, ...), custom_call_target="tpu_custom_call" | custom-call | flops 536870912 | bytes 5242880 | tf_op jit(solution)/shard_map/pallas_call | solution.py:435
  (22 shorter events, 0.1 us)
Async XLA Ops:
  0.1 1.2 %copy-start = (bf16[1024,512]{1,0:T(8,128)(2,1)S(1)}, bf16[1024,512]{1,0:T(8,128)(2,1)}, u32[]{:S(2)}) copy-start(bf16[1024,512]{1,0:T(8,128)(2,1)} %weight_ref.2) | copy-start | bytes 3145732
  1.3 11.8 %copy-start.1 = (bf16[1024,512]{1,0:T(8,128)(2,1)S(1)}, bf16[1024,512]{1,0:T(8,128)(2,1)}, u32[]{:S(2)}) copy-start(bf16[1024,512]{1,0:T(8,128)(2,1)} %weight_ref.3) | copy-start | bytes 3145732
  1.9 12.3 %collective-permute-start.3 = (bf16[512,256]{1,0:T(8,128)(2,1)S(1)}, bf16[512,256]{1,0:T(8,128)(2,1)S(1)}, u32[]{:S(2)}, u32[]{:S(2)}) collective-permute-start(bf16[512,256]{1,0:T(8,128)(2,1)S(1)} %shard_map.73.refs_0_.refs_2_.refs_4_), channel_id=1, source_target_pairs={{0,2},{1,3},{2,4},{3,5},{4,6},{5,7},{6,0},{7,1},{8,10},{9,11},{10,... | collective-permute-start | bytes 786440 | tf_op jit(solution)/shard_map/ppermute | solution.py:323
  5.0 13.6 %collective-permute-start.4 = (bf16[512,256]{1,0:T(8,128)(2,1)S(1)}, bf16[512,256]{1,0:T(8,128)(2,1)S(1)}, u32[]{:S(2)}, u32[]{:S(2)}) collective-permute-start(bf16[512,256]{1,0:T(8,128)(2,1)S(1)} %shard_map.73.refs_0_.refs_2_.refs_4_), channel_id=1, source_target_pairs={{0,6},{1,7},{2,0},{3,1},{4,2},{5,3},{6,4},{7,5},{8,14},{9,15},{10,... | collective-permute-start | bytes 786440 | tf_op jit(solution)/shard_map/ppermute | solution.py:323
  7.1 7.1 %copy-start.4 = (s32[1,128]{1,0:T(1,128)S(1)}, s32[1,128]{1,0:T(1,128)}, u32[]{:S(2)}) copy-start(s32[1,128]{1,0:T(1,128)} %param.11) | copy-start | bytes 1540
  7.1 14.2 %copy-start.3 = (s32[1,2,6]{2,1,0:T(2,128)S(1)}, s32[1,2,6]{2,1,0:T(2,128)}, u32[]{:S(2)}) copy-start(s32[1,2,6]{2,1,0:T(2,128)} %param.12) | copy-start | bytes 148
  10.0 21.8 %collective-permute-start.1 = (bf16[4,128,512]{2,1,0:T(8,128)(2,1)}, bf16[4,128,512]{2,1,0:T(8,128)(2,1)S(1)}, u32[]{:S(2)}, u32[]{:S(2)}) collective-permute-start(bf16[4,128,512]{2,1,0:T(8,128)(2,1)} %get-tuple-element.32), channel_id=1, source_target_pairs={{0,1},{1,0},{2,3},{3,2},{4,5},{5,4},{6,7},{7,6},{8,9},{9,8},{10,11... | collective-permute-start | bytes 1572872 | tf_op jit(solution)/shard_map/ppermute | solution.py:320
  11.6 24.4 %collective-permute-start.2 = (bf16[4,128,512]{2,1,0:T(8,128)(2,1)}, bf16[4,128,512]{2,1,0:T(8,128)(2,1)S(1)}, u32[]{:S(2)}, u32[]{:S(2)}) collective-permute-start(bf16[4,128,512]{2,1,0:T(8,128)(2,1)} %get-tuple-element.33), channel_id=1, source_target_pairs={{0,16},{8,24},{16,0},{24,8},{1,17},{9,25},{17,1},{25,9},{2,18},{10... | collective-permute-start | bytes 1572872 | tf_op jit(solution)/shard_map/ppermute | solution.py:317
  13.7 13.2 %collective-permute-start.6 = (bf16[512,256]{1,0:T(8,128)(2,1)S(1)}, bf16[512,256]{1,0:T(8,128)(2,1)}, u32[]{:S(2)}, u32[]{:S(2)}) collective-permute-start(bf16[512,256]{1,0:T(8,128)(2,1)S(1)} %shard_map.75.refs_8_), channel_id=1, source_target_pairs={{0,2},{1,3},{2,4},{3,5},{4,6},{5,7},{6,0},{7,1},{8,10},{9,11},{10,... | collective-permute-start | bytes 786440 | tf_op jit(solution)/shard_map/ppermute | solution.py:323
  14.2 7.8 %collective-permute-start.7 = (s32[1,128]{1,0:T(1,128)S(1)}, s32[1,128]{1,0:T(1,128)S(1)}, u32[]{:S(2)}, u32[]{:S(2)}) collective-permute-start(s32[1,128]{1,0:T(1,128)S(1)} %copy-done.4), channel_id=1, source_target_pairs={{0,8},{8,0},{16,24},{24,16},{1,9},{9,1},{17,25},{25,17},{2,10},{10... | collective-permute-start | bytes 1544 | tf_op jit(solution)/shard_map/ppermute | solution.py:314
  18.6 18.0 %collective-permute-start.10 = (bf16[4,128,512]{2,1,0:T(8,128)(2,1)}, bf16[4,128,512]{2,1,0:T(8,128)(2,1)S(1)}, u32[]{:S(2)}, u32[]{:S(2)}) collective-permute-start(bf16[4,128,512]{2,1,0:T(8,128)(2,1)} %get-tuple-element.38), channel_id=1, source_target_pairs={{0,17},{1,16},{2,19},{3,18},{4,21},{5,20},{6,23},{7,22},{8,25},{9,... | collective-permute-start | bytes 1572872 | tf_op jit(solution)/shard_map/ppermute | solution.py:329
  22.0 1.8 %copy-start.5 = (s32[1,128]{1,0:T(1,128)}, s32[1,128]{1,0:T(1,128)S(1)}, u32[]{:S(2)}) copy-start(s32[1,128]{1,0:T(1,128)S(1)} %collective-permute-done.7) | copy-start | bytes 1540
  22.0 14.0 %collective-permute-start.5 = (bf16[512,256]{1,0:T(8,128)(2,1)S(1)}, bf16[512,256]{1,0:T(8,128)(2,1)S(1)}, u32[]{:S(2)}, u32[]{:S(2)}) collective-permute-start(bf16[512,256]{1,0:T(8,128)(2,1)S(1)} %collective-permute-done.3.after_ref.refs_0_.refs_3_.refs_5_), channel_id=1, source_target_pairs={{0,2},{1,3},{2,4},{3,5},{4,6},{5,7},{6,0},{7,1},{8,10},{9,11},{10,... | collective-permute-start | bytes 786440 | tf_op jit(solution)/shard_map/ppermute | solution.py:323
  26.9 9.6 %collective-permute-start.11 = (bf16[512,256]{1,0:T(8,128)(2,1)S(1)}, bf16[512,256]{1,0:T(8,128)(2,1)S(1)}, u32[]{:S(2)}, u32[]{:S(2)}) collective-permute-start(bf16[512,256]{1,0:T(8,128)(2,1)S(1)} %shard_map.75.refs_8_), channel_id=1, source_target_pairs={{0,6},{1,7},{2,0},{3,1},{4,2},{5,3},{6,4},{7,5},{8,14},{9,15},{10,... | collective-permute-start | bytes 786440 | tf_op jit(solution)/shard_map/ppermute | solution.py:323
  29.2 1.2 %copy-start.2 = (bf16[1,128,4096]{2,1,0:T(8,128)(2,1)S(1)}, bf16[1,128,4096]{2,1,0:T(8,128)(2,1)}, u32[]{:S(2)}) copy-start(bf16[1,128,4096]{2,1,0:T(8,128)(2,1)} %param.8) | copy-start | bytes 3145732
  36.0 1.9 %collective-permute-start.9 = (bf16[4,128,512]{2,1,0:T(8,128)(2,1)S(1)}, bf16[4,128,512]{2,1,0:T(8,128)(2,1)S(1)}, u32[]{:S(2)}, u32[]{:S(2)}) collective-permute-start(bf16[4,128,512]{2,1,0:T(8,128)(2,1)S(1)} %collective-permute-done.2.refs_0_.refs_4_), channel_id=1, source_target_pairs={{0,8},{8,0},{16,24},{24,16},{1,9},{9,1},{17,25},{25,17},{2,10},{10... | collective-permute-start | bytes 1572872 | tf_op jit(solution)/shard_map/ppermute | solution.py:314
  36.0 2.9 %collective-permute-start.8 = (bf16[4,128,512]{2,1,0:T(8,128)(2,1)S(1)}, bf16[4,128,512]{2,1,0:T(8,128)(2,1)S(1)}, u32[]{:S(2)}, u32[]{:S(2)}) collective-permute-start(bf16[4,128,512]{2,1,0:T(8,128)(2,1)S(1)} %collective-permute-done.1.refs_0_.refs_2_), channel_id=1, source_target_pairs={{0,8},{8,0},{16,24},{24,16},{1,9},{9,1},{17,25},{25,17},{2,10},{10... | collective-permute-start | bytes 1572872 | tf_op jit(solution)/shard_map/ppermute | solution.py:314
  36.5 5.5 %collective-permute-start = (bf16[4,128,512]{2,1,0:T(8,128)(2,1)S(1)}, bf16[4,128,512]{2,1,0:T(8,128)(2,1)S(1)}, u32[]{:S(2)}, u32[]{:S(2)}) collective-permute-start(bf16[4,128,512]{2,1,0:T(8,128)(2,1)S(1)} %get-tuple-element.31.refs_0_), channel_id=1, source_target_pairs={{0,8},{8,0},{16,24},{24,16},{1,9},{9,1},{17,25},{25,17},{2,10},{10... | collective-permute-start | bytes 1572872 | tf_op jit(solution)/shard_map/ppermute | solution.py:314
  36.6 5.5 %collective-permute-start.12 = (bf16[4,128,512]{2,1,0:T(8,128)(2,1)S(1)}, bf16[4,128,512]{2,1,0:T(8,128)(2,1)S(1)}, u32[]{:S(2)}, u32[]{:S(2)}) collective-permute-start(bf16[4,128,512]{2,1,0:T(8,128)(2,1)S(1)} %collective-permute-done.10.refs_2_.refs_6_), channel_id=1, source_target_pairs={{0,8},{8,0},{16,24},{24,16},{1,9},{9,1},{17,25},{25,17},{2,10},{10... | collective-permute-start | bytes 1572872 | tf_op jit(solution)/shard_map/ppermute | solution.py:314
  37.0 10.3 %collective-permute-start.13 = (bf16[512,256]{1,0:T(8,128)(2,1)}, bf16[512,256]{1,0:T(8,128)(2,1)S(1)}, u32[]{:S(2)}, u32[]{:S(2)}) collective-permute-start(bf16[512,256]{1,0:T(8,128)(2,1)} %collective-permute-done.6.refs_9_), channel_id=1, source_target_pairs={{0,2},{1,3},{2,4},{3,5},{4,6},{5,7},{6,0},{7,1},{8,10},{9,11},{10,... | collective-permute-start | bytes 786440 | tf_op jit(solution)/shard_map/ppermute | solution.py:323
  39.9 10.7 %collective-permute-start.18 = (f32[256,256]{1,0:T(8,128)S(1)}, f32[256,256]{1,0:T(8,128)S(1)}, u32[]{:S(2)}, u32[]{:S(2)}) collective-permute-start(f32[256,256]{1,0:T(8,128)S(1)} %shard_map.79.refs_8_), channel_id=1, source_target_pairs={{0,1},{1,0},{2,3},{3,2},{4,5},{5,4},{6,7},{7,6},{8,9},{9,8},{10,11... | collective-permute-start | bytes 786440 | tf_op jit(solution)/shard_map/ppermute | solution.py:320
  40.0 12.6 %collective-permute-start.19 = (f32[256,256]{1,0:T(8,128)S(1)}, f32[256,256]{1,0:T(8,128)S(1)}, u32[]{:S(2)}, u32[]{:S(2)}) collective-permute-start(f32[256,256]{1,0:T(8,128)S(1)} %shard_map.78.refs_6_), channel_id=1, source_target_pairs={{0,16},{8,24},{16,0},{24,8},{1,17},{9,25},{17,1},{25,9},{2,18},{10... | collective-permute-start | bytes 786440 | tf_op jit(solution)/shard_map/ppermute | solution.py:317
  43.3 12.4 %collective-permute-start.20 = (f32[256,256]{1,0:T(8,128)S(1)}, f32[256,256]{1,0:T(8,128)S(1)}, u32[]{:S(2)}, u32[]{:S(2)}) collective-permute-start(f32[256,256]{1,0:T(8,128)S(1)} %get-tuple-element.49), channel_id=1, source_target_pairs={{0,17},{1,16},{2,19},{3,18},{4,21},{5,20},{6,23},{7,22},{8,25},{9,... | collective-permute-start | bytes 786440 | tf_op jit(solution)/shard_map/ppermute | solution.py:329
  48.3 9.3 %collective-permute-start.14 = (bf16[256,256]{1,0:T(8,128)(2,1)S(1)}, bf16[256,256]{1,0:T(8,128)(2,1)S(1)}, u32[]{:S(2)}, u32[]{:S(2)}) collective-permute-start(bf16[256,256]{1,0:T(8,128)(2,1)S(1)} %get-tuple-element.46), channel_id=1, source_target_pairs={{0,1},{1,0},{2,3},{3,2},{4,5},{5,4},{6,7},{7,6},{8,9},{9,8},{10,11... | collective-permute-start | bytes 393224 | tf_op jit(solution)/shard_map/ppermute | solution.py:320
  49.1 9.5 %collective-permute-start.15 = (bf16[256,256]{1,0:T(8,128)(2,1)S(1)}, bf16[256,256]{1,0:T(8,128)(2,1)S(1)}, u32[]{:S(2)}, u32[]{:S(2)}) collective-permute-start(bf16[256,256]{1,0:T(8,128)(2,1)S(1)} %get-tuple-element.47), channel_id=1, source_target_pairs={{0,16},{8,24},{16,0},{24,8},{1,17},{9,25},{17,1},{25,9},{2,18},{10... | collective-permute-start | bytes 393224 | tf_op jit(solution)/shard_map/ppermute | solution.py:317
  50.6 10.1 %collective-permute-start.16 = (bf16[256,256]{1,0:T(8,128)(2,1)S(1)}, bf16[256,256]{1,0:T(8,128)(2,1)S(1)}, u32[]{:S(2)}, u32[]{:S(2)}) collective-permute-start(bf16[256,256]{1,0:T(8,128)(2,1)S(1)} %get-tuple-element.48), channel_id=1, source_target_pairs={{0,17},{1,16},{2,19},{3,18},{4,21},{5,20},{6,23},{7,22},{8,25},{9,... | collective-permute-start | bytes 393224 | tf_op jit(solution)/shard_map/ppermute | solution.py:329
  55.9 7.6 %collective-permute-start.21 = (bf16[256,256]{1,0:T(8,128)(2,1)S(1)}, bf16[256,256]{1,0:T(8,128)(2,1)S(1)}, u32[]{:S(2)}, u32[]{:S(2)}) collective-permute-start(bf16[256,256]{1,0:T(8,128)(2,1)S(1)} %shard_map.84.refs_0_), channel_id=1, source_target_pairs={{0,16},{8,24},{16,0},{24,8},{1,17},{9,25},{17,1},{25,9},{2,18},{10... | collective-permute-start | bytes 393224 | tf_op jit(solution)/shard_map/ppermute | solution.py:332
  60.7 5.4 %collective-permute-start.17 = (bf16[256,256]{1,0:T(8,128)(2,1)S(1)}, bf16[256,256]{1,0:T(8,128)(2,1)S(1)}, u32[]{:S(2)}, u32[]{:S(2)}) collective-permute-start(bf16[256,256]{1,0:T(8,128)(2,1)S(1)} %shard_map.83.refs_4_), channel_id=1, source_target_pairs={{0,16},{8,24},{16,0},{24,8},{1,17},{9,25},{17,1},{25,9},{2,18},{10... | collective-permute-start | bytes 393224 | tf_op jit(solution)/shard_map/ppermute | solution.py:332
  61.6 5.0 %collective-permute-start.22 = (bf16[256,256]{1,0:T(8,128)(2,1)S(1)}, bf16[256,256]{1,0:T(8,128)(2,1)S(1)}, u32[]{:S(2)}, u32[]{:S(2)}) collective-permute-start(bf16[256,256]{1,0:T(8,128)(2,1)S(1)} %shard_map.84.refs_0_), channel_id=1, source_target_pairs={{0,8},{8,0},{16,24},{24,16},{1,9},{9,1},{17,25},{25,17},{2,10},{10... | collective-permute-start | bytes 393224 | tf_op jit(solution)/shard_map/ppermute | solution.py:314
  63.5 3.1 %collective-permute-start.23 = (bf16[256,256]{1,0:T(8,128)(2,1)S(1)}, bf16[256,256]{1,0:T(8,128)(2,1)S(1)}, u32[]{:S(2)}, u32[]{:S(2)}) collective-permute-start(bf16[256,256]{1,0:T(8,128)(2,1)S(1)} %collective-permute-done.21.refs_1_), channel_id=1, source_target_pairs={{0,8},{8,0},{16,24},{24,16},{1,9},{9,1},{17,25},{25,17},{2,10},{10... | collective-permute-start | bytes 393224 | tf_op jit(solution)/shard_map/ppermute | solution.py:314
  66.1 1.9 %collective-permute-start.24 = (bf16[256,256]{1,0:T(8,128)(2,1)S(1)}, bf16[256,256]{1,0:T(8,128)(2,1)S(1)}, u32[]{:S(2)}, u32[]{:S(2)}) collective-permute-start(bf16[256,256]{1,0:T(8,128)(2,1)S(1)} %shard_map.83.refs_4_), channel_id=1, source_target_pairs={{0,8},{8,0},{16,24},{24,16},{1,9},{9,1},{17,25},{25,17},{2,10},{10... | collective-permute-start | bytes 393224 | tf_op jit(solution)/shard_map/ppermute | solution.py:314
  66.2 1.9 %collective-permute-start.25 = (bf16[256,256]{1,0:T(8,128)(2,1)S(1)}, bf16[256,256]{1,0:T(8,128)(2,1)S(1)}, u32[]{:S(2)}, u32[]{:S(2)}) collective-permute-start(bf16[256,256]{1,0:T(8,128)(2,1)S(1)} %collective-permute-done.17.refs_5_), channel_id=1, source_target_pairs={{0,8},{8,0},{16,24},{24,16},{1,9},{9,1},{17,25},{25,17},{2,10},{10... | collective-permute-start | bytes 393224 | tf_op jit(solution)/shard_map/ppermute | solution.py:314
